TPU v7x, 32 devices: a whole 2x2x4 slice. The times are simulated.
32 devices in a mesh: pipe: 4 (over y, x), dp: 8 (over z, core).
Axes of the slice: x: 2, y: 2, z: 4, core: 2. Of those that a mesh axis runs over, the one named last changes fastest.
Arguments:
- tokens: bfloat16 [12480, 768], P('dp', 'pipe'), may hold values from -6 to 6
- cotangent: bfloat16 [12480, 768], P('dp', 'pipe'), may hold values from -6 to 6
- captions: int32 [120], P('dp'), may hold values from 5 to 60, as said below
- projection: bfloat16 [4, 768, 1152], P('pipe'), may hold values from -0.21875 to 0.21875
- biases: bfloat16 [4, 768], P('pipe'), may hold values from -1.5 to 1.5
- combiner: bfloat16 [4, 384, 768], P('pipe'), may hold values from -2 to 2
- offsets: bfloat16 [4, 384], P('pipe'), may hold values from -1.5 to 1.5
- scaling: bfloat16 [4, 384], P('pipe'), may hold values from 0.5 to 1.5
- centring: bfloat16 [4, 384], P('pipe'), may hold values from -1.5 to 1.5
- expansion: bfloat16 [4, 768, 1536], P('pipe'), may hold values from -0.21875 to 0.21875
- lifting: bfloat16 [4, 1536], P('pipe'), may hold values from -1.5 to 1.5
- reduction: bfloat16 [4, 1536, 768], P('pipe'), may hold values from -0.109375 to 0.109375
- settling: bfloat16 [4, 384], P('pipe'), may hold values from -1.5 to 1.5
- stretch: bfloat16 [4, 384], P('pipe'), may hold values from 0.5 to 1.5
- translate: bfloat16 [4, 384], P('pipe'), may hold values from -1.5 to 1.5
Outputs:
- encoded: bfloat16 [12480, 768], P('dp', 'pipe')
- tokens_grad: float32 [12480, 768], P('dp', 'pipe')
- projection_grad: float32 [4, 768, 1152], P('pipe', 'dp')
- biases_grad: float32 [4, 768], P('pipe', 'dp')
- combiner_grad: float32 [4, 384, 768], P('pipe', 'dp')
- offsets_grad: float32 [4, 384], P('pipe', 'dp')
- scaling_grad: float32 [4, 384], P('pipe', 'dp')
- centring_grad: float32 [4, 384], P('pipe', 'dp')
- expansion_grad: float32 [4, 768, 1536], P('pipe', 'dp')
- lifting_grad: float32 [4, 1536], P('pipe', 'dp')
- reduction_grad: float32 [4, 1536, 768], P('pipe', 'dp')
- settling_grad: float32 [4, 384], P('pipe', 'dp')
- stretch_grad: float32 [4, 384], P('pipe', 'dp')
- translate_grad: float32 [4, 384], P('pipe', 'dp')
Inputs may be any that keep to these rules, and one draw needn't show every extreme that they name: `captions`: word slots at or beyond a pair's caption length are padding keys; some pair has 5 and some 60; lengths lean to short ones.
All inputs are finite; a program needn't handle non-finite values.
Results may differ from a plain program's by a relative error of at most 0.025.
Values may be sent and summed in bfloat16 or wider, within the bound.
A program may use at most 320 MiB of HBM per device.

v0:
```python
import jax
import jax.numpy as jnp
from jax import lax
from jax.sharding import PartitionSpec as P

D = 768
HEADS = 12
HEAD_DIM = 64
FF = 3072
WORDS = 64
MICRO = 3
PAIRS_MB = 5
PAIR_ROWS = 104


EPSILON = 1e-05
NEGATIVE = -1e30


def from_partner(value, axis, distance):
    return lax.ppermute(value, axis, [(i, i ^ 1 << distance) for i in range(lax.axis_size(axis))])


def passed_along(value, axis, by):
    size = lax.axis_size(axis)
    pairs = [(i, i + by) for i in range(size) if 0 <= i + by < size]
    return lax.ppermute(value, axis, pairs)


def layer_norm(residual, gain_row, shift_row):
    average = jnp.mean(residual, axis=-1, keepdims=True)
    centred = residual - average
    variance = jnp.mean(centred * centred, axis=-1, keepdims=True)
    return centred * lax.rsqrt(variance + EPSILON) * gain_row + shift_row


def gelu_exact(argument):
    return jax.nn.gelu(argument, approximate=False)


def matmul(left_side, right_side):
    return jnp.dot(left_side, right_side, preferred_element_type=jnp.float32)


def inner_rows(left_side, right_side):
    return lax.dot_general(
        left_side, right_side, (((0,), (0,)), ((), ())), preferred_element_type=jnp.float32
    )


def inner_columns(left_side, right_side):
    return lax.dot_general(
        left_side, right_side, (((1,), (1,)), ((), ())), preferred_element_type=jnp.float32
    )


def take_slot(stacked, position):
    return lax.dynamic_index_in_dim(stacked, position, 0, keepdims=False)


def put_slot(stacked, update, position):
    return lax.dynamic_update_index_in_dim(stacked, update, position, 0)


def shards(
    tokens,
    cotangent,
    captions,
    projection,
    biases,
    combiner,
    offsets,
    scaling,
    centring,
    expansion,
    lifting,
    reduction,
    settling,
    stretch,
    translate,
):
    sections = lax.axis_size("pipe")
    section_index = lax.axis_index("pipe")
    section_kind = section_index % 2
    half_width = D // 2
    hidden_half = FF // 2
    block_rows = PAIRS_MB * PAIR_ROWS
    score_scale = HEAD_DIM ** (-0.5)
    whole_tokens, whole_cotangent = (
        lax.all_gather(tokens, "pipe", axis=1, tiled=True),
        lax.all_gather(cotangent, "pipe", axis=1, tiled=True),
    )
    own_shards = (
        projection,
        biases,
        combiner,
        offsets,
        scaling,
        centring,
        expansion,
        lifting,
        reduction,
        settling,
        stretch,
        translate,
    )
    partner_shards = from_partner(
        (
            projection,
            biases,
            combiner,
            offsets,
            scaling,
            centring,
            expansion,
            lifting,
            reduction,
            settling,
            stretch,
            translate,
        ),
        "pipe",
        0,
    )
    attention_pair = [
        jnp.concatenate([own_shards[member], partner_shards[member]], 0) for member in range(6)
    ]
    dense_pair = [
        jnp.concatenate([partner_shards[member], own_shards[member]], 0) for member in range(6, 12)
    ]
    joint_weight = (
        attention_pair[0].reshape(2, D, 3, half_width).transpose(1, 2, 0, 3).reshape(D, 3 * D)
    )
    query_value = (
        attention_pair[1]
        .astype(jnp.float32)
        .reshape(2, 2, half_width)
        .transpose(1, 0, 2)
        .reshape(2, D)
    )
    joint_bias = jnp.concatenate([query_value[0], jnp.zeros((D,), jnp.float32), query_value[1]])
    mixing_weight = attention_pair[2].reshape(D, D)
    mixing_bias = attention_pair[3].astype(jnp.float32).reshape(D)
    attend_gain = attention_pair[4].astype(jnp.float32).reshape(D)
    attend_shift = attention_pair[5].astype(jnp.float32).reshape(D)
    expand_weight = dense_pair[0].transpose(1, 0, 2).reshape(D, FF)
    expand_bias = dense_pair[1].astype(jnp.float32).reshape(FF)
    reduce_weight = dense_pair[2].reshape(FF, D)
    reduce_bias = dense_pair[3].astype(jnp.float32).reshape(D)
    dense_gain = dense_pair[4].astype(jnp.float32).reshape(D)
    dense_shift = dense_pair[5].astype(jnp.float32).reshape(D)
    position_rows = jnp.arange(PAIR_ROWS)
    visible = (position_rows[None, :] < captions[:, None]) | (position_rows[None, :] >= WORDS)

    def head_scores(projected, visible_keys):
        heads_view = projected.reshape(PAIRS_MB, PAIR_ROWS, 3, HEADS, HEAD_DIM)
        scores = (
            jnp.einsum(
                "pqhd,pkhd->phqk",
                heads_view[:, :, 0],
                heads_view[:, :, 1],
                preferred_element_type=jnp.float32,
            )
            * score_scale
        )
        return (heads_view, jnp.where(visible_keys[:, None, None, :], scores, NEGATIVE))

    def attend_forward(inputs, visible_keys):
        projected = (matmul(inputs, joint_weight) + joint_bias).astype(jnp.bfloat16)
        heads_view, scores = head_scores(projected, visible_keys)
        highest = jnp.max(scores, axis=-1, keepdims=True)
        exponent = jnp.exp(scores - highest)
        summed = jnp.sum(exponent, axis=-1, keepdims=True)
        probabilities = (exponent / summed).astype(jnp.bfloat16)
        context = jnp.einsum(
            "phqk,pkhd->pqhd",
            probabilities,
            heads_view[:, :, 2],
            preferred_element_type=jnp.float32,
        )
        context = context.reshape(block_rows, D).astype(jnp.bfloat16)
        residual = inputs.astype(jnp.float32) + matmul(context, mixing_weight) + mixing_bias
        log_norm = (highest + jnp.log(summed))[..., 0]
        return (
            layer_norm(residual, attend_gain, attend_shift),
            residual,
            projected,
            context,
            log_norm,
        )

    def attend_backward(gradient, inputs, residual, projected, context, log_norm, visible_keys):
        _, norm_pull = jax.vjp(layer_norm, residual, attend_gain, attend_shift)
        grad_residual, grad_gain, grad_shift = norm_pull(gradient)
        grad_branch = grad_residual.astype(jnp.bfloat16)
        grad_mixing = inner_rows(context, grad_branch)
        grad_context = inner_columns(grad_branch, mixing_weight).astype(jnp.bfloat16)
        grad_context = grad_context.reshape(PAIRS_MB, PAIR_ROWS, HEADS, HEAD_DIM)
        heads_view, scores = head_scores(projected, visible_keys)
        query_heads = heads_view[:, :, 0]
        key_heads = heads_view[:, :, 1]
        probabilities = jnp.exp(scores - log_norm[..., None])
        grad_probability = jnp.einsum(
            "pqhd,pkhd->phqk", grad_context, heads_view[:, :, 2], preferred_element_type=jnp.float32
        )
        grad_values = jnp.einsum(
            "phqk,pqhd->pkhd",
            probabilities.astype(jnp.bfloat16),
            grad_context,
            preferred_element_type=jnp.float32,
        )
        grad_scores = probabilities * (
            grad_probability - jnp.sum(probabilities * grad_probability, axis=-1, keepdims=True)
        )
        grad_scores = grad_scores.astype(jnp.bfloat16)
        grad_query = (
            jnp.einsum(
                "phqk,pkhd->pqhd", grad_scores, key_heads, preferred_element_type=jnp.float32
            )
            * score_scale
        )
        grad_keys = (
            jnp.einsum(
                "phqk,pqhd->pkhd", grad_scores, query_heads, preferred_element_type=jnp.float32
            )
            * score_scale
        )
        grad_joint = (
            jnp.stack([grad_query, grad_keys, grad_values], axis=2)
            .reshape(block_rows, 3 * D)
            .astype(jnp.bfloat16)
        )
        grad_weight = inner_rows(inputs, grad_joint)
        grad_bias = jnp.sum(grad_joint.astype(jnp.float32), axis=0)
        grad_inputs = grad_residual + inner_columns(grad_joint, joint_weight)
        terms = (
            grad_weight,
            grad_bias[:D],
            grad_bias[2 * D :],
            grad_mixing,
            jnp.sum(grad_residual, axis=0),
            grad_gain,
            grad_shift,
        )
        return (grad_inputs, terms)

    def dense_forward(inputs):
        expanded = matmul(inputs, expand_weight) + expand_bias
        hidden = gelu_exact(expanded).astype(jnp.bfloat16)
        residual = inputs.astype(jnp.float32) + matmul(hidden, reduce_weight) + reduce_bias
        return (layer_norm(residual, dense_gain, dense_shift), residual, expanded)

    def dense_backward(gradient, inputs, residual, expanded):
        _, norm_pull = jax.vjp(layer_norm, residual, dense_gain, dense_shift)
        grad_residual, grad_gain, grad_shift = norm_pull(gradient)
        grad_branch = grad_residual.astype(jnp.bfloat16)
        hidden, gelu_pull = jax.vjp(gelu_exact, expanded)
        grad_reduce = inner_rows(hidden.astype(jnp.bfloat16), grad_branch)
        grad_hidden = inner_columns(grad_branch, reduce_weight)
        grad_expanded = gelu_pull(grad_hidden)[0]
        grad_rounded = grad_expanded.astype(jnp.bfloat16)
        grad_expand = inner_rows(inputs, grad_rounded)
        grad_inputs = grad_residual + inner_columns(grad_rounded, expand_weight)
        terms = (
            grad_expand,
            jnp.sum(grad_expanded, axis=0),
            grad_reduce,
            jnp.sum(grad_residual, axis=0),
            grad_gain,
            grad_shift,
        )
        return (grad_inputs, terms)

    zero_rows = jnp.zeros((block_rows, D), jnp.float32)
    stored_start = (
        jnp.zeros((MICRO, block_rows, D), jnp.bfloat16),
        jnp.zeros((MICRO, block_rows, D), jnp.float32),
        jnp.zeros((MICRO, block_rows, 3 * D), jnp.bfloat16),
        jnp.zeros((MICRO, block_rows, D), jnp.bfloat16),
        jnp.zeros((MICRO, PAIRS_MB, HEADS, PAIR_ROWS), jnp.float32),
        jnp.zeros((MICRO, block_rows, FF), jnp.float32),
        jnp.zeros((MICRO, block_rows, D), jnp.float32),
    )

    def forward_tick(tick_index, state_tuple):
        outgoing, stored = state_tuple
        arrived = passed_along(outgoing, "pipe", 1)
        micro_index = tick_index - section_index
        active = (micro_index >= 0) & (micro_index < MICRO)
        position = jnp.clip(micro_index, 0, MICRO - 1)
        fresh_rows = lax.dynamic_slice_in_dim(whole_tokens, position * block_rows, block_rows, 0)
        inputs = jnp.where(section_index == 0, fresh_rows, arrived)
        visible_keys = lax.dynamic_slice_in_dim(visible, position * PAIRS_MB, PAIRS_MB, 0)

        def forward_run_attention(stored_now):
            normed, residual, projected, context, log_norm = attend_forward(inputs, visible_keys)
            updated = (
                put_slot(stored_now[0], inputs, position),
                put_slot(stored_now[1], residual, position),
                put_slot(stored_now[2], projected, position),
                put_slot(stored_now[3], context, position),
                put_slot(stored_now[4], log_norm, position),
                stored_now[5],
                put_slot(stored_now[6], normed, position),
            )
            return (normed, updated)

        def forward_run_dense(stored_now):
            normed, residual, expanded = dense_forward(inputs)
            updated = (
                put_slot(stored_now[0], inputs, position),
                put_slot(stored_now[1], residual, position),
                stored_now[2],
                stored_now[3],
                stored_now[4],
                put_slot(stored_now[5], expanded, position),
                put_slot(stored_now[6], normed, position),
            )
            return (normed, updated)

        def forward_stay_spare(stored_now):
            return (zero_rows, stored_now)

        normed, stored = lax.switch(
            jnp.where(active, section_kind, 2),
            [forward_run_attention, forward_run_dense, forward_stay_spare],
            stored,
        )
        return (normed.astype(jnp.bfloat16), stored)

    ticks = MICRO + sections - 1
    _, stored = lax.fori_loop(
        0, ticks, forward_tick, (jnp.zeros((block_rows, D), jnp.bfloat16), stored_start)
    )
    (
        kept_inputs,
        kept_residual,
        kept_projected,
        kept_context,
        kept_lognorm,
        kept_expanded,
        kept_outputs,
    ) = stored
    attention_start = (
        jnp.zeros((D, 3 * D), jnp.float32),
        jnp.zeros((D,), jnp.float32),
        jnp.zeros((D,), jnp.float32),
        jnp.zeros((D, D), jnp.float32),
        jnp.zeros((D,), jnp.float32),
        jnp.zeros((D,), jnp.float32),
        jnp.zeros((D,), jnp.float32),
    )
    dense_start = (
        jnp.zeros((D, FF), jnp.float32),
        jnp.zeros((FF,), jnp.float32),
        jnp.zeros((FF, D), jnp.float32),
        jnp.zeros((D,), jnp.float32),
        jnp.zeros((D,), jnp.float32),
        jnp.zeros((D,), jnp.float32),
    )

    def backward_tick(tick_index, state_tuple):
        outgoing, input_grads, sums_pair = state_tuple
        arrived = passed_along(outgoing, "pipe", -1)
        micro_index = tick_index - (sections - 1 - section_index)
        active = (micro_index >= 0) & (micro_index < MICRO)
        position = jnp.clip(micro_index, 0, MICRO - 1)
        fresh_rows = lax.dynamic_slice_in_dim(whole_cotangent, position * block_rows, block_rows, 0)
        gradient = jnp.where(section_index == sections - 1, fresh_rows, arrived).astype(jnp.float32)
        visible_keys = lax.dynamic_slice_in_dim(visible, position * PAIRS_MB, PAIRS_MB, 0)
        inputs = take_slot(kept_inputs, position)
        residual = take_slot(kept_residual, position)

        def backward_run_attention(sums_now):
            grad_inputs, terms = attend_backward(
                gradient,
                inputs,
                residual,
                take_slot(kept_projected, position),
                take_slot(kept_context, position),
                take_slot(kept_lognorm, position),
                visible_keys,
            )
            return (
                grad_inputs,
                (tuple((total + term for total, term in zip(sums_now[0], terms))), sums_now[1]),
            )

        def backward_run_dense(sums_now):
            grad_inputs, terms = dense_backward(
                gradient, inputs, residual, take_slot(kept_expanded, position)
            )
            return (
                grad_inputs,
                (sums_now[0], tuple((total + term for total, term in zip(sums_now[1], terms)))),
            )

        def backward_stay_spare(sums_now):
            return (zero_rows, sums_now)

        grad_inputs, sums_pair = lax.switch(
            jnp.where(active, section_kind, 2),
            [backward_run_attention, backward_run_dense, backward_stay_spare],
            sums_pair,
        )
        input_grads = put_slot(
            input_grads, jnp.where(active, grad_inputs, take_slot(input_grads, position)), position
        )
        return (grad_inputs.astype(jnp.bfloat16), input_grads, sums_pair)

    _, input_grads, sums_pair = lax.fori_loop(
        0,
        ticks,
        backward_tick,
        (
            jnp.zeros((block_rows, D), jnp.bfloat16),
            jnp.zeros((MICRO, block_rows, D), jnp.float32),
            (attention_start, dense_start),
        ),
    )
    attention_sums, dense_sums = sums_pair
    last_section = (section_index == sections - 1).astype(jnp.float32)
    first_section = (section_index == 0).astype(jnp.float32)
    encoded, tokens_grad = (
        lax.psum_scatter(
            (kept_outputs.reshape(MICRO * block_rows, D) * last_section).astype(jnp.bfloat16),
            "pipe",
            scatter_dimension=1,
            tiled=True,
        ).astype(jnp.float32),
        lax.psum_scatter(
            (input_grads.reshape(MICRO * block_rows, D) * first_section).astype(jnp.bfloat16),
            "pipe",
            scatter_dimension=1,
            tiled=True,
        ).astype(jnp.float32),
    )
    grad_halves = (
        attention_sums[0]
        .reshape(D, 3, 2, half_width)
        .transpose(2, 0, 1, 3)
        .reshape(2, D, 3 * half_width),
        jnp.stack(
            [attention_sums[1].reshape(2, half_width), attention_sums[2].reshape(2, half_width)],
            axis=1,
        ).reshape(2, D),
        attention_sums[3].reshape(2, half_width, D),
        attention_sums[4].reshape(2, half_width),
        attention_sums[5].reshape(2, half_width),
        attention_sums[6].reshape(2, half_width),
        dense_sums[0].reshape(D, 2, hidden_half).transpose(1, 0, 2),
        dense_sums[1].reshape(2, hidden_half),
        dense_sums[2].reshape(2, hidden_half, D),
        dense_sums[3].reshape(2, half_width),
        dense_sums[4].reshape(2, half_width),
        dense_sums[5].reshape(2, half_width),
    )
    summed = (
        lax.psum_scatter(grad_halves[0], "dp", scatter_dimension=1, tiled=True),
        lax.psum_scatter(grad_halves[1], "dp", scatter_dimension=1, tiled=True),
        lax.psum_scatter(grad_halves[2], "dp", scatter_dimension=1, tiled=True),
        lax.psum_scatter(grad_halves[3], "dp", scatter_dimension=1, tiled=True),
        lax.psum_scatter(grad_halves[4], "dp", scatter_dimension=1, tiled=True),
        lax.psum_scatter(grad_halves[5], "dp", scatter_dimension=1, tiled=True),
        lax.psum_scatter(grad_halves[6], "dp", scatter_dimension=1, tiled=True),
        lax.psum_scatter(grad_halves[7], "dp", scatter_dimension=1, tiled=True),
        lax.psum_scatter(grad_halves[8], "dp", scatter_dimension=1, tiled=True),
        lax.psum_scatter(grad_halves[9], "dp", scatter_dimension=1, tiled=True),
        lax.psum_scatter(grad_halves[10], "dp", scatter_dimension=1, tiled=True),
        lax.psum_scatter(grad_halves[11], "dp", scatter_dimension=1, tiled=True),
    )
    keep_part = tuple((take_slot(member, section_kind) for member in summed))
    send_part = tuple((take_slot(member, 1 - section_kind) for member in summed))
    received = (
        from_partner(send_part[0].astype(jnp.bfloat16), "pipe", 0).astype(jnp.float32),
        from_partner(send_part[1].astype(jnp.bfloat16), "pipe", 0).astype(jnp.float32),
        from_partner(send_part[2].astype(jnp.bfloat16), "pipe", 0).astype(jnp.float32),
        from_partner(send_part[3].astype(jnp.bfloat16), "pipe", 0).astype(jnp.float32),
        from_partner(send_part[4].astype(jnp.bfloat16), "pipe", 0).astype(jnp.float32),
        from_partner(send_part[5].astype(jnp.bfloat16), "pipe", 0).astype(jnp.float32),
        from_partner(send_part[6].astype(jnp.bfloat16), "pipe", 0).astype(jnp.float32),
        from_partner(send_part[7].astype(jnp.bfloat16), "pipe", 0).astype(jnp.float32),
        from_partner(send_part[8].astype(jnp.bfloat16), "pipe", 0).astype(jnp.float32),
        from_partner(send_part[9].astype(jnp.bfloat16), "pipe", 0).astype(jnp.float32),
        from_partner(send_part[10].astype(jnp.bfloat16), "pipe", 0).astype(jnp.float32),
        from_partner(send_part[11].astype(jnp.bfloat16), "pipe", 0).astype(jnp.float32),
    )
    final = tuple((kept + got for kept, got in zip(keep_part, received)))
    return (
        encoded.astype(jnp.bfloat16),
        tokens_grad,
        final[0][None],
        final[1][None],
        final[2][None],
        final[3][None],
        final[4][None],
        final[5][None],
        final[6][None],
        final[7][None],
        final[8][None],
        final[9][None],
        final[10][None],
        final[11][None],
    )


def solution(mesh):
    in_specs = (
        P("dp", "pipe"),
        P("dp", "pipe"),
        P("dp"),
        P("pipe", None, None),
        P("pipe", None),
        P("pipe", None, None),
        P("pipe", None),
        P("pipe", None),
        P("pipe", None),
        P("pipe", None, None),
        P("pipe", None),
        P("pipe", None, None),
        P("pipe", None),
        P("pipe", None),
        P("pipe", None),
    )
    out_specs = (
        P("dp", "pipe"),
        P("dp", "pipe"),
        P("pipe", "dp", None),
        P("pipe", "dp"),
        P("pipe", "dp", None),
        P("pipe", "dp"),
        P("pipe", "dp"),
        P("pipe", "dp"),
        P("pipe", "dp", None),
        P("pipe", "dp"),
        P("pipe", "dp", None),
        P("pipe", "dp"),
        P("pipe", "dp"),
        P("pipe", "dp"),
    )
    return jax.shard_map(shards, mesh=mesh, in_specs=in_specs, out_specs=out_specs, check_vma=False)
```

profile of v0, /device:TPU:0, one launch (start us, length us, event | category | flops | bytes accessed | tf_op | source)
XLA Modules:
  0.0 2101.0 jit_solution(10234218258116936680)
XLA Ops:
  19.1 173.8 %collective-permute-done.5 = bf16[1,384]{1,0:T(2,128)(2,1)} collective-permute-done((bf16[1,384]{1,0:T(2,128)(2,1)S(1)}, bf16[1,384]{1,0:T(2,128)(2,1)}, u32[]{:S(2)}, u32[]{:S(2)}) %collective-permute-start.5) | collective-permute-done | bytes 800 | tf_op jit(solution)/shard_map/ppermute | solution.py:21
  266.1 313.5 %while.73 = (s32[]{:T(128)}, bf16[520,768]{1,0:T(8,128)(2,1)}, bf16[3,520,768]{2,1,0:T(8,128)(2,1)}, f32[3,520,768]{2,1,0:T(8,128)}, bf16[3,520,2304]{2,1,0:T(8,...) while((s32[]{:T(128)}, bf16[520,768]{1,0:T(8,128)(2,1)}, ...), condition=%wide.region_10.11_spmd.clone, body=%wide.region_0.10_spmd.clone.sunk | while | flops 5021153792 | bytes 69958008 | solution.py:332
  290.6 13.4 collective-permute-done
  305.3 53.7 %conditional.6 = (bf16[3,520,768]{2,1,0:T(8,128)(2,1)}, f32[3,520,768]{2,1,0:T(8,128)}, bf16[3,520,2304]{2,1,0:T(8,128)(2,1)}, bf16[3,520,768]{2,1,0:T(8,128)(2,...) conditional(s32[]{:T(128)} %clamp.45, ...), branch_computations={%region_1.5_spmd, %region_6.8_spmd, %region_9.9_spmd} | conditional | flops 5020754432 | bytes 64359944 | solution.py:324
  360.4 12.8 collective-permute-done
  374.6 53.7 %conditional.6 = (bf16[3,520,768]{2,1,0:T(8,128)(2,1)}, f32[3,520,768]{2,1,0:T(8,128)}, bf16[3,520,2304]{2,1,0:T(8,128)(2,1)}, bf16[3,520,768]{2,1,0:T(8,128)(2,...) conditional(s32[]{:T(128)} %clamp.45, ...), branch_computations={%region_1.5_spmd, %region_6.8_spmd, %region_9.9_spmd} | conditional | flops 5020754432 | bytes 64359944 | solution.py:324
  429.7 12.1 collective-permute-done
  443.1 53.7 %conditional.6 = (bf16[3,520,768]{2,1,0:T(8,128)(2,1)}, f32[3,520,768]{2,1,0:T(8,128)}, bf16[3,520,2304]{2,1,0:T(8,128)(2,1)}, bf16[3,520,768]{2,1,0:T(8,128)(2,...) conditional(s32[]{:T(128)} %clamp.45, ...), branch_computations={%region_1.5_spmd, %region_6.8_spmd, %region_9.9_spmd} | conditional | flops 5020754432 | bytes 64359944 | solution.py:324
  512.1 32.6 %collective-permute-start = (bf16[520,768]{1,0:T(8,128)(2,1)}, bf16[520,768]{1,0:T(8,128)(2,1)S(1)}, u32[]{:S(2)}, u32[]{:S(2)}) collective-permute-start(bf16[520,768]{1,0:T(8,128)(2,1)} %get-tuple-element.3144), channel_id=1, source_target_pairs={{0,8},{8,16},{16,24},{1,9},{9,17},{17,25},{2,10},{10,18},{18,26},{... | collective-permute-start | bytes 2396168 | tf_op jit(solution)/shard_map/while/body/eval_jaxpr/ppermute | solution.py:27
  596.6 698.3 %while.74 = (s32[]{:T(128)}, bf16[520,768]{1,0:T(8,128)(2,1)}, f32[3,520,768]{2,1,0:T(8,128)}, f32[768,2304]{1,0:T(8,128)}, f32[768]{0:T(1024)S(1)}, /*index=5*/...) while((s32[]{:T(128)}, bf16[520,768]{1,0:T(8,128)(2,1)}, ...), condition=%wide.region_33.34_spmd.clone, body=%wide.region_12.33_spmd.clone.sunk | while | flops 9959569408 | bytes 252377904 | solution.py:411
  627.9 60.6 %collective-permute-done.1 = bf16[520,768]{1,0:T(8,128)(2,1)S(1)} collective-permute-done((bf16[520,768]{1,0:T(8,128)(2,1)}, bf16[520,768]{1,0:T(8,128)(2,1)S(1)}, u32[]{:S(2)}, u32[]{:S(2)}) %collective-permute-start.1) | collective-permute-done | bytes 798752 | tf_op jit(solution)/shard_map/while/body/eval_jaxpr/ppermute | solution.py:27
  726.6 31.4 %collective-permute-done.1 = bf16[520,768]{1,0:T(8,128)(2,1)S(1)} collective-permute-done((bf16[520,768]{1,0:T(8,128)(2,1)}, bf16[520,768]{1,0:T(8,128)(2,1)S(1)}, u32[]{:S(2)}, u32[]{:S(2)}) %collective-permute-start.1) | collective-permute-done | bytes 798752 | tf_op jit(solution)/shard_map/while/body/eval_jaxpr/ppermute | solution.py:27
  773.1 202.7 %collective-permute-done.1 = bf16[520,768]{1,0:T(8,128)(2,1)S(1)} collective-permute-done((bf16[520,768]{1,0:T(8,128)(2,1)}, bf16[520,768]{1,0:T(8,128)(2,1)S(1)}, u32[]{:S(2)}, u32[]{:S(2)}) %collective-permute-start.1) | collective-permute-done | bytes 798752 | tf_op jit(solution)/shard_map/while/body/eval_jaxpr/ppermute | solution.py:27
  978.3 89.0 %conditional.7 = (f32[520,768]{1,0:T(8,128)}, f32[768,2304]{1,0:T(8,128)}, f32[768]{0:T(1024)S(1)}, f32[768]{0:T(1024)S(1)}, f32[768,768]{1,0:T(8,128)}, /*index...) conditional(s32[]{:T(128)} %clamp.46, ...), branch_computations={%region_13.22_spmd, %region_23.31_spmd, %region_32.32_spmd} | conditional | flops 9958371328 | bytes 230005952 | solution.py:401
  986.6 12.0 copy.166
  1087.2 89.0 %conditional.7 = (f32[520,768]{1,0:T(8,128)}, f32[768,2304]{1,0:T(8,128)}, f32[768]{0:T(1024)S(1)}, f32[768]{0:T(1024)S(1)}, f32[768,768]{1,0:T(8,128)}, /*index...) conditional(s32[]{:T(128)} %clamp.46, ...), branch_computations={%region_13.22_spmd, %region_23.31_spmd, %region_32.32_spmd} | conditional | flops 9958371328 | bytes 230005952 | solution.py:401
  1095.6 12.0 copy.166
  1196.2 89.0 %conditional.7 = (f32[520,768]{1,0:T(8,128)}, f32[768,2304]{1,0:T(8,128)}, f32[768]{0:T(1024)S(1)}, f32[768]{0:T(1024)S(1)}, f32[768,768]{1,0:T(8,128)}, /*index...) conditional(s32[]{:T(128)} %clamp.46, ...), branch_computations={%region_13.22_spmd, %region_23.31_spmd, %region_32.32_spmd} | conditional | flops 9958371328 | bytes 230005952 | solution.py:401
  1204.5 12.0 copy.166
  1325.1 12.3 copy.178
  1337.4 15.0 copy.180
  1363.6 22.1 %reduce-scatter.47.cloned.1.call-done = f32[48,2]{1,0:T(8,128)} async-done(((f32[384,2]{1,0:T(8,128)}), f32[48,2]{1,0:T(8,128)}) %reduce-scatter.47.cloned.1.call-update) | async-done | bytes 400
  1386.5 29.8 %reduce-scatter.51.cloned.1.call-done = f32[48,2]{1,0:T(8,128)} async-done(((f32[384,2]{1,0:T(8,128)}), f32[48,2]{1,0:T(8,128)}) %reduce-scatter.51.cloned.1.call-update) | async-done | bytes 400
  1418.0 29.0 %reduce-scatter.53.cloned.1.call-done = f32[48,2]{1,0:T(8,128)} async-done(((f32[384,2]{1,0:T(8,128)}), f32[48,2]{1,0:T(8,128)}) %reduce-scatter.53.cloned.1.call-update) | async-done | bytes 400
  1447.8 30.0 %reduce-scatter.55.cloned.1.call-done = f32[48,2]{1,0:T(8,128)} async-done(((f32[384,2]{1,0:T(8,128)}), f32[48,2]{1,0:T(8,128)}) %reduce-scatter.55.cloned.1.call-update) | async-done | bytes 400
  1490.0 19.5 reduce-scatter.41.cloned.1.call-done
  1514.5 27.4 %reduce-scatter.49.cloned.1.call-done = f32[192,2]{1,0:T(8,128)} async-done(((f32[1536,2]{1,0:T(8,128)}), f32[192,2]{1,0:T(8,128)}) %reduce-scatter.49.cloned.1.call-update) | async-done | bytes 1552
  1545.8 32.9 %reduce-scatter.33.cloned.1.call-done = f32[2,48,768]{2,1,0:T(8,128)} async-done(((f32[2,384,768]{2,1,0:T(8,128)}), f32[2,48,768]{2,1,0:T(8,128)}) %reduce-scatter.33.cloned.1.call-update) | async-done | bytes 294928 | tf_op jit(solution)/shard_map/reduce_scatter | solution.py:461
  1581.8 38.1 %reduce-scatter.39.cloned.1.call-done = bf16[192,1560]{1,0:T(8,128)(2,1)} async-done(((bf16[768,1560]{1,0:T(8,128)(2,1)}), bf16[192,1560]{1,0:T(8,128)(2,1)}) %reduce-scatter.39.cloned.1.call-update) | async-done | bytes 599056
  1623.3 327.9 %all-reduce.5.cloned.1.call-done = (f32[2,768,1152]{2,0,1:T(2,128)}, f32[2,768,1536]{2,0,1:T(2,128)}) async-done(((f32[2,768,1152]{2,0,1:T(2,128)}, f32[2,768,1536]{2,0,1:T(2,128)}), (f32[2,768,1152]{2,0,1:T(2,128)}, f32[2,768,1536]{2,0,1:T(2,128)})) %all-reduce.5.cloned.1.call-update) | async-done | bytes 16515088
  1962.0 91.1 %reduce-scatter.35.cloned.1.call-done = f32[2,192,768]{2,1,0:T(8,128)} async-done(((f32[2,1536,768]{2,1,0:T(8,128)}), f32[2,192,768]{2,1,0:T(8,128)}) %reduce-scatter.35.cloned.1.call-update) | async-done | bytes 1179664 | tf_op jit(solution)/shard_map/reduce_scatter | solution.py:467
  2063.1 31.2 %reduce-scatter.37.cloned.1.call-done = bf16[192,1560]{1,0:T(8,128)(2,1)} async-done(((bf16[768,1560]{1,0:T(8,128)(2,1)}), bf16[192,1560]{1,0:T(8,128)(2,1)}) %reduce-scatter.37.cloned.1.call-update) | async-done | bytes 599056
  (585 shorter events, 760.1 us)
Async XLA Ops:
  7.2 228.4 %all-gather.3.cloned.1.call-start = ((), (), s32[]{:S(2)}) async-start(), calls=%async_computation.12 | async-start | bytes 3194880 | tf_op jit(solution)/shard_map/all_gather | solution.py:90
  7.9 232.2 %all-gather.5.cloned.1.call-start = ((), (), s32[]{:S(2)}) async-start(), calls=%async_computation.13 | async-start | bytes 3194880 | tf_op jit(solution)/shard_map/all_gather | solution.py:91
  8.7 1352.5 %reduce-scatter.43.cloned.1.call-start = ((), (), s32[]{:S(2)}) async-start(), calls=%async_computation.19 | async-start | bytes 221184
  8.7 217.0 %collective-permute-start.8 = (bf16[1,768,1536]{2,1,0:T(8,128)(2,1)}, bf16[1,768,1536]{2,1,0:T(8,128)(2,1)}, u32[]{:S(2)}, u32[]{:S(2)}) collective-permute-start(bf16[1,768,1536]{2,1,0:T(8,128)(2,1)} %param.34), channel_id=1, source_target_pairs={{0,8},{8,0},{16,24},{24,16},{1,9},{9,1},{17,25},{25,17},{2,10},{10... | collective-permute-start | bytes 7077896 | tf_op jit(solution)/shard_map/ppermute | solution.py:21
  14.4 206.9 %collective-permute-start.2 = (bf16[1,768,1152]{1,2,0:T(8,128)(2,1)S(1)}, bf16[1,768,1152]{1,2,0:T(8,128)(2,1)S(1)}, u32[]{:S(2)}, u32[]{:S(2)}) collective-permute-start(bf16[1,768,1152]{1,2,0:T(8,128)(2,1)S(1)} %copy.169), channel_id=1, source_target_pairs={{0,8},{8,0},{16,24},{24,16},{1,9},{9,1},{17,25},{25,17},{2,10},{10... | collective-permute-start | bytes 5308424 | tf_op jit(solution)/shard_map/ppermute | solution.py:21
  14.4 217.0 %collective-permute-start.10 = (bf16[1,1536,768]{2,1,0:T(8,128)(2,1)}, bf16[1,1536,768]{2,1,0:T(8,128)(2,1)}, u32[]{:S(2)}, u32[]{:S(2)}) collective-permute-start(bf16[1,1536,768]{2,1,0:T(8,128)(2,1)} %param.36), channel_id=1, source_target_pairs={{0,8},{8,0},{16,24},{24,16},{1,9},{9,1},{17,25},{25,17},{2,10},{10... | collective-permute-start | bytes 7077896 | tf_op jit(solution)/shard_map/ppermute | solution.py:21
  16.5 176.5 %collective-permute-start.5 = (bf16[1,384]{1,0:T(2,128)(2,1)S(1)}, bf16[1,384]{1,0:T(2,128)(2,1)}, u32[]{:S(2)}, u32[]{:S(2)}) collective-permute-start(bf16[1,384]{1,0:T(2,128)(2,1)S(1)} %copy-done.29), channel_id=1, source_target_pairs={{0,8},{8,0},{16,24},{24,16},{1,9},{9,1},{17,25},{25,17},{2,10},{10... | collective-permute-start | bytes 2312 | tf_op jit(solution)/shard_map/ppermute | solution.py:21
  17.1 178.8 %collective-permute-start.6 = (bf16[1,384]{1,0:T(2,128)(2,1)}, bf16[1,384]{1,0:T(2,128)(2,1)S(1)}, u32[]{:S(2)}, u32[]{:S(2)}) collective-permute-start(bf16[1,384]{1,0:T(2,128)(2,1)} %param.32), channel_id=1, source_target_pairs={{0,8},{8,0},{16,24},{24,16},{1,9},{9,1},{17,25},{25,17},{2,10},{10... | collective-permute-start | bytes 2312 | tf_op jit(solution)/shard_map/ppermute | solution.py:21
  288.0 16.0 collective-permute-start
  512.1 43.2 %collective-permute-start = (bf16[520,768]{1,0:T(8,128)(2,1)}, bf16[520,768]{1,0:T(8,128)(2,1)S(1)}, u32[]{:S(2)}, u32[]{:S(2)}) collective-permute-start(bf16[520,768]{1,0:T(8,128)(2,1)} %get-tuple-element.3144), channel_id=1, source_target_pairs={{0,8},{8,16},{16,24},{1,9},{9,17},{17,25},{2,10},{10,18},{18,26},{... | collective-permute-start | bytes 2396168 | tf_op jit(solution)/shard_map/while/body/eval_jaxpr/ppermute | solution.py:27
  557.7 19.1 collective-permute-start
  620.3 68.2 %collective-permute-start.1 = (bf16[520,768]{1,0:T(8,128)(2,1)}, bf16[520,768]{1,0:T(8,128)(2,1)S(1)}, u32[]{:S(2)}, u32[]{:S(2)}) collective-permute-start(bf16[520,768]{1,0:T(8,128)(2,1)} %get-tuple-element.3250), channel_id=1, source_target_pairs={{8,0},{16,8},{24,16},{9,1},{17,9},{25,17},{10,2},{18,10},{26,18},{... | collective-permute-start | bytes 2396168 | tf_op jit(solution)/shard_map/while/body/eval_jaxpr/ppermute | solution.py:27
  696.0 15.5 collective-permute-start.1
  719.0 39.0 %collective-permute-start.1 = (bf16[520,768]{1,0:T(8,128)(2,1)}, bf16[520,768]{1,0:T(8,128)(2,1)S(1)}, u32[]{:S(2)}, u32[]{:S(2)}) collective-permute-start(bf16[520,768]{1,0:T(8,128)(2,1)} %get-tuple-element.3250), channel_id=1, source_target_pairs={{8,0},{16,8},{24,16},{9,1},{17,9},{25,17},{10,2},{18,10},{26,18},{... | collective-permute-start | bytes 2396168 | tf_op jit(solution)/shard_map/while/body/eval_jaxpr/ppermute | solution.py:27
  765.5 210.3 %collective-permute-start.1 = (bf16[520,768]{1,0:T(8,128)(2,1)}, bf16[520,768]{1,0:T(8,128)(2,1)S(1)}, u32[]{:S(2)}, u32[]{:S(2)}) collective-permute-start(bf16[520,768]{1,0:T(8,128)(2,1)} %get-tuple-element.3250), channel_id=1, source_target_pairs={{8,0},{16,8},{24,16},{9,1},{17,9},{25,17},{10,2},{18,10},{26,18},{... | collective-permute-start | bytes 2396168 | tf_op jit(solution)/shard_map/while/body/eval_jaxpr/ppermute | solution.py:27
  1070.6 14.2 collective-permute-start.1
  1179.5 14.2 collective-permute-start.1
  1295.8 66.2 %reduce-scatter.45.cloned.1.call-start = ((), (), s32[]{:S(2)}) async-start(), calls=%async_computation.20 | async-start | bytes 221184
  1296.7 89.0 %reduce-scatter.47.cloned.1.call-start = ((), (), s32[]{:S(2)}) async-start(), calls=%async_computation.21 | async-start | bytes 221184
  1297.6 118.7 %reduce-scatter.51.cloned.1.call-start = ((), (), s32[]{:S(2)}) async-start(), calls=%async_computation.23 | async-start | bytes 221184
  1298.5 148.5 %reduce-scatter.53.cloned.1.call-start = ((), (), s32[]{:S(2)}) async-start(), calls=%async_computation.24 | async-start | bytes 221184
  1299.5 178.3 %reduce-scatter.55.cloned.1.call-start = ((), (), s32[]{:S(2)}) async-start(), calls=%async_computation.25 | async-start | bytes 221184
  1300.4 209.0 %reduce-scatter.41.cloned.1.call-start = ((), (), s32[]{:S(2)}) async-start(), calls=%async_computation.18 | async-start | bytes 442368
  1301.4 240.4 %reduce-scatter.49.cloned.1.call-start = ((), (), s32[]{:S(2)}) async-start(), calls=%async_computation.22 | async-start | bytes 884736
  1302.7 275.9 %reduce-scatter.33.cloned.1.call-start = ((), (), s32[]{:S(2)}) async-start(), calls=%async_computation.14 | async-start | bytes 2654208 | tf_op jit(solution)/shard_map/reduce_scatter | solution.py:461
  1303.5 316.4 %reduce-scatter.39.cloned.1.call-start = ((), (), s32[]{:S(2)}) async-start(), calls=%async_computation.17 | async-start | bytes 3194880
  1310.3 640.9 %all-reduce.5.cloned.1.call-start = ((), (), s32[]{:S(2)}) async-start(), calls=%async_computation.26 | async-start | bytes 33030144
  1352.4 700.7 %reduce-scatter.35.cloned.1.call-start = ((), (), s32[]{:S(2)}) async-start(), calls=%async_computation.15 | async-start | bytes 10616832 | tf_op jit(solution)/shard_map/reduce_scatter | solution.py:467
  1353.0 741.3 %reduce-scatter.37.cloned.1.call-start = ((), (), s32[]{:S(2)}) async-start(), calls=%async_computation.16 | async-start | bytes 3194880
  1544.0 37.2 %collective-permute-start.21 = (bf16[192]{0:T(256)(128)(2,1)S(1)}, bf16[192]{0:T(256)(128)(2,1)S(1)}, u32[]{:S(2)}, u32[]{:S(2)}) collective-permute-start(bf16[192]{0:T(256)(128)(2,1)S(1)} %convert_reduce_fusion.1), channel_id=1, source_target_pairs={{0,8},{8,0},{16,24},{24,16},{1,9},{9,1},{17,25},{25,17},{2,10},{10... | collective-permute-start | bytes 1160 | tf_op jit(solution)/shard_map/ppermute | solution.py:21
  1579.6 43.0 %collective-permute-start.16 = (bf16[48,768]{1,0:T(8,128)(2,1)S(1)}, bf16[48,768]{1,0:T(8,128)(2,1)S(1)}, u32[]{:S(2)}, u32[]{:S(2)}) collective-permute-start(bf16[48,768]{1,0:T(8,128)(2,1)S(1)} %fusion.114), channel_id=1, source_target_pairs={{0,8},{8,0},{16,24},{24,16},{1,9},{9,1},{17,25},{25,17},{2,10},{10... | collective-permute-start | bytes 221192 | tf_op jit(solution)/shard_map/ppermute | solution.py:21
  1956.2 99.6 %collective-permute-start.20 = (bf16[96,1536]{1,0:T(8,128)(2,1)S(1)}, bf16[96,1536]{1,0:T(8,128)(2,1)S(1)}, u32[]{:S(2)}, u32[]{:S(2)}) collective-permute-start(bf16[96,1536]{1,0:T(8,128)(2,1)S(1)} %bitcast.343), channel_id=1, source_target_pairs={{0,8},{8,0},{16,24},{24,16},{1,9},{9,1},{17,25},{25,17},{2,10},{10... | collective-permute-start | bytes 884744 | tf_op jit(solution)/shard_map/ppermute | solution.py:21
  (67 other events, 331.5 us)
Sparse Core Ops, SparseCore 0:
  9.9 62.2 all-gather.2
  74.0 59.5 all-gather.4
  1295.9 28.0 reduce-scatter.42
  1326.8 28.4 reduce-scatter.44
  1357.3 28.3 reduce-scatter.46
  1387.9 28.3 reduce-scatter.50
  1418.6 28.3 reduce-scatter.52
  1449.3 28.3 reduce-scatter.54
  1480.6 28.7 reduce-scatter.40
  1512.2 29.5 reduce-scatter.48
  1544.2 34.3 reduce-scatter.32
  1581.6 38.2 reduce-scatter.38
  1622.5 328.6 all-reduce.4
  1953.5 99.6 reduce-scatter.34
  2056.9 37.3 reduce-scatter.36
where the time goes:
time: 2110 us; the launch traced here: 2100 us
  waiting for transfers between devices  1250 us (59%)
  local copies, waits for them, and re-layouts  474 us (22%)
  matrix products  122 us (6%)
  other arithmetic  95 us (5%)
  starting transfers between devices  86.3 us (4%)
  loops' own time  54.1 us (3%)
    unnamed x26, waiting for transfers between devices  558 us
    ppermute x12, waiting for transfers between devices, passed_along(): return lax.ppermute(value, axis, pairs)  386 us
    ppermute x24, waiting for transfers between devices, from_partner(): lax.ppermute(value, axis, [(i, i ^ 1 << distance) for i in range(lax.axis...  187 us
    another operation x24, local copies, waits for them, and re-layouts  96.9 us
    reduce_scatter x1, waiting for transfers between devices, shards(): lax.psum_scatter(grad_halves[8], 'dp', scatter_dimension=1, tiled=True)  91.1 us
    ppermute x12, starting transfers between devices, passed_along(): return lax.ppermute(value, axis, pairs)  56.1 us
  transfers between devices with their start and end apart: 51, of which 32 were waited for; matrix products, arithmetic and copies ran while one was open for 8% of the time, Pallas kernels for 0%

commit v1 on v0

v1 whole, which is shorter than its diff:
```python
import functools

import jax
import jax.numpy as jnp
from jax import lax
from jax.experimental import pallas as pl
from jax.experimental.pallas import tpu as pltpu
from jax.sharding import PartitionSpec as P

D = 768
HEADS = 12
HEAD_DIM = 64
FF = 3072
WORDS = 64
PAIR_ROWS = 104
HALF = D // 2
HIDDEN_HALF = FF // 2
QUARTER = D // 4
PIPE = 4
KEYS = 128
GROUP = 4
GROUP_WIDTH = GROUP * HEAD_DIM
GROUPS = HEADS // GROUP

EPSILON = 1e-05
NEGATIVE = -1e30
SCALE = HEAD_DIM ** (-0.5)

MESH = pl.DeviceIdType.MESH
BF = jnp.bfloat16
F32 = jnp.float32
VMEM_LIMIT = 60 << 20


def dot_nn(left, right):
    return lax.dot_general(left, right, (((1,), (0,)), ((), ())), preferred_element_type=F32)


def dot_nt(left, right):
    return lax.dot_general(left, right, (((1,), (1,)), ((), ())), preferred_element_type=F32)


def dot_tn(left, right):
    return lax.dot_general(left, right, (((0,), (0,)), ((), ())), preferred_element_type=F32)


def place():
    pipe = lax.axis_index("pipe")
    dp = lax.axis_index("dp")
    layer = pipe // 2
    half = pipe % 2
    across_x = pipe + 1 - 2 * half
    across_y = (pipe + 2) % 4
    core = dp % 2
    other_core = dp + 1 - 2 * core
    return pipe, dp, layer, half, across_x, across_y, core, other_core


def greet(devices):
    barrier = pltpu.get_barrier_semaphore()
    for device in devices:
        pl.semaphore_signal(barrier, inc=1, device_id=device, device_id_type=MESH)
    pl.semaphore_wait(barrier, len(devices))


def remote(source, target, send, recv, device):
    return pltpu.make_async_remote_copy(
        src_ref=source,
        dst_ref=target,
        send_sem=send,
        recv_sem=recv,
        device_id=device,
        device_id_type=MESH,
    )


def gather_kernel(
    rows,
    both, projection, combiner, expansion, reduction, vectors,
    pieces, joint, mixing, expand, reduce, whole_vectors,
    send, recv, local_sem, piece_send, piece_recv, vec_sem,
):
    pipe, dp, layer, half, across_x, across_y, core, other_core = place()
    diagonal = (across_x + 2) % 4
    parity = (dp // 2) % 2
    across_z = dp + 2 - 4 * parity
    greet([(across_x, dp), (across_y, dp), (diagonal, dp), (pipe, across_z), (pipe, other_core)])

    def regions(owner_half, quarter):
        found = []
        for part in range(3):
            r = D // 4
            found.append((
                projection.at[pl.ds(quarter * r, r), pl.ds(part * HALF, HALF)],
                joint.at[pl.ds(quarter * r, r), pl.ds(pl.multiple_of(part * D + owner_half * HALF, 128), HALF)],
            ))
        r = HALF // 4
        found.append((
            combiner.at[pl.ds(quarter * r, r)],
            mixing.at[pl.ds(owner_half * HALF + quarter * r, r)],
        ))
        r = D // 4
        found.append((
            expansion.at[pl.ds(quarter * r, r)],
            expand.at[pl.ds(quarter * r, r), pl.ds(pl.multiple_of(owner_half * HIDDEN_HALF, 128), HIDDEN_HALF)],
        ))
        r = HIDDEN_HALF // 4
        found.append((
            reduction.at[pl.ds(quarter * r, r)],
            reduce.at[pl.ds(owner_half * HIDDEN_HALF + quarter * r, r)],
        ))
        return found

    mine = 2 * parity + core
    paired = 2 * (1 - parity) + core
    own = regions(half, mine)
    got_x = regions(1 - half, mine)
    got_z = regions(1 - half, paired)
    n = len(own)
    sent = []

    vec_copy = remote(vectors, whole_vectors.at[half], vec_sem.at[0], vec_sem.at[1], (across_x, dp))
    vec_copy.start()
    x_copies = []
    for i in range(4):
        copy = remote(own[i][0], own[i][1], send.at[0, i], recv.at[0, i], (across_x, dp))
        copy.start()
        x_copies.append(copy)
    piece_copies = []
    for j, target in enumerate((across_x, across_y, diagonal)):
        copy = remote(
            both.at[target // 2, pl.ds((target % 2) * rows, rows)],
            pieces.at[pipe],
            piece_send.at[j], piece_recv.at[j],
            (target, dp),
        )
        copy.start()
        piece_copies.append(copy)
    for i in range(4, n):
        copy = remote(own[i][0], own[i][1], send.at[0, i], recv.at[0, i], (across_x, dp))
        copy.start()
        x_copies.append(copy)

    locals_ = [
        pltpu.make_async_copy(both.at[layer, pl.ds(half * rows, rows)], pieces.at[pipe], local_sem.at[0]),
        pltpu.make_async_copy(vectors, whole_vectors.at[half], local_sem.at[1]),
        pltpu.make_async_copy(combiner, mixing.at[pl.ds(half * HALF, HALF)], local_sem.at[2]),
        pltpu.make_async_copy(
            expansion, expand.at[:, pl.ds(pl.multiple_of(half * HIDDEN_HALF, 128), HIDDEN_HALF)], local_sem.at[3]
        ),
        pltpu.make_async_copy(reduction, reduce.at[pl.ds(half * HIDDEN_HALF, HIDDEN_HALF)], local_sem.at[4]),
    ]
    for part in range(3):
        locals_.append(
            pltpu.make_async_copy(
                projection.at[:, pl.ds(part * HALF, HALF)],
                joint.at[:, pl.ds(pl.multiple_of(part * D + half * HALF, 128), HALF)],
                local_sem.at[5 + part],
            )
        )
    for copy in locals_:
        copy.start()

    z_copies = []
    core_copies = []
    for i in range(n):
        x_copies[i].wait_recv()
        copy = remote(got_x[i][1], got_x[i][1], send.at[1, i], recv.at[1, i], (pipe, across_z))
        copy.start()
        z_copies.append(copy)
        copy = remote(got_x[i][1], got_x[i][1], send.at[2, i], recv.at[2, i], (pipe, other_core))
        copy.start()
        core_copies.append(copy)
    for i in range(n):
        z_copies[i].wait_recv()
        copy = remote(got_z[i][1], got_z[i][1], send.at[3, i], recv.at[3, i], (pipe, other_core))
        copy.start()
        core_copies.append(copy)
    for copy in core_copies:
        copy.wait_recv()
    for copy in x_copies + z_copies + core_copies:
        copy.wait_send()
    for copy in piece_copies + [vec_copy]:
        copy.wait()
    for copy in locals_:
        copy.wait()


def gather(rows, both, projection, combiner, expansion, reduction, vectors):
    hbm = pl.BlockSpec(memory_space=pl.ANY)
    return pl.pallas_call(
        functools.partial(gather_kernel, rows),
        out_shape=(
            jax.ShapeDtypeStruct((PIPE, rows, QUARTER), BF),
            jax.ShapeDtypeStruct((D, 3 * D), BF),
            jax.ShapeDtypeStruct((D, D), BF),
            jax.ShapeDtypeStruct((D, FF), BF),
            jax.ShapeDtypeStruct((FF, D), BF),
            jax.ShapeDtypeStruct((2,) + vectors.shape, BF),
        ),
        in_specs=[hbm] * 6,
        out_specs=(hbm,) * 6,
        scratch_shapes=[
            pltpu.SemaphoreType.DMA((4, 6)),
            pltpu.SemaphoreType.DMA((4, 6)),
            pltpu.SemaphoreType.DMA((8,)),
            pltpu.SemaphoreType.DMA((3,)),
            pltpu.SemaphoreType.DMA((3,)),
            pltpu.SemaphoreType.DMA((2,)),
        ],
        compiler_params=pltpu.CompilerParams(collective_id=0, has_side_effects=True, vmem_limit_bytes=VMEM_LIMIT),
        name="gather_weights",
    )(both, projection, combiner, expansion, reduction, vectors)


def head_of_lane():
    return lax.broadcasted_iota(jnp.int32, (KEYS, GROUP_WIDTH), 1) // HEAD_DIM


def stacked_keys(values, scale=None):
    padded = jnp.concatenate([values, jnp.zeros((KEYS - PAIR_ROWS, GROUP_WIDTH), F32)], 0)
    if scale is not None:
        padded = padded * scale
    owner = head_of_lane()
    return jnp.concatenate([jnp.where(owner == i, padded, 0.0) for i in range(GROUP)], 0).astype(BF)


def own_lanes(stacked):
    left = lax.broadcasted_iota(jnp.int32, (KEYS, KEYS), 1) < HEAD_DIM
    low = jnp.where(left, stacked[0:KEYS, :KEYS], stacked[KEYS : 2 * KEYS, :KEYS])
    high = jnp.where(left, stacked[2 * KEYS : 3 * KEYS, KEYS:], stacked[3 * KEYS :, KEYS:])
    return jnp.concatenate([low, high], 1)[:PAIR_ROWS]


def normalized(residual):
    average = jnp.mean(residual, axis=-1, keepdims=True)
    centred = residual - average
    variance = jnp.mean(centred * centred, axis=-1, keepdims=True)
    inverse = lax.rsqrt(variance + EPSILON)
    return centred * inverse, inverse


def forward_kernel(
    micros, block,
    pieces, masks, joint, mixing, expand, reduce, vectors,
    a0_out, qkv_out, prob_out, context_out, n1_out, r1_out, a1_out, hidden_out, slope_out, n2_out, r2_out, y2_out,
    slots, outgoing, a_s, qkv_s, prob_s, context_s, send, recv,
):
    pipe, dp, layer, half, across_x, across_y, core, other_core = place()
    micro = pl.program_id(0)
    pairs = block // PAIR_ROWS

    @pl.when(micro == 0)
    def _():
        greet([(across_y, dp)])

    def copy_of(index):
        return remote(outgoing.at[index], slots.at[index], send.at[index], recv.at[index], (across_y, dp))

    @pl.when(layer == 0)
    def _():
        a_s[...] = jnp.concatenate([pieces[i] for i in range(PIPE)], 1)

    @pl.when(layer == 1)
    def _():
        copy_of(micro).wait_recv()
        a_s[...] = slots[micro]

    inputs = a_s[...]
    a0_out[...] = inputs
    for part in range(3):
        cols = slice(part * D, (part + 1) * D)
        value = dot_nn(inputs, joint[:, cols]) + vectors[0:1, cols]
        qkv_s[:, cols] = value
        qkv_out[:, cols] = value.astype(BF)
    for pair in range(pairs):
        rows = slice(pair * PAIR_ROWS, (pair + 1) * PAIR_ROWS)
        mask = masks[pl.ds(micro * pairs + pair, 1), :]
        for group in range(GROUPS):
            lanes = slice(group * GROUP_WIDTH, (group + 1) * GROUP_WIDTH)
            query = qkv_s[rows, group * GROUP_WIDTH : (group + 1) * GROUP_WIDTH].astype(BF)
            keys = stacked_keys(qkv_s[rows, D + group * GROUP_WIDTH : D + (group + 1) * GROUP_WIDTH], SCALE)
            values = stacked_keys(qkv_s[rows, 2 * D + group * GROUP_WIDTH : 2 * D + (group + 1) * GROUP_WIDTH])
            scores = dot_nt(query, keys)
            found = []
            for i in range(GROUP):
                score = scores[:, i * KEYS : (i + 1) * KEYS] + mask
                exponent = jnp.exp(score - jnp.max(score, axis=-1, keepdims=True))
                found.append(exponent * (1.0 / jnp.sum(exponent, axis=-1, keepdims=True)))
            probs = jnp.concatenate(found, 1)
            prob_s[rows, group * GROUP * KEYS : (group + 1) * GROUP * KEYS] = probs
            context_s[rows, lanes] = dot_nn(probs.astype(BF), values)
    prob_out[...] = prob_s[...].astype(BF)
    context = context_s[...].astype(BF)
    context_out[...] = context
    residual = inputs.astype(F32) + dot_nn(context, mixing[...]) + vectors[1:2, :D]
    norm, inverse = normalized(residual)
    n1_out[...] = norm.astype(BF)
    r1_out[...] = inverse
    attended = (norm * vectors[2:3, :D] + vectors[3:4, :D]).astype(BF)
    a1_out[...] = attended

    chunk = 512
    residual = attended.astype(F32) + vectors[5:6, :D]
    for start in range(0, FF, chunk):
        cols = slice(start, start + chunk)
        raised = dot_nn(attended, expand[:, cols]) + vectors[4:5, cols]
        below = 0.5 * (1.0 + lax.erf(raised * (0.5**0.5)))
        hidden = (raised * below).astype(BF)
        hidden_out[:, cols] = hidden
        density = jnp.exp(raised * raised * (-0.5)) * 0.3989422804014327
        slope_out[:, cols] = (below + raised * density).astype(BF)
        residual = residual + dot_nn(hidden, reduce[cols, :])
    norm, inverse = normalized(residual)
    n2_out[...] = norm.astype(BF)
    r2_out[...] = inverse
    result = (norm * vectors[6:7, :D] + vectors[7:8, :D]).astype(BF)
    for i in range(PIPE):
        y2_out[i] = result[:, i * QUARTER : (i + 1) * QUARTER]

    @pl.when(layer == 0)
    def _():
        outgoing[micro] = result
        copy_of(micro).start()

    @pl.when((layer == 0) & (micro == micros - 1))
    def _():
        for index in range(micros):
            copy_of(index).wait_send()


def forward(micros, block, pieces, masks, joint, mixing, expand, reduce, vectors):
    rows = micros * block

    def whole(array):
        return pl.BlockSpec(array.shape, lambda m: (0,) * array.ndim, pipeline_mode=pl.Buffered(1))

    def by_rows(width):
        return pl.BlockSpec((block, width), lambda m: (m, 0))

    by_pieces = pl.BlockSpec((PIPE, block, QUARTER), lambda m: (0, m, 0))
    widths = [D, 3 * D, HEADS * KEYS, D, D, 1, D, FF, FF, D, 1]
    types = [BF, BF, BF, BF, BF, F32, BF, BF, BF, BF, F32]
    return pl.pallas_call(
        functools.partial(forward_kernel, micros, block),
        grid=(micros,),
        out_shape=[jax.ShapeDtypeStruct((rows, w), t) for w, t in zip(widths, types)]
        + [jax.ShapeDtypeStruct((PIPE, rows, QUARTER), BF)],
        in_specs=[by_pieces] + [whole(a) for a in (masks, joint, mixing, expand, reduce, vectors)],
        out_specs=[by_rows(w) for w in widths] + [by_pieces],
        scratch_shapes=[
            pltpu.VMEM((micros, block, D), BF),
            pltpu.VMEM((micros, block, D), BF),
            pltpu.VMEM((block, D), BF),
            pltpu.VMEM((block, 3 * D), F32),
            pltpu.VMEM((block, HEADS * KEYS), F32),
            pltpu.VMEM((block, D), F32),
            pltpu.SemaphoreType.DMA((micros,)),
            pltpu.SemaphoreType.DMA((micros,)),
        ],
        compiler_params=pltpu.CompilerParams(collective_id=1, has_side_effects=True, vmem_limit_bytes=VMEM_LIMIT),
        name="layer_forward",
    )(pieces, masks, joint, mixing, expand, reduce, vectors)


def norm_backward(gradient, norm, inverse, gain):
    scaled = gradient * gain
    first = jnp.mean(scaled, axis=-1, keepdims=True)
    second = jnp.mean(scaled * norm, axis=-1, keepdims=True)
    return (scaled - first - norm * second) * inverse


def column_sums(value):
    return jnp.sum(value, axis=0, keepdims=True)


def backward_kernel(
    micros, block,
    pieces, joint, mixing, expand, reduce, vectors,
    n2, r2, slope, n1, r1, qkv, prob,
    dr2_out, du_out, dr1_out, dqkv_out, da_out, sums_out,
    slots, outgoing, g_s, qkv_s, prob_s, dc_s, dqkv_s, send, recv,
):
    pipe, dp, layer, half, across_x, across_y, core, other_core = place()
    micro = pl.program_id(0)
    pairs = block // PAIR_ROWS

    @pl.when(micro == 0)
    def _():
        greet([(across_y, dp)])
        sums_out[...] = jnp.zeros_like(sums_out)

    def copy_of(index):
        return remote(outgoing.at[index], slots.at[index], send.at[index], recv.at[index], (across_y, dp))

    @pl.when(layer == 1)
    def _():
        g_s[...] = jnp.concatenate([pieces[i] for i in range(PIPE)], 1)

    @pl.when(layer == 0)
    def _():
        copy_of(micro).wait_recv()
        g_s[...] = slots[micro]

    def add_sum(row, value):
        width = value.shape[1]
        sums_out[row : row + 1, :width] += column_sums(value)

    gradient = g_s[...].astype(F32)
    norm = n2[...].astype(F32)
    add_sum(6, gradient * norm)
    add_sum(7, gradient)
    grad_residual = norm_backward(gradient, norm, r2[...], vectors[6:7, :D])
    add_sum(5, grad_residual)
    branch = grad_residual.astype(BF)
    dr2_out[...] = branch
    chunk = 512
    total = grad_residual
    for start in range(0, FF, chunk):
        cols = slice(start, start + chunk)
        raised = dot_nt(branch, reduce[cols, :]) * slope[:, cols].astype(F32)
        sums_out[4:5, cols] += column_sums(raised)
        raised = raised.astype(BF)
        du_out[:, cols] = raised
        total = total + dot_nt(raised, expand[:, cols])

    gradient = total.astype(BF).astype(F32)
    norm = n1[...].astype(F32)
    add_sum(2, gradient * norm)
    add_sum(3, gradient)
    grad_residual = norm_backward(gradient, norm, r1[...], vectors[2:3, :D])
    add_sum(1, grad_residual)
    branch = grad_residual.astype(BF)
    dr1_out[...] = branch
    dc_s[...] = dot_nt(branch, mixing[...])
    qkv_s[...] = qkv[...].astype(F32)
    prob_s[...] = prob[...].astype(F32)
    for pair in range(pairs):
        rows = slice(pair * PAIR_ROWS, (pair + 1) * PAIR_ROWS)
        for group in range(GROUPS):
            lanes = [
                slice(part * D + group * GROUP_WIDTH, part * D + (group + 1) * GROUP_WIDTH) for part in range(3)
            ]
            query = qkv_s[rows, lanes[0]].astype(BF)
            keys = stacked_keys(qkv_s[rows, lanes[1]], SCALE)
            values = stacked_keys(qkv_s[rows, lanes[2]])
            grad_context = dc_s[rows, lanes[0]].astype(BF)
            probs = prob_s[rows, group * GROUP * KEYS : (group + 1) * GROUP * KEYS]
            grad_probs = dot_nt(grad_context, values)
            found = []
            for i in range(GROUP):
                at = slice(i * KEYS, (i + 1) * KEYS)
                weighted = probs[:, at] * grad_probs[:, at]
                found.append(weighted - probs[:, at] * jnp.sum(weighted, axis=-1, keepdims=True))
            grad_scores = jnp.concatenate(found, 1).astype(BF)
            dqkv_s[rows, lanes[0]] = dot_nn(grad_scores, keys)
            dqkv_s[rows, lanes[1]] = own_lanes(dot_tn(grad_scores, query)) * SCALE
            dqkv_s[rows, lanes[2]] = own_lanes(dot_tn(probs.astype(BF), grad_context))
    total = grad_residual
    for part in range(3):
        cols = slice(part * D, (part + 1) * D)
        value = dqkv_s[:, cols].astype(BF)
        dqkv_out[:, cols] = value
        sums_out[0:1, cols] += column_sums(value.astype(F32))
        total = total + dot_nt(value, joint[:, cols])
    result = total.astype(BF)
    for i in range(PIPE):
        da_out[i] = result[:, i * QUARTER : (i + 1) * QUARTER]

    @pl.when(layer == 1)
    def _():
        outgoing[micro] = result
        copy_of(micro).start()

    @pl.when((layer == 1) & (micro == micros - 1))
    def _():
        for index in range(micros):
            copy_of(index).wait_send()


def backward(micros, block, pieces, joint, mixing, expand, reduce, vectors, n2, r2, slope, n1, r1, qkv, prob):
    rows = micros * block

    def whole(array):
        return pl.BlockSpec(array.shape, lambda m: (0,) * array.ndim, pipeline_mode=pl.Buffered(1))

    def by_rows(width):
        return pl.BlockSpec((block, width), lambda m: (m, 0))

    by_pieces = pl.BlockSpec((PIPE, block, QUARTER), lambda m: (0, m, 0))
    kept = (n2, r2, slope, n1, r1, qkv, prob)
    widths = [D, FF, D, 3 * D]
    return pl.pallas_call(
        functools.partial(backward_kernel, micros, block),
        grid=(micros,),
        out_shape=[jax.ShapeDtypeStruct((rows, w), BF) for w in widths]
        + [jax.ShapeDtypeStruct((PIPE, rows, QUARTER), BF), jax.ShapeDtypeStruct((8, FF), F32)],
        in_specs=[by_pieces]
        + [whole(a) for a in (joint, mixing, expand, reduce, vectors)]
        + [by_rows(a.shape[1]) for a in kept],
        out_specs=[by_rows(w) for w in widths] + [by_pieces, pl.BlockSpec((8, FF), lambda m: (0, 0))],
        scratch_shapes=[
            pltpu.VMEM((micros, block, D), BF),
            pltpu.VMEM((micros, block, D), BF),
            pltpu.VMEM((block, D), BF),
            pltpu.VMEM((block, 3 * D), F32),
            pltpu.VMEM((block, HEADS * KEYS), F32),
            pltpu.VMEM((block, D), F32),
            pltpu.VMEM((block, 3 * D), F32),
            pltpu.SemaphoreType.DMA((micros,)),
            pltpu.SemaphoreType.DMA((micros,)),
        ],
        compiler_params=pltpu.CompilerParams(collective_id=2, has_side_effects=True, vmem_limit_bytes=VMEM_LIMIT),
        name="layer_backward",
    )(pieces, joint, mixing, expand, reduce, vectors, *kept)


TILE = 384


def weights_kernel(
    n_dp,
    a0, dqkv, context, dr1, a1, du, hidden, dr2, sums, y2, da,
    g_proj, g_comb, g_exp, g_red, sums_out, pieces_out,
    b_proj, b_comb, b_exp, b_red,
    c_proj, c_comb, c_exp, c_red,
    x_proj, x_comb, x_exp, x_red,
    z_proj, z_comb, z_exp, z_red,
    sums_core, sums_x, sums_z, sums_a, sums_b,
    core_send, core_recv, x_send, x_recv, z_send, z_recv, piece_send, piece_recv, local_sem,
):
    pipe, dp, layer, half, across_x, across_y, core, other_core = place()
    diagonal = (across_x + 2) % 4
    n_z = n_dp // 2
    z = dp // 2
    z_others = [(z + step) % n_z for step in range(1, n_z)]
    greet(
        [(across_x, dp), (across_y, dp), (diagonal, dp), (pipe, other_core)]
        + [(pipe, 2 * other + core) for other in z_others]
    )

    waits = []
    for j, target in enumerate((across_x, across_y, diagonal)):

        @pl.when(layer == 0)
        def _():
            remote(da.at[target], pieces_out.at[pipe], piece_send.at[j], piece_recv.at[j], (target, dp)).start()

        @pl.when(layer == 1)
        def _():
            remote(y2.at[target], pieces_out.at[pipe], piece_send.at[j], piece_recv.at[j], (target, dp)).start()

        waits.append(remote(da.at[target], pieces_out.at[pipe], piece_send.at[j], piece_recv.at[j], (target, dp)))

    @pl.when(layer == 0)
    def _():
        pltpu.make_async_copy(da.at[pipe], pieces_out.at[pipe], local_sem.at[0]).start()

    @pl.when(layer == 1)
    def _():
        pltpu.make_async_copy(y2.at[pipe], pieces_out.at[pipe], local_sem.at[0]).start()

    own_piece = pltpu.make_async_copy(da.at[pipe], pieces_out.at[pipe], local_sem.at[0])

    mine = [b_red, b_exp, b_proj, b_comb]
    from_core = [c_red, c_exp, c_proj, c_comb]
    from_x = [x_red, x_exp, x_proj, x_comb]
    from_z = [z_red, z_exp, z_proj, z_comb]
    outs = [g_red, g_exp, g_proj, g_comb]

    def fill_red(i, carry):
        lanes = pl.ds(pl.multiple_of(i * TILE, 128), TILE)
        tile = dot_tn(hidden[:, lanes], dr2[...])
        per_half = HIDDEN_HALF // TILE
        r = b_red.shape[3]
        per = TILE // r // 2
        for k in range(per):
            for c in range(2):
                b_red[c, i // per_half, (i % per_half) * per + k] = tile[(2 * k + c) * r : (2 * k + c + 1) * r].astype(BF)
        return carry

    def fill_exp(step, carry):
        i, j = step // 4, step % 4
        r = b_exp.shape[3]
        per = TILE // r // 2
        tile = dot_tn(
            a1[:, pl.ds(pl.multiple_of(i * TILE, 128), TILE)], du[:, pl.ds(pl.multiple_of(j * D, 128), D)]
        )
        lanes = pl.ds(pl.multiple_of((j % 2) * D, 128), D)
        for k in range(per):
            for c in range(2):
                b_exp[c, j // 2, i * per + k, :, lanes] = tile[(2 * k + c) * r : (2 * k + c + 1) * r].astype(BF)
        return carry

    def fill_proj(step, carry):
        i, j = step // 3, step % 3
        r = b_proj.shape[3]
        per = TILE // r // 2
        tile = dot_tn(
            a0[:, pl.ds(pl.multiple_of(i * TILE, 128), TILE)], dqkv[:, pl.ds(pl.multiple_of(j * D, 128), D)]
        )
        lanes = pl.ds(pl.multiple_of(j * HALF, 128), HALF)
        for k in range(per):
            for c in range(2):
                rows = tile[(2 * k + c) * r : (2 * k + c + 1) * r].astype(BF)
                b_proj[c, 0, i * per + k, :, lanes] = rows[:, :HALF]
                b_proj[c, 1, i * per + k, :, lanes] = rows[:, HALF:]
        return carry

    def fill_comb(i, carry):
        r = b_comb.shape[3]
        per = TILE // r // 2
        tile = dot_tn(context[:, pl.ds(pl.multiple_of(i * TILE, 128), TILE)], dr1[...])
        for k in range(per):
            for c in range(2):
                b_comb[c, i, k] = tile[(2 * k + c) * r : (2 * k + c + 1) * r].astype(BF)
        return carry

    fills = [(fill_red, FF // TILE), (fill_exp, 4 * D // TILE), (fill_proj, 3 * D // TILE), (fill_comb, D // TILE)]

    def core_copy(a):
        return remote(mine[a].at[1 - core], from_core[a], core_send.at[a], core_recv.at[a], (pipe, other_core))

    def x_copy(a):
        return remote(mine[a].at[core, 1 - half], from_x[a], x_send.at[a], x_recv.at[a], (across_x, dp))

    def z_copy(a, step):
        other = z_others[step]
        return remote(
            mine[a].at[core, half, other], from_z[a].at[step], z_send.at[a, step], z_recv.at[a, step],
            (pipe, 2 * other + core),
        )

    def after_core(a):
        core_copy(a).wait()

        @pl.loop(0, n_z)
        def _(k):
            total = mine[a][core, 1 - half, k].astype(F32) + from_core[a][1 - half, k].astype(F32)
            mine[a][core, 1 - half, k] = total.astype(BF)

        x_copy(a).start()

    def after_x(a):
        x_copy(a).wait()

        def total_of(k):
            return (
                mine[a][core, half, k].astype(F32) + from_core[a][half, k].astype(F32) + from_x[a][k].astype(F32)
            )

        for step, other in enumerate(z_others):
            mine[a][core, half, other] = total_of(other).astype(BF)
            z_copy(a, step).start()
        outs[a][...] = total_of(z)

    def after_z(a):
        for step in range(n_z - 1):
            z_copy(a, step).wait()
        total = outs[a][...]
        for step in range(n_z - 1):
            total = total + from_z[a][step].astype(F32)
        outs[a][...] = total

    small = 4
    sums_copy_core = remote(sums, sums_core, core_send.at[small], core_recv.at[small], (pipe, other_core))
    sums_copy_x = remote(sums_a, sums_x, x_send.at[small], x_recv.at[small], (across_x, dp))
    sums_copies_z = [
        remote(
            sums_b, sums_z.at[step], z_send.at[small, step], z_recv.at[small, step], (pipe, 2 * other + core)
        )
        for step, other in enumerate(z_others)
    ]

    sums_copy_core.start()
    for a, (fill, count) in enumerate(fills):
        lax.fori_loop(0, count, fill, 0)
        core_copy(a).start()
        if a == 0:
            sums_copy_core.wait()
            sums_a[...] = sums[...] + sums_core[...]
            sums_copy_x.start()
        else:
            after_core(a - 1)
    after_core(3)
    sums_copy_x.wait()
    sums_b[...] = sums_a[...] + sums_x[...]
    for copy in sums_copies_z:
        copy.start()
    for a in range(4):
        after_x(a)
    for a in range(4):
        after_z(a)
    total = sums_b[...]
    for step in range(n_z - 1):
        sums_copies_z[step].wait()
        total = total + sums_z[step]
    sums_out[...] = total
    own_piece.wait()
    for copy in waits:
        copy.wait()


def weight_gradients(n_dp, a0, dqkv, context, dr1, a1, du, hidden, dr2, sums, y2, da):
    vmem = pl.BlockSpec(memory_space=pltpu.VMEM)
    hbm = pl.BlockSpec(memory_space=pl.ANY)
    n_z = n_dp // 2
    shapes = [(D // n_dp, 3 * HALF), (HALF // n_dp, D), (D // n_dp, HIDDEN_HALF), (HIDDEN_HALF // n_dp, D)]
    return pl.pallas_call(
        functools.partial(weights_kernel, n_dp),
        out_shape=[jax.ShapeDtypeStruct(s, F32) for s in shapes]
        + [jax.ShapeDtypeStruct(sums.shape, F32), jax.ShapeDtypeStruct(y2.shape, BF)],
        in_specs=[vmem] * 9 + [hbm] * 2,
        out_specs=[vmem] * 5 + [hbm],
        scratch_shapes=[pltpu.VMEM((2, 2, n_z) + s, BF) for s in shapes]
        + [pltpu.VMEM((2, n_z) + s, BF) for s in shapes]
        + [pltpu.VMEM((n_z,) + s, BF) for s in shapes]
        + [pltpu.VMEM((n_z - 1,) + s, BF) for s in shapes]
        + [
            pltpu.VMEM(sums.shape, F32),
            pltpu.VMEM(sums.shape, F32),
            pltpu.VMEM((n_z - 1,) + sums.shape, F32),
            pltpu.VMEM(sums.shape, F32),
            pltpu.VMEM(sums.shape, F32),
            pltpu.SemaphoreType.DMA((5,)),
            pltpu.SemaphoreType.DMA((5,)),
            pltpu.SemaphoreType.DMA((5,)),
            pltpu.SemaphoreType.DMA((5,)),
            pltpu.SemaphoreType.DMA((5, n_z - 1)),
            pltpu.SemaphoreType.DMA((5, n_z - 1)),
            pltpu.SemaphoreType.DMA((3,)),
            pltpu.SemaphoreType.DMA((3,)),
            pltpu.SemaphoreType.DMA((1,)),
        ],
        compiler_params=pltpu.CompilerParams(collective_id=3, has_side_effects=True, vmem_limit_bytes=VMEM_LIMIT),
        name="weight_gradients",
    )(a0, dqkv, context, dr1, a1, du, hidden, dr2, sums, y2, da)


def weight_gradients_by_scatter(n_dp, a0, dqkv, context, dr1, a1, du, hidden, dr2, sums, y2, da):
    half = lax.axis_index("pipe") % 2
    layer = lax.axis_index("pipe") // 2
    halves = (
        dot_tn(a0, dqkv).reshape(D, 3, 2, HALF).transpose(2, 0, 1, 3).reshape(2, D, 3 * HALF),
        dot_tn(context, dr1).reshape(2, HALF, D),
        dot_tn(a1, du).reshape(D, 2, HIDDEN_HALF).transpose(1, 0, 2),
        dot_tn(hidden, dr2).reshape(2, HIDDEN_HALF, D),
    )
    swap = [(i, i ^ 1) for i in range(PIPE)]
    found = []
    for member in halves:
        part = lax.psum_scatter(member, "dp", scatter_dimension=1, tiled=True)
        keep = lax.dynamic_index_in_dim(part, half, 0, keepdims=False)
        send = lax.dynamic_index_in_dim(part, 1 - half, 0, keepdims=False)
        found.append(keep + lax.ppermute(send.astype(BF), "pipe", swap).astype(F32))
    small = lax.psum(sums, "dp")
    small = small + lax.ppermute(small, "pipe", swap)
    mine = jnp.where(layer == 1, y2, da)
    pieces = lax.all_to_all(mine, "pipe", 0, 0, tiled=False)
    return found + [small, pieces]


def shards(
    n_dp,
    tokens, cotangent, captions, projection, biases, combiner, offsets, scaling, centring,
    expansion, lifting, reduction, settling, stretch, translate,
):
    pipe = lax.axis_index("pipe")
    dp = lax.axis_index("dp")
    half = pipe % 2
    local_rows = tokens.shape[0]
    local_pairs = local_rows // PAIR_ROWS
    pairs = 2 * ((local_pairs + 3) // 4)
    rows = pairs * PAIR_ROWS
    spare = 2 * rows - local_rows
    block = 2 * PAIR_ROWS
    micros = rows // block

    both = jnp.pad(jnp.stack([tokens, cotangent]), ((0, 0), (0, spare), (0, 0)))
    wide = [jnp.pad(v[0], (0, HIDDEN_HALF - v.shape[1])) for v in (
        biases, offsets, scaling, centring, lifting, settling, stretch, translate
    )]
    packed = jnp.pad(jnp.stack(wide), ((0, 8), (0, 0)))
    pieces, joint, mixing, expand, reduce, halves = gather(
        rows, both, projection[0], combiner[0], expansion[0], reduction[0], packed
    )
    halves = halves.astype(F32)

    def joined(index, width):
        return jnp.pad(halves[:, index, :width].reshape(2 * width), (0, FF - 2 * width))

    joint_bias = jnp.pad(
        jnp.concatenate([
            halves[:, 0, :HALF].reshape(D), jnp.zeros((D,), F32), halves[:, 0, HALF:D].reshape(D)
        ]),
        (0, FF - 3 * D),
    )
    vectors = jnp.stack([
        joint_bias, joined(1, HALF), joined(2, HALF), joined(3, HALF),
        joined(4, HIDDEN_HALF), joined(5, HALF), joined(6, HALF), joined(7, HALF),
    ])
    lengths = lax.dynamic_slice_in_dim(jnp.pad(captions, (0, 2 * pairs - local_pairs)), half * pairs, pairs)
    key = jnp.arange(KEYS)[None, :]
    visible = (key < PAIR_ROWS) & ((key >= WORDS) | (key < lengths[:, None]))
    masks = jnp.where(visible, 0.0, NEGATIVE).astype(F32)

    a0, qkv, prob, context, n1, r1, a1, hidden, slope, n2, r2, y2 = forward(
        micros, block, pieces, masks, joint, mixing, expand, reduce, vectors
    )
    dr2, du, dr1, dqkv, da, sums = backward(
        micros, block, pieces, joint, mixing, expand, reduce, vectors, n2, r2, slope, n1, r1, qkv, prob
    )
    whole_tiles = HALF % (16 * n_dp) == 0
    collect = weight_gradients if whole_tiles else weight_gradients_by_scatter
    g_proj, g_comb, g_exp, g_red, small, outs = collect(
        n_dp, a0, dqkv, context, dr1, a1, du, hidden, dr2, sums, y2, da
    )
    tokens_grad = jnp.concatenate([outs[0], outs[1]])[:local_rows].astype(F32)
    encoded = jnp.concatenate([outs[2], outs[3]])[:local_rows]

    def own(row, start, width):
        count = width // n_dp
        return lax.dynamic_slice(small, (row, start + half * width + dp * count), (1, count))

    per_bias = jnp.concatenate([
        lax.dynamic_slice(small, (0, half * HALF), (1, HALF)),
        lax.dynamic_slice(small, (0, 2 * D + half * HALF), (1, HALF)),
    ], 1)
    g_bias = lax.dynamic_slice(per_bias, (0, dp * (D // n_dp)), (1, D // n_dp))
    return (
        encoded,
        tokens_grad,
        g_proj[None],
        g_bias,
        g_comb[None],
        own(1, 0, HALF),
        own(2, 0, HALF),
        own(3, 0, HALF),
        g_exp[None],
        own(4, 0, HIDDEN_HALF),
        g_red[None],
        own(5, 0, HALF),
        own(6, 0, HALF),
        own(7, 0, HALF),
    )


def solution(mesh):
    rows = P("dp", "pipe")
    matrix = P("pipe", None, None)
    vector = P("pipe", None)
    matrix_out = P("pipe", "dp", None)
    vector_out = P("pipe", "dp")
    in_specs = (
        rows, rows, P("dp"), matrix, vector, matrix, vector, vector, vector,
        matrix, vector, matrix, vector, vector, vector,
    )
    out_specs = (
        rows, rows, matrix_out, vector_out, matrix_out, vector_out, vector_out, vector_out,
        matrix_out, vector_out, matrix_out, vector_out, vector_out, vector_out,
    )
    return jax.shard_map(
        functools.partial(shards, mesh.shape["dp"]),
        mesh=mesh, in_specs=in_specs, out_specs=out_specs, check_vma=False,
    )
```

time: 2110 us -> 501 us (0.24)
  waiting for transfers between devices: 1250 us -> 0 us
  Pallas kernels: 0 us -> 479 us
  local copies, waits for them, and re-layouts: 474 us -> 15.9 us
  matrix products: 122 us -> 0 us
  other arithmetic: 95 us -> 4.12 us
  starting transfers between devices: 86.3 us -> 0 us
  loops' own time: 54.1 us -> 0 us
    ppermute x36 -> x0, waiting for transfers between devices: 573 us -> none  [the longest x12 386 us: passed_along(): return lax.ppermute(value, axis, pairs)]
    unnamed x26 -> x0, waiting for transfers between devices: 558 us -> none
    pallas_call x0 -> x4, Pallas kernels: none -> 479 us  [the longest x1 234 us: gather(): pl.pallas_call(functools.partial(gather_kernel, rows), out_shape=(jax.Sha...]
    reduce_scatter x2 -> x0, waiting for transfers between devices: 124 us -> none  [the longest x1 91.1 us: shards(): lax.psum_scatter(grad_halves[8], 'dp', scatter_dimension=1, tiled=True)]
    dot_general x39 -> x0, matrix products: 122 us -> none  [the longest x6 34.9 us: inner_rows(): lax.dot_general(left_side, right_side, (((0,), (0,)), ((), ())), preferre...]
    another operation x26 -> x17, local copies, waits for them, and re-layouts: 96.9 us -> 0.99 us  [the longest x1 0.78 us: shards(): jnp.stack([joint_bias, joined(1, HALF), joined(2, HALF), joined(3, HALF),...]
    ppermute x36 -> x0, starting transfers between devices: 85.7 us -> none  [the longest x12 56.1 us: passed_along(): return lax.ppermute(value, axis, pairs)]
    convert_element_type x25 -> x0, local copies, waits for them, and re-layouts: 67.3 us -> none  [the longest x6 33.2 us: attend_backward(): grad_joint = jnp.stack([grad_query, grad_keys, grad_values], axis=2).resh...]
  transfers between devices with their start and end apart: 51 -> 0, of which waited for: 32 -> 0; matrix products, arithmetic and copies ran while one was open for 8% -> 0% of each run, Pallas kernels for 0% -> 0%
where the time goes in v1:
time: 501 us; the launch traced here: 500 us
  Pallas kernels  479 us (96%)
  local copies, waits for them, and re-layouts  15.9 us (3%)
    pallas_call x1, Pallas kernels, gather(): pl.pallas_call(functools.partial(gather_kernel, rows), out_shape=(jax.Sha...  234 us
    pallas_call x1, Pallas kernels, weight_gradients(): pl.pallas_call(functools.partial(weights_kernel, n_dp), out_shape=[jax.Sh...  135 us
    pallas_call x1, Pallas kernels, backward(): pl.pallas_call(functools.partial(backward_kernel, micros, block), grid=(m...  66.2 us
    pallas_call x1, Pallas kernels, forward(): pl.pallas_call(functools.partial(forward_kernel, micros, block), grid=(mi...  44 us

profile of v1, /device:TPU:0, one launch (start us, length us, event | category | flops | bytes accessed | tf_op | source)
XLA Modules:
  0.0 500.4 jit_solution(2555478888383130218)
XLA Ops:
  0.7 0.8 pad_dynamic-slice_fusion.2
  1.5 0.7 fusion.6.masks
  2.1 1.4 copy.29
  3.5 0.3 copy.30
  3.8 0.0 copy-start.6
  3.8 0.0 copy-start.7
  3.9 0.0 copy-start.10
  3.9 0.0 copy-start.11
  3.9 1.5 fusion.2.both
  5.8 0.1 stack.71
  5.9 0.6 pad.66.vectors
  6.6 234.4 %gather_weights.1 = (bf16[4,832,192]{2,1,0:T(8,128)(2,1)}, bf16[768,2304]{1,0:T(8,128)(2,1)}, bf16[768,768]{1,0:T(8,128)(2,1)}, bf16[768,3072]{1,0:T(8,128)(2,1)...) custom-call(bf16[2,1664,192]{2,1,0:T(8,128)(2,1)} %fusion.2.both, bf16[768,1152]{1,0:T(8,128)(2,1)} %bitcast.30, ...), custom_call_target="tpu_custom_call" | custom-call | tf_op jit(solution)/shard_map/gather_weights/pallas_call | solution.py:191
  240.9 0.9 convert_element_type.28
  241.8 0.1 slice_reduce_fusion
  242.1 0.8 slice.65
  242.9 0.8 stack.80.vectors
  243.7 44.0 %layer_forward.1 = (bf16[832,768]{1,0:T(8,128)(2,1)}, bf16[832,2304]{1,0:T(8,128)(2,1)}, bf16[832,1536]{1,0:T(8,128)(2,1)}, bf16[832,768]{1,0:T(8,128)(2,1)}, bf...) custom-call(bf16[4,832,192]{2,1,0:T(8,128)(2,1)} %get-tuple-element., ...), custom_call_target="tpu_custom_call" | custom-call | tf_op jit(solution)/shard_map/layer_forward/pallas_call | solution.py:344
  287.8 66.2 %layer_backward.1 = (bf16[832,768]{1,0:T(8,128)(2,1)}, bf16[832,3072]{1,0:T(8,128)(2,1)}, bf16[832,768]{1,0:T(8,128)(2,1)}, bf16[832,2304]{1,0:T(8,128)(2,1)}, b...) custom-call(bf16[4,832,192]{2,1,0:T(8,128)(2,1)} %get-tuple-element.44.pieces, bf16[768,2304]{1,0:T(8,128)(2,1)} %get-tuple-element.45.joint, ...), custom_call_target="tpu_custom_call" | custom-call | tf_op jit(solution)/shard_map/layer_backward/pallas_call | solution.py:493
  353.9 134.7 %weight_gradients.1 = (f32[96,1152]{1,0:T(8,128)}, f32[48,768]{1,0:T(8,128)}, f32[96,1536]{1,0:T(8,128)}, f32[192,768]{1,0:T(8,128)}, f32[8,3072]{1,0:T(8,128)}, /*index=5*/bf16[4,832,192]{2,1,0:T(8,128)(2,1)}) custom-call(bf16[832,768]{1,0:T(8,128)(2,1)} %get-tuple-element.50.a0, bf16[832,2304]{1,0:T(8,128)(2,1)} %get-tuple-element.58.dqkv, ...), custom_call_target="tpu_custom_call" | custom-call | tf_op jit(solution)/shard_map/weight_gradients/pallas_call | solution.py:709
  488.7 0.7 constant_dynamic-slice_fusion
  489.4 0.6 fusion.7
  490.0 1.5 slice_bitcast_fusion.1
  491.5 0.1 fusion.3
  491.6 1.5 copy.32
  493.2 0.1 pad_maximum_fusion.1
  493.3 1.1 copy.31
  494.5 1.5 constant_dynamic-slice_fusion.2
  496.0 1.3 constant_dynamic-slice_fusion.5
  497.3 0.8 copy.37
  498.1 0.7 copy.38
  498.7 0.8 copy.39
  499.6 0.8 copy.40
  (60 shorter events, 0.4 us)
Async XLA Ops:
  0.6 2.9 copy-start
  3.8 1.6 copy-start.6
  3.8 1.7 copy-start.7
  3.8 1.7 copy-start.8
  3.8 1.8 copy-start.9
  3.9 1.8 copy-start.10
  3.9 1.8 copy-start.11
  3.9 1.9 copy-start.12
  3.9 1.9 copy-start.5
  493.2 4.2 copy-start.3
  493.2 4.9 copy-start.4
  493.3 5.4 %copy-start.2 = (f32[96,1536]{1,0:T(8,128)S(1)}, f32[96,1536]{1,0:T(8,128)}, u32[]{:S(2)}) copy-start(f32[96,1536]{1,0:T(8,128)} %get-tuple-element.72) | copy-start | bytes 1769476
  493.3 6.2 %copy-start.1 = (f32[192,768]{1,0:T(8,128)S(1)}, f32[192,768]{1,0:T(8,128)}, u32[]{:S(2)}) copy-start(f32[192,768]{1,0:T(8,128)} %get-tuple-element.73) | copy-start | bytes 1769476

commit v2 on v1

v2 whole, which is shorter than its diff:
```python
import functools

import jax
import jax.numpy as jnp
from jax import lax
from jax.experimental import pallas as pl
from jax.experimental.pallas import tpu as pltpu
from jax.sharding import PartitionSpec as P

D = 768
HEADS = 12
HEAD_DIM = 64
FF = 3072
WORDS = 64
PAIR_ROWS = 104
HALF = D // 2
HIDDEN_HALF = FF // 2
QUARTER = D // 4
PIPE = 4
KEYS = 128
GROUP = 4
GROUP_WIDTH = GROUP * HEAD_DIM
GROUPS = HEADS // GROUP

EPSILON = 1e-05
NEGATIVE = -1e30
SCALE = HEAD_DIM ** (-0.5)

MESH = pl.DeviceIdType.MESH
BF = jnp.bfloat16
F32 = jnp.float32
VMEM_LIMIT = 60 << 20


def dot_nn(left, right):
    return lax.dot_general(left, right, (((1,), (0,)), ((), ())), preferred_element_type=F32)


def dot_nt(left, right):
    return lax.dot_general(left, right, (((1,), (1,)), ((), ())), preferred_element_type=F32)


def dot_tn(left, right):
    return lax.dot_general(left, right, (((0,), (0,)), ((), ())), preferred_element_type=F32)


def place():
    pipe = lax.axis_index("pipe")
    dp = lax.axis_index("dp")
    layer = pipe // 2
    half = pipe % 2
    across_x = pipe + 1 - 2 * half
    across_y = (pipe + 2) % 4
    core = dp % 2
    other_core = dp + 1 - 2 * core
    return pipe, dp, layer, half, across_x, across_y, core, other_core


def greet(devices):
    barrier = pltpu.get_barrier_semaphore()
    for device in devices:
        pl.semaphore_signal(barrier, inc=1, device_id=device, device_id_type=MESH)
    pl.semaphore_wait(barrier, len(devices))


def remote(source, target, send, recv, device):
    return pltpu.make_async_remote_copy(
        src_ref=source,
        dst_ref=target,
        send_sem=send,
        recv_sem=recv,
        device_id=device,
        device_id_type=MESH,
    )


WEIGHT_SHAPES = [(D, 3 * HALF), (HALF, D), (D, HIDDEN_HALF), (HIDDEN_HALF, D)]
WEIGHT_SCRATCH = [pltpu.VMEM((2,) + shape, BF) for shape in WEIGHT_SHAPES]
CHUNKS = [(0, 0, 96), (0, 96, 96), (1, 0, 96), (2, 0, 96), (2, 96, 96), (3, 0, 192), (3, 192, 192)]
ATTENTION_CHUNKS = 3
DEPTH = 3


def head_of_lane():
    return lax.broadcasted_iota(jnp.int32, (KEYS, GROUP_WIDTH), 1) // HEAD_DIM


def stacked_keys(values, scale=None):
    padded = jnp.concatenate([values, jnp.zeros((KEYS - PAIR_ROWS, GROUP_WIDTH), F32)], 0)
    if scale is not None:
        padded = padded * scale
    owner = head_of_lane()
    return jnp.concatenate([jnp.where(owner == i, padded, 0.0) for i in range(GROUP)], 0).astype(BF)


def own_lanes(stacked):
    left = lax.broadcasted_iota(jnp.int32, (KEYS, KEYS), 1) < HEAD_DIM
    low = jnp.where(left, stacked[0:KEYS, :KEYS], stacked[KEYS : 2 * KEYS, :KEYS])
    high = jnp.where(left, stacked[2 * KEYS : 3 * KEYS, KEYS:], stacked[3 * KEYS :, KEYS:])
    return jnp.concatenate([low, high], 1)[:PAIR_ROWS]


def normalized(residual):
    average = jnp.mean(residual, axis=-1, keepdims=True)
    centred = residual - average
    variance = jnp.mean(centred * centred, axis=-1, keepdims=True)
    inverse = lax.rsqrt(variance + EPSILON)
    return centred * inverse, inverse


def forward_kernel(
    micros, block,
    own_vectors, masks, both, own_proj, own_comb, own_exp, own_red,
    a0_out, qkv_out, prob_out, context_out, n1_out, r1_out, a1_out, hidden_out, slope_out, n2_out, r2_out, y2_out,
    vectors, pieces_out, other_proj, other_comb, other_exp, other_red,
    slots, outgoing, a_s, qkv_s, prob_s, context_s, send, recv,
    joint, mixing, expand, reduce, pieces, other_vectors,
    x_send, x_recv, z_send, z_recv, near_send, near_recv, far_send, far_recv,
    own_sem, piece_send, piece_recv, vec_sem, out_sem,
):
    pipe, dp, layer, half, across_x, across_y, core, other_core = place()
    micro = pl.program_id(0)
    pairs = block // PAIR_ROWS
    rows = micros * block
    diagonal = (across_x + 2) % 4
    parity = (dp // 2) % 2
    across_z = dp + 2 - 4 * parity
    mine = 2 * parity + core
    paired = 2 * (1 - parity) + core
    owned = [own_proj, own_comb, own_exp, own_red]
    held = [joint, mixing, expand, reduce]
    others = [other_proj, other_comb, other_exp, other_red]

    def span(chunk, quarter):
        which, start, count = chunk
        return pl.ds(quarter * (WEIGHT_SHAPES[which][0] // 4) + start, count)

    def x_copy(k):
        at = span(CHUNKS[k], mine)
        which = CHUNKS[k][0]
        return remote(owned[which].at[at], held[which].at[half, at], x_send.at[k], x_recv.at[k], (across_x, dp))

    def z_copy(k):
        region = held[CHUNKS[k][0]].at[1 - half, span(CHUNKS[k], mine)]
        return remote(region, region, z_send.at[k], z_recv.at[k], (pipe, across_z))

    def near_copy(k):
        region = held[CHUNKS[k][0]].at[1 - half, span(CHUNKS[k], mine)]
        return remote(region, region, near_send.at[k], near_recv.at[k], (pipe, other_core))

    def far_copy(k):
        region = held[CHUNKS[k][0]].at[1 - half, span(CHUNKS[k], paired)]
        return remote(region, region, far_send.at[k], far_recv.at[k], (pipe, other_core))

    own_copies = [pltpu.make_async_copy(owned[i], held[i].at[half], own_sem.at[i]) for i in range(4)]
    own_piece = pltpu.make_async_copy(both.at[layer, pl.ds(half * rows, rows)], pieces.at[pipe], own_sem.at[4])
    vec_copy = remote(own_vectors, other_vectors, vec_sem.at[0], vec_sem.at[1], (across_x, dp))
    piece_copies = [
        remote(
            both.at[target // 2, pl.ds((target % 2) * rows, rows)],
            pieces.at[pipe],
            piece_send.at[j], piece_recv.at[j],
            (target, dp),
        )
        for j, target in enumerate((across_x, across_y, diagonal))
    ]
    out_copies = [pltpu.make_async_copy(held[i].at[1 - half], others[i], out_sem.at[i]) for i in range(4)] + [
        pltpu.make_async_copy(pieces, pieces_out, out_sem.at[4])
    ]
    n = len(CHUNKS)

    def gathered(first, last):
        for k in range(first, last):
            x_copy(k).wait_recv()
            z_copy(k).start()
            near_copy(k).start()
            if k + DEPTH < n:
                x_copy(k).wait_send()
                x_copy(k + DEPTH).start()
            if k + DEPTH == n - 1:
                send_pieces(1)
        for k in range(first, last):
            z_copy(k).wait_recv()
            far_copy(k).start()
        for k in range(first, last):
            near_copy(k).wait_recv()
            far_copy(k).wait_recv()

    def send_pieces(to_layer):
        for j, target in enumerate((across_x, across_y, diagonal)):
            @pl.when(target // 2 == to_layer)
            def _():
                piece_copies[j].start()

    def rest_gathered():
        gathered(ATTENTION_CHUNKS, n)
        own_copies[2].wait()
        own_copies[3].wait()
        for copy in out_copies[:4]:
            copy.start()

    @pl.when(micro == 0)
    def _():
        own_piece.start()
        for copy in own_copies:
            copy.start()
        greet([(across_x, dp), (across_y, dp), (diagonal, dp), (pipe, across_z), (pipe, other_core)])
        vec_copy.start()
        send_pieces(0)
        for k in range(DEPTH):
            x_copy(k).start()
        vec_copy.wait_recv()
        for which in range(2):
            value = jnp.where(half == which, own_vectors[...], other_vectors[...]).astype(F32)
            vectors[0:1, which * 3 * HALF : which * 3 * HALF + HALF] = value[0:1, :HALF]
            vectors[0:1, which * 3 * HALF + HALF : which * 3 * HALF + D] = jnp.zeros((1, HALF), F32)
            vectors[0:1, which * 3 * HALF + D : (which + 1) * 3 * HALF] = value[0:1, HALF:D]
            for i in (1, 2, 3, 5, 6, 7):
                vectors[i : i + 1, which * HALF : (which + 1) * HALF] = value[i : i + 1, :HALF]
            vectors[4:5, which * HIDDEN_HALF : (which + 1) * HIDDEN_HALF] = value[4:5, :]
        own_piece.wait()

        @pl.when(layer == 0)
        def _():
            for copy in piece_copies:
                copy.wait_recv()

        gathered(0, ATTENTION_CHUNKS)
        own_copies[0].wait()
        own_copies[1].wait()

        @pl.when(layer == 1)
        def _():
            rest_gathered()

    def copy_of(index):
        return remote(outgoing.at[index], slots.at[index], send.at[index], recv.at[index], (across_y, dp))

    @pl.when(layer == 0)
    def _():
        at = pl.ds(pl.multiple_of(micro * block, 16), block)
        a_s[...] = jnp.concatenate([pieces[i, at, :] for i in range(PIPE)], 1)

    @pl.when(layer == 1)
    def _():
        copy_of(micro).wait_recv()
        a_s[...] = slots[micro]

    inputs = a_s[...]
    a0_out[...] = inputs
    for which in range(2):
        value = dot_nn(inputs, joint[which]) + vectors[0:1, which * 3 * HALF : (which + 1) * 3 * HALF]
        for part in range(3):
            cols = slice(part * D + which * HALF, part * D + (which + 1) * HALF)
            found = value[:, part * HALF : (part + 1) * HALF]
            qkv_s[:, cols] = found
            qkv_out[:, cols] = found.astype(BF)
    for pair in range(pairs):
        rows_at = slice(pair * PAIR_ROWS, (pair + 1) * PAIR_ROWS)
        mask = masks[pl.ds(micro * pairs + pair, 1), :]
        for group in range(GROUPS):
            lanes = slice(group * GROUP_WIDTH, (group + 1) * GROUP_WIDTH)
            query = qkv_s[rows_at, group * GROUP_WIDTH : (group + 1) * GROUP_WIDTH].astype(BF)
            keys = stacked_keys(qkv_s[rows_at, D + group * GROUP_WIDTH : D + (group + 1) * GROUP_WIDTH], SCALE)
            values = stacked_keys(qkv_s[rows_at, 2 * D + group * GROUP_WIDTH : 2 * D + (group + 1) * GROUP_WIDTH])
            scores = dot_nt(query, keys)
            found = []
            for i in range(GROUP):
                score = scores[:, i * KEYS : (i + 1) * KEYS] + mask
                exponent = jnp.exp(score - jnp.max(score, axis=-1, keepdims=True))
                found.append(exponent * (1.0 / jnp.sum(exponent, axis=-1, keepdims=True)))
            probs = jnp.concatenate(found, 1)
            prob_s[rows_at, group * GROUP * KEYS : (group + 1) * GROUP * KEYS] = probs
            context_s[rows_at, lanes] = dot_nn(probs.astype(BF), values)
    prob_out[...] = prob_s[...].astype(BF)
    context = context_s[...].astype(BF)
    context_out[...] = context
    residual = inputs.astype(F32) + dot_nn(context, mixing[...].reshape(D, D)) + vectors[1:2, :D]
    norm, inverse = normalized(residual)
    n1_out[...] = norm.astype(BF)
    r1_out[...] = inverse
    attended = (norm * vectors[2:3, :D] + vectors[3:4, :D]).astype(BF)
    a1_out[...] = attended

    @pl.when((micro == 0) & (layer == 0))
    def _():
        rest_gathered()

    chunk = 512
    residual = attended.astype(F32) + vectors[5:6, :D]
    for which in range(2):
        for start in range(0, HIDDEN_HALF, chunk):
            at = slice(start, start + chunk)
            cols = slice(which * HIDDEN_HALF + start, which * HIDDEN_HALF + start + chunk)
            raised = dot_nn(attended, expand[which, :, at]) + vectors[4:5, cols]
            below = 0.5 * (1.0 + lax.erf(raised * (0.5**0.5)))
            hidden = (raised * below).astype(BF)
            hidden_out[:, cols] = hidden
            density = jnp.exp(raised * raised * (-0.5)) * 0.3989422804014327
            slope_out[:, cols] = (below + raised * density).astype(BF)
            residual = residual + dot_nn(hidden, reduce[which, at, :])
    norm, inverse = normalized(residual)
    n2_out[...] = norm.astype(BF)
    r2_out[...] = inverse
    result = (norm * vectors[6:7, :D] + vectors[7:8, :D]).astype(BF)
    for i in range(PIPE):
        y2_out[i] = result[:, i * QUARTER : (i + 1) * QUARTER]

    @pl.when(layer == 0)
    def _():
        outgoing[micro] = result
        copy_of(micro).start()

    @pl.when(micro == micros - 1)
    def _():
        @pl.when(layer == 0)
        def _():
            for index in range(micros):
                copy_of(index).wait_send()

        for k in range(n):
            if k + DEPTH >= n:
                x_copy(k).wait_send()
            z_copy(k).wait_send()
            near_copy(k).wait_send()
            far_copy(k).wait_send()
        for copy in piece_copies + [vec_copy]:
            copy.wait_send()

        @pl.when(layer == 1)
        def _():
            for copy in piece_copies:
                copy.wait_recv()

        out_copies[4].start()
        for copy in out_copies:
            copy.wait()


def forward(micros, block, own_vectors, masks, both, owned):
    rows = micros * block
    n = len(CHUNKS)

    def by_rows(width):
        return pl.BlockSpec((block, width), lambda m: (m, 0))

    vmem = pl.BlockSpec(memory_space=pltpu.VMEM)
    hbm = pl.BlockSpec(memory_space=pl.ANY)
    by_pieces = pl.BlockSpec((PIPE, block, QUARTER), lambda m: (0, m, 0))
    widths = [D, 3 * D, HEADS * KEYS, D, D, 1, D, FF, FF, D, 1]
    types = [BF, BF, BF, BF, BF, F32, BF, BF, BF, BF, F32]
    pieces = jax.ShapeDtypeStruct((PIPE, rows, QUARTER), BF)
    return pl.pallas_call(
        functools.partial(forward_kernel, micros, block),
        grid=(micros,),
        out_shape=[jax.ShapeDtypeStruct((rows, w), t) for w, t in zip(widths, types)]
        + [pieces, jax.ShapeDtypeStruct((8, FF), F32), pieces]
        + [jax.ShapeDtypeStruct(shape, BF) for shape in WEIGHT_SHAPES],
        in_specs=[vmem, vmem] + [hbm] * 5,
        out_specs=[by_rows(w) for w in widths] + [by_pieces, vmem] + [hbm] * 5,
        scratch_shapes=[
            pltpu.VMEM((micros, block, D), BF),
            pltpu.VMEM((micros, block, D), BF),
            pltpu.VMEM((block, D), BF),
            pltpu.VMEM((block, 3 * D), F32),
            pltpu.VMEM((block, HEADS * KEYS), F32),
            pltpu.VMEM((block, D), F32),
            pltpu.SemaphoreType.DMA((micros,)),
            pltpu.SemaphoreType.DMA((micros,)),
        ]
        + WEIGHT_SCRATCH
        + [pltpu.VMEM((PIPE, rows, QUARTER), BF), pltpu.VMEM(own_vectors.shape, BF)]
        + [pltpu.SemaphoreType.DMA((n,))] * 8
        + [
            pltpu.SemaphoreType.DMA((5,)),
            pltpu.SemaphoreType.DMA((3,)),
            pltpu.SemaphoreType.DMA((3,)),
            pltpu.SemaphoreType.DMA((2,)),
            pltpu.SemaphoreType.DMA((5,)),
        ],
        compiler_params=pltpu.CompilerParams(collective_id=1, has_side_effects=True, vmem_limit_bytes=VMEM_LIMIT),
        name="layer_forward",
    )(own_vectors, masks, both, *owned)


def norm_backward(gradient, norm, inverse, gain):
    scaled = gradient * gain
    first = jnp.mean(scaled, axis=-1, keepdims=True)
    second = jnp.mean(scaled * norm, axis=-1, keepdims=True)
    return (scaled - first - norm * second) * inverse


def column_sums(value):
    return jnp.sum(value, axis=0, keepdims=True)


def backward_kernel(
    micros, block,
    pieces, vectors,
    own_proj, own_comb, own_exp, own_red, other_proj, other_comb, other_exp, other_red,
    n2, r2, slope, n1, r1, qkv, prob,
    dr2_out, du_out, dr1_out, dqkv_out, da_out, sums_out,
    slots, outgoing, g_s, qkv_s, prob_s, dc_s, dqkv_s, send, recv,
    joint, mixing, expand, reduce, weight_sem,
):
    pipe, dp, layer, half, across_x, across_y, core, other_core = place()
    micro = pl.program_id(0)
    pairs = block // PAIR_ROWS

    owned = [own_proj, own_comb, own_exp, own_red]
    others = [other_proj, other_comb, other_exp, other_red]
    held = [joint, mixing, expand, reduce]
    loads = [
        [
            pltpu.make_async_copy(owned[i], held[i].at[half], weight_sem.at[0, i]),
            pltpu.make_async_copy(others[i], held[i].at[1 - half], weight_sem.at[1, i]),
        ]
        for i in range(4)
    ]

    def loaded(*which):
        @pl.when(micro == 0)
        def _():
            for index in which:
                for copy in loads[index]:
                    copy.wait()

    @pl.when(micro == 0)
    def _():
        for index in (3, 2, 1, 0):
            for copy in loads[index]:
                copy.start()
        greet([(across_y, dp)])
        sums_out[...] = jnp.zeros_like(sums_out)

    def copy_of(index):
        return remote(outgoing.at[index], slots.at[index], send.at[index], recv.at[index], (across_y, dp))

    @pl.when(layer == 1)
    def _():
        g_s[...] = jnp.concatenate([pieces[i] for i in range(PIPE)], 1)

    @pl.when(layer == 0)
    def _():
        copy_of(micro).wait_recv()
        g_s[...] = slots[micro]

    def add_sum(row, value):
        width = value.shape[1]
        sums_out[row : row + 1, :width] += column_sums(value)

    gradient = g_s[...].astype(F32)
    norm = n2[...].astype(F32)
    add_sum(6, gradient * norm)
    add_sum(7, gradient)
    grad_residual = norm_backward(gradient, norm, r2[...], vectors[6:7, :D])
    add_sum(5, grad_residual)
    branch = grad_residual.astype(BF)
    dr2_out[...] = branch
    loaded(3, 2)
    chunk = 512
    total = grad_residual
    for which in range(2):
        for start in range(0, HIDDEN_HALF, chunk):
            at = slice(start, start + chunk)
            cols = slice(which * HIDDEN_HALF + start, which * HIDDEN_HALF + start + chunk)
            raised = dot_nt(branch, reduce[which, at, :]) * slope[:, cols].astype(F32)
            sums_out[4:5, cols] += column_sums(raised)
            raised = raised.astype(BF)
            du_out[:, cols] = raised
            total = total + dot_nt(raised, expand[which, :, at])

    gradient = total.astype(BF).astype(F32)
    norm = n1[...].astype(F32)
    add_sum(2, gradient * norm)
    add_sum(3, gradient)
    grad_residual = norm_backward(gradient, norm, r1[...], vectors[2:3, :D])
    add_sum(1, grad_residual)
    branch = grad_residual.astype(BF)
    dr1_out[...] = branch
    loaded(1, 0)
    dc_s[...] = dot_nt(branch, mixing[...].reshape(D, D))
    qkv_s[...] = qkv[...].astype(F32)
    prob_s[...] = prob[...].astype(F32)
    for pair in range(pairs):
        rows = slice(pair * PAIR_ROWS, (pair + 1) * PAIR_ROWS)
        for group in range(GROUPS):
            lanes = [
                slice(part * D + group * GROUP_WIDTH, part * D + (group + 1) * GROUP_WIDTH) for part in range(3)
            ]
            query = qkv_s[rows, lanes[0]].astype(BF)
            keys = stacked_keys(qkv_s[rows, lanes[1]], SCALE)
            values = stacked_keys(qkv_s[rows, lanes[2]])
            grad_context = dc_s[rows, lanes[0]].astype(BF)
            probs = prob_s[rows, group * GROUP * KEYS : (group + 1) * GROUP * KEYS]
            grad_probs = dot_nt(grad_context, values)
            found = []
            for i in range(GROUP):
                at = slice(i * KEYS, (i + 1) * KEYS)
                weighted = probs[:, at] * grad_probs[:, at]
                found.append(weighted - probs[:, at] * jnp.sum(weighted, axis=-1, keepdims=True))
            grad_scores = jnp.concatenate(found, 1).astype(BF)
            dqkv_s[rows, lanes[0]] = dot_nn(grad_scores, keys)
            dqkv_s[rows, lanes[1]] = own_lanes(dot_tn(grad_scores, query)) * SCALE
            dqkv_s[rows, lanes[2]] = own_lanes(dot_tn(probs.astype(BF), grad_context))
    total = grad_residual
    for which in range(2):
        value = jnp.concatenate(
            [dqkv_s[:, part * D + which * HALF : part * D + (which + 1) * HALF] for part in range(3)], 1
        ).astype(BF)
        cols = slice(which * 3 * HALF, (which + 1) * 3 * HALF)
        dqkv_out[:, cols] = value
        sums_out[0:1, cols] += column_sums(value.astype(F32))
        total = total + dot_nt(value, joint[which])
    result = total.astype(BF)
    for i in range(PIPE):
        da_out[i] = result[:, i * QUARTER : (i + 1) * QUARTER]

    @pl.when(layer == 1)
    def _():
        outgoing[micro] = result
        copy_of(micro).start()

    @pl.when((layer == 1) & (micro == micros - 1))
    def _():
        for index in range(micros):
            copy_of(index).wait_send()


def backward(micros, block, pieces, vectors, owned, others, n2, r2, slope, n1, r1, qkv, prob):
    rows = micros * block

    def whole(array):
        return pl.BlockSpec(array.shape, lambda m: (0,) * array.ndim, pipeline_mode=pl.Buffered(1))

    def by_rows(width):
        return pl.BlockSpec((block, width), lambda m: (m, 0))

    by_pieces = pl.BlockSpec((PIPE, block, QUARTER), lambda m: (0, m, 0))
    kept = (n2, r2, slope, n1, r1, qkv, prob)
    widths = [D, FF, D, 3 * D]
    return pl.pallas_call(
        functools.partial(backward_kernel, micros, block),
        grid=(micros,),
        out_shape=[jax.ShapeDtypeStruct((rows, w), BF) for w in widths]
        + [jax.ShapeDtypeStruct((PIPE, rows, QUARTER), BF), jax.ShapeDtypeStruct((8, FF), F32)],
        in_specs=[by_pieces, whole(vectors)]
        + [pl.BlockSpec(memory_space=pl.ANY)] * 8
        + [by_rows(a.shape[1]) for a in kept],
        out_specs=[by_rows(w) for w in widths] + [by_pieces, pl.BlockSpec((8, FF), lambda m: (0, 0))],
        scratch_shapes=[
            pltpu.VMEM((micros, block, D), BF),
            pltpu.VMEM((micros, block, D), BF),
            pltpu.VMEM((block, D), BF),
            pltpu.VMEM((block, 3 * D), F32),
            pltpu.VMEM((block, HEADS * KEYS), F32),
            pltpu.VMEM((block, D), F32),
            pltpu.VMEM((block, 3 * D), F32),
            pltpu.SemaphoreType.DMA((micros,)),
            pltpu.SemaphoreType.DMA((micros,)),
        ]
        + WEIGHT_SCRATCH
        + [pltpu.SemaphoreType.DMA((2, 4))],
        compiler_params=pltpu.CompilerParams(collective_id=2, has_side_effects=True, vmem_limit_bytes=VMEM_LIMIT),
        name="layer_backward",
    )(pieces, vectors, *owned, *others, *kept)


TILE = 384


def weights_kernel(
    n_dp,
    a0_in, dqkv_in, context_in, dr1_in, a1_in, du_in, hidden_in, dr2_in, sums, y2, da,
    g_proj, g_comb, g_exp, g_red, sums_out, pieces_out,
    b_proj, b_comb, b_exp, b_red,
    c_proj, c_comb, c_exp, c_red,
    x_proj, x_comb, x_exp, x_red,
    z_proj, z_comb, z_exp, z_red,
    sums_core, sums_x, sums_z, sums_a, sums_b,
    a0, dqkv, context, dr1, a1, du, hidden, dr2,
    core_send, core_recv, x_send, x_recv, z_send, z_recv, piece_send, piece_recv, local_sem,
    small_send, small_recv, load_sem,
):
    pipe, dp, layer, half, across_x, across_y, core, other_core = place()
    diagonal = (across_x + 2) % 4
    n_z = n_dp // 2
    z = dp // 2
    offsets = sorted(range(1, n_z), key=lambda off: -min(off, n_z - off)) + [0]
    z_order = [(z + off) % n_z for off in offsets]
    z_others = z_order[:-1]
    loads = [
        pltpu.make_async_copy(source, target, load_sem.at[i])
        for i, (source, target) in enumerate((
            (hidden_in, hidden), (dr2_in, dr2), (a1_in, a1), (du_in, du),
            (a0_in, a0), (dqkv_in, dqkv), (context_in, context), (dr1_in, dr1),
        ))
    ]
    for copy in loads:
        copy.start()
    greet(
        [(across_x, dp), (across_y, dp), (diagonal, dp), (pipe, other_core)]
        + [(pipe, 2 * other + core) for other in z_others]
    )

    waits = []
    for j, target in enumerate((across_x, across_y, diagonal)):

        @pl.when(layer == 0)
        def _():
            remote(da.at[target], pieces_out.at[pipe], piece_send.at[j], piece_recv.at[j], (target, dp)).start()

        @pl.when(layer == 1)
        def _():
            remote(y2.at[target], pieces_out.at[pipe], piece_send.at[j], piece_recv.at[j], (target, dp)).start()

        waits.append(remote(da.at[target], pieces_out.at[pipe], piece_send.at[j], piece_recv.at[j], (target, dp)))

    @pl.when(layer == 0)
    def _():
        pltpu.make_async_copy(da.at[pipe], pieces_out.at[pipe], local_sem.at[0]).start()

    @pl.when(layer == 1)
    def _():
        pltpu.make_async_copy(y2.at[pipe], pieces_out.at[pipe], local_sem.at[0]).start()

    own_piece = pltpu.make_async_copy(da.at[pipe], pieces_out.at[pipe], local_sem.at[0])

    mine = [b_red, b_exp, b_proj, b_comb]
    from_core = [c_red, c_exp, c_proj, c_comb]
    from_x = [x_red, x_exp, x_proj, x_comb]
    from_z = [z_red, z_exp, z_proj, z_comb]
    outs = [g_red, g_exp, g_proj, g_comb]

    def fill_red(i, carry):
        lanes = pl.ds(pl.multiple_of(i * TILE, 128), TILE)
        tile = dot_tn(hidden[:, lanes], dr2[...])
        per_half = HIDDEN_HALF // TILE
        r = b_red.shape[3]
        per = TILE // r // 2
        for k in range(per):
            for c in range(2):
                b_red[c, i // per_half, (i % per_half) * per + k] = tile[(2 * k + c) * r : (2 * k + c + 1) * r].astype(BF)
        return carry

    def fill_exp(step, carry):
        i, j = step // 4, step % 4
        r = b_exp.shape[3]
        per = TILE // r // 2
        tile = dot_tn(
            a1[:, pl.ds(pl.multiple_of(i * TILE, 128), TILE)], du[:, pl.ds(pl.multiple_of(j * D, 128), D)]
        )
        lanes = pl.ds(pl.multiple_of((j % 2) * D, 128), D)
        for k in range(per):
            for c in range(2):
                b_exp[c, j // 2, i * per + k, :, lanes] = tile[(2 * k + c) * r : (2 * k + c + 1) * r].astype(BF)
        return carry

    def fill_proj(step, carry):
        i, h = step // 2, step % 2
        r = b_proj.shape[3]
        per = TILE // r // 2
        tile = dot_tn(
            a0[:, pl.ds(pl.multiple_of(i * TILE, 128), TILE)],
            dqkv[:, pl.ds(pl.multiple_of(h * 3 * HALF, 128), 3 * HALF)],
        )
        for k in range(per):
            for c in range(2):
                b_proj[c, h, i * per + k] = tile[(2 * k + c) * r : (2 * k + c + 1) * r].astype(BF)
        return carry

    def fill_comb(i, carry):
        r = b_comb.shape[3]
        per = TILE // r // 2
        tile = dot_tn(context[:, pl.ds(pl.multiple_of(i * TILE, 128), TILE)], dr1[...])
        for k in range(per):
            for c in range(2):
                b_comb[c, i, k] = tile[(2 * k + c) * r : (2 * k + c + 1) * r].astype(BF)
        return carry

    def core_copy(a, which):
        at = 1 - half if which == 0 else half
        return remote(
            mine[a].at[1 - core, at], from_core[a].at[at], core_send.at[a, which], core_recv.at[a, which],
            (pipe, other_core),
        )

    def x_copy(k):
        a, i = chunks[k]
        return remote(
            mine[a].at[core, 1 - half, z_order[i]], from_x[a].at[z_order[i]], x_send.at[a, i], x_recv.at[a, i],
            (across_x, dp),
        )

    def z_copy(a, i):
        other = z_order[i]
        return remote(
            mine[a].at[core, half, other], from_z[a].at[i], z_send.at[a, i], z_recv.at[a, i],
            (pipe, 2 * other + core),
        )

    chunks = [(a, i) for a in range(4) for i in range(n_z)]

    def start_x(k):
        if k >= len(chunks):
            return
        a, i = chunks[k]
        at = z_order[i]
        total = mine[a][core, 1 - half, at].astype(F32) + from_core[a][1 - half, at].astype(F32)
        mine[a][core, 1 - half, at] = total.astype(BF)
        x_copy(k).start()

    def after_x(k):
        a, i = chunks[k]
        at = z_order[i]
        x_copy(k).wait()
        start_x(k + DEPTH)
        if i == 0:
            core_copy(a, 1).wait_recv()
        total = mine[a][core, half, at].astype(F32) + from_core[a][half, at].astype(F32) + from_x[a][at].astype(F32)
        if i < n_z - 1:
            mine[a][core, half, at] = total.astype(BF)
            z_copy(a, i).start()
        else:
            outs[a][...] = total

    def after_z(a):
        total = outs[a][...]
        for i in range(n_z - 1):
            z_copy(a, i).wait()
            total = total + from_z[a][i].astype(F32)
        outs[a][...] = total

    sums_copy_core = remote(sums, sums_core, small_send.at[0], small_recv.at[0], (pipe, other_core))
    sums_copy_x = remote(sums_a, sums_x, small_send.at[1], small_recv.at[1], (across_x, dp))
    sums_copies_z = [
        remote(sums_b, sums_z.at[i], small_send.at[2 + i], small_recv.at[2 + i], (pipe, 2 * other + core))
        for i, other in enumerate(z_others)
    ]

    sums_copy_core.start()
    loads[0].wait()
    loads[1].wait()
    per_half = HIDDEN_HALF // TILE
    lax.fori_loop(0, per_half, lambda i, carry: fill_red((1 - half) * per_half + i, carry), 0)
    core_copy(0, 0).start()
    lax.fori_loop(0, per_half, lambda i, carry: fill_red(half * per_half + i, carry), 0)
    core_copy(0, 1).start()
    core_copy(0, 0).wait_recv()
    for k in range(DEPTH):
        start_x(k)
    loads[2].wait()
    loads[3].wait()
    lax.fori_loop(0, 4 * D // TILE, fill_exp, 0)
    core_copy(1, 0).start()
    core_copy(1, 1).start()
    sums_copy_core.wait()
    sums_a[...] = sums[...] + sums_core[...]
    sums_copy_x.start()
    core_copy(1, 0).wait_recv()
    after_x(0)
    loads[4].wait()
    loads[5].wait()
    lax.fori_loop(0, 2 * D // TILE, fill_proj, 0)
    core_copy(2, 0).start()
    core_copy(2, 1).start()
    after_x(1)
    loads[6].wait()
    loads[7].wait()
    lax.fori_loop(0, D // TILE, fill_comb, 0)
    core_copy(3, 0).start()
    core_copy(3, 1).start()
    sums_copy_x.wait()
    sums_b[...] = sums_a[...] + sums_x[...]
    for copy in sums_copies_z:
        copy.start()
    core_copy(2, 0).wait_recv()
    core_copy(3, 0).wait_recv()
    for k in range(2, len(chunks)):
        after_x(k)
        if k % n_z == n_z - 2 and k >= n_z:
            after_z(k // n_z - 1)
    after_z(3)
    for a in range(4):
        for which in range(2):
            core_copy(a, which).wait_send()
    total = sums_b[...]
    for i in range(n_z - 1):
        sums_copies_z[i].wait()
        total = total + sums_z[i]
    sums_out[...] = total
    own_piece.wait()
    for copy in waits:
        copy.wait()


def weight_gradients(n_dp, a0, dqkv, context, dr1, a1, du, hidden, dr2, sums, y2, da):
    vmem = pl.BlockSpec(memory_space=pltpu.VMEM)
    hbm = pl.BlockSpec(memory_space=pl.ANY)
    n_z = n_dp // 2
    shapes = [(D // n_dp, 3 * HALF), (HALF // n_dp, D), (D // n_dp, HIDDEN_HALF), (HIDDEN_HALF // n_dp, D)]
    return pl.pallas_call(
        functools.partial(weights_kernel, n_dp),
        out_shape=[jax.ShapeDtypeStruct(s, F32) for s in shapes]
        + [jax.ShapeDtypeStruct(sums.shape, F32), jax.ShapeDtypeStruct(y2.shape, BF)],
        in_specs=[hbm] * 8 + [vmem] + [hbm] * 2,
        out_specs=[vmem] * 5 + [hbm],
        scratch_shapes=[pltpu.VMEM((2, 2, n_z) + s, BF) for s in shapes]
        + [pltpu.VMEM((2, n_z) + s, BF) for s in shapes]
        + [pltpu.VMEM((n_z,) + s, BF) for s in shapes]
        + [pltpu.VMEM((n_z - 1,) + s, BF) for s in shapes]
        + [
            pltpu.VMEM(sums.shape, F32),
            pltpu.VMEM(sums.shape, F32),
            pltpu.VMEM((n_z - 1,) + sums.shape, F32),
            pltpu.VMEM(sums.shape, F32),
            pltpu.VMEM(sums.shape, F32),
        ]
        + [pltpu.VMEM(v.shape, BF) for v in (a0, dqkv, context, dr1, a1, du, hidden, dr2)]
        + [
            pltpu.SemaphoreType.DMA((4, 2)),
            pltpu.SemaphoreType.DMA((4, 2)),
            pltpu.SemaphoreType.DMA((4, n_z)),
            pltpu.SemaphoreType.DMA((4, n_z)),
            pltpu.SemaphoreType.DMA((4, n_z - 1)),
            pltpu.SemaphoreType.DMA((4, n_z - 1)),
            pltpu.SemaphoreType.DMA((3,)),
            pltpu.SemaphoreType.DMA((3,)),
            pltpu.SemaphoreType.DMA((1,)),
            pltpu.SemaphoreType.DMA((n_z + 1,)),
            pltpu.SemaphoreType.DMA((n_z + 1,)),
            pltpu.SemaphoreType.DMA((8,)),
        ],
        compiler_params=pltpu.CompilerParams(collective_id=3, has_side_effects=True, vmem_limit_bytes=VMEM_LIMIT),
        name="weight_gradients",
    )(a0, dqkv, context, dr1, a1, du, hidden, dr2, sums, y2, da)


def weight_gradients_by_scatter(n_dp, a0, dqkv, context, dr1, a1, du, hidden, dr2, sums, y2, da):
    half = lax.axis_index("pipe") % 2
    layer = lax.axis_index("pipe") // 2
    halves = (
        dot_tn(a0, dqkv).reshape(D, 2, 3 * HALF).transpose(1, 0, 2),
        dot_tn(context, dr1).reshape(2, HALF, D),
        dot_tn(a1, du).reshape(D, 2, HIDDEN_HALF).transpose(1, 0, 2),
        dot_tn(hidden, dr2).reshape(2, HIDDEN_HALF, D),
    )
    swap = [(i, i ^ 1) for i in range(PIPE)]
    found = []
    for member in halves:
        part = lax.psum_scatter(member, "dp", scatter_dimension=1, tiled=True)
        keep = lax.dynamic_index_in_dim(part, half, 0, keepdims=False)
        send = lax.dynamic_index_in_dim(part, 1 - half, 0, keepdims=False)
        found.append(keep + lax.ppermute(send.astype(BF), "pipe", swap).astype(F32))
    small = lax.psum(sums, "dp")
    small = small + lax.ppermute(small, "pipe", swap)
    mine = jnp.where(layer == 1, y2, da)
    pieces = lax.all_to_all(mine, "pipe", 0, 0, tiled=False)
    return found + [small, pieces]


def shards(
    n_dp,
    tokens, cotangent, captions, projection, biases, combiner, offsets, scaling, centring,
    expansion, lifting, reduction, settling, stretch, translate,
):
    pipe = lax.axis_index("pipe")
    dp = lax.axis_index("dp")
    half = pipe % 2
    local_rows = tokens.shape[0]
    local_pairs = local_rows // PAIR_ROWS
    pairs = 2 * ((local_pairs + 3) // 4)
    rows = pairs * PAIR_ROWS
    spare = 2 * rows - local_rows
    block = 2 * PAIR_ROWS
    micros = rows // block

    both = jnp.pad(jnp.stack([tokens, cotangent]), ((0, 0), (0, spare), (0, 0)))
    wide = [jnp.pad(v[0], (0, HIDDEN_HALF - v.shape[1])) for v in (
        biases, offsets, scaling, centring, lifting, settling, stretch, translate
    )]
    packed = jnp.pad(jnp.stack(wide), ((0, 8), (0, 0)))
    owned = (projection[0], combiner[0], expansion[0], reduction[0])
    lengths = lax.dynamic_slice_in_dim(jnp.pad(captions, (0, 2 * pairs - local_pairs)), half * pairs, pairs)
    key = jnp.arange(KEYS)[None, :]
    visible = (key < PAIR_ROWS) & ((key >= WORDS) | (key < lengths[:, None]))
    masks = jnp.where(visible, 0.0, NEGATIVE).astype(F32)

    a0, qkv, prob, context, n1, r1, a1, hidden, slope, n2, r2, y2, vectors, pieces, *others = forward(
        micros, block, packed, masks, both, owned
    )
    dr2, du, dr1, dqkv, da, sums = backward(
        micros, block, pieces, vectors, owned, others, n2, r2, slope, n1, r1, qkv, prob
    )
    whole_tiles = HALF % (16 * n_dp) == 0
    collect = weight_gradients if whole_tiles else weight_gradients_by_scatter
    g_proj, g_comb, g_exp, g_red, small, outs = collect(
        n_dp, a0, dqkv, context, dr1, a1, du, hidden, dr2, sums, y2, da
    )
    tokens_grad = jnp.concatenate([outs[0], outs[1]])[:local_rows].astype(F32)
    encoded = jnp.concatenate([outs[2], outs[3]])[:local_rows]

    def own(row, start, width):
        count = width // n_dp
        return lax.dynamic_slice(small, (row, start + half * width + dp * count), (1, count))

    own_bias = lax.dynamic_slice(small, (0, half * 3 * HALF), (1, 3 * HALF))
    per_bias = jnp.concatenate([own_bias[:, :HALF], own_bias[:, D:]], 1)
    g_bias = lax.dynamic_slice(per_bias, (0, dp * (D // n_dp)), (1, D // n_dp))
    return (
        encoded,
        tokens_grad,
        g_proj[None],
        g_bias,
        g_comb[None],
        own(1, 0, HALF),
        own(2, 0, HALF),
        own(3, 0, HALF),
        g_exp[None],
        own(4, 0, HIDDEN_HALF),
        g_red[None],
        own(5, 0, HALF),
        own(6, 0, HALF),
        own(7, 0, HALF),
    )


def solution(mesh):
    rows = P("dp", "pipe")
    matrix = P("pipe", None, None)
    vector = P("pipe", None)
    matrix_out = P("pipe", "dp", None)
    vector_out = P("pipe", "dp")
    in_specs = (
        rows, rows, P("dp"), matrix, vector, matrix, vector, vector, vector,
        matrix, vector, matrix, vector, vector, vector,
    )
    out_specs = (
        rows, rows, matrix_out, vector_out, matrix_out, vector_out, vector_out, vector_out,
        matrix_out, vector_out, matrix_out, vector_out, vector_out, vector_out,
    )
    return jax.shard_map(
        functools.partial(shards, mesh.shape["dp"]),
        mesh=mesh, in_specs=in_specs, out_specs=out_specs, check_vma=False,
    )
```

time: 501 us -> 314 us (0.63)
  Pallas kernels: 479 us -> 295 us
    pallas_call x1 -> x0, Pallas kernels: 234 us -> none  [gather(): pl.pallas_call(functools.partial(gather_kernel, rows), out_shape=(jax.Sha...]
    pallas_call x1, Pallas kernels: 44 us -> 109 us  [forward(): pl.pallas_call(functools.partial(forward_kernel, micros, block), grid=(mi...]
    pallas_call x1, Pallas kernels: 135 us -> 117 us  [weight_gradients(): pl.pallas_call(functools.partial(weights_kernel, n_dp), out_shape=[jax.Sh...]
where the time goes in v2:
time: 314 us
  Pallas kernels  295 us (94%)
  local copies, waits for them, and re-layouts  14.1 us (4%)
    pallas_call x1, Pallas kernels, weight_gradients(): pl.pallas_call(functools.partial(weights_kernel, n_dp), out_shape=[jax.Sh...  117 us
    pallas_call x1, Pallas kernels, forward(): pl.pallas_call(functools.partial(forward_kernel, micros, block), grid=(mi...  109 us
    pallas_call x1, Pallas kernels, backward(): pl.pallas_call(functools.partial(backward_kernel, micros, block), grid=(m...  69.4 us
    unnamed x34, local copies, waits for them, and re-layouts  7.43 us

profile of v2, /device:TPU:0, one launch (start us, length us, event | category | flops | bytes accessed | tf_op | source)
XLA Modules:
  0.0 313.7 jit_solution(12643814775074829843)
XLA Ops:
  0.7 0.8 pad_dynamic-slice_fusion.2
  1.5 0.7 fusion.6.masks
  2.1 1.4 copy.29
  3.5 0.3 copy.30
  3.8 0.0 copy-start.6
  3.8 0.0 copy-start.7
  3.8 0.0 copy-start.8
  3.8 0.0 copy-start.9
  3.9 0.0 copy-start.10
  3.9 0.0 copy-start.11
  3.9 0.0 copy-start.12
  3.9 0.0 copy-start.5
  3.9 1.5 fusion.2.both
  5.4 0.0 copy-done.6
  5.8 0.1 stack.41
  5.9 0.6 pad.42.own_vectors
  6.5 109.3 %layer_forward.1 = (bf16[832,768]{1,0:T(8,128)(2,1)}, bf16[832,2304]{1,0:T(8,128)(2,1)}, bf16[832,1536]{1,0:T(8,128)(2,1)}, bf16[832,768]{1,0:T(8,128)(2,1)}, bf...) custom-call(bf16[16,1536]{1,0:T(8,128)(2,1)} %pad.42.own_vectors, ...), custom_call_target="tpu_custom_call" | custom-call | tf_op jit(solution)/shard_map/layer_forward/pallas_call | solution.py:353
  115.8 69.4 %layer_backward.1 = (bf16[832,768]{1,0:T(8,128)(2,1)}, bf16[832,3072]{1,0:T(8,128)(2,1)}, bf16[832,768]{1,0:T(8,128)(2,1)}, bf16[832,2304]{1,0:T(8,128)(2,1)}, b...) custom-call(bf16[4,832,192]{2,1,0:T(8,128)(2,1)} %get-tuple-element.45.pieces, f32[8,3072]{1,0:T(8,128)} %get-tuple-element.46.vectors, ...), custom_call_target="tpu_custom_call" | custom-call | tf_op jit(solution)/shard_map/layer_backward/pallas_call | solution.py:542
  185.2 116.8 %weight_gradients.1 = (f32[96,1152]{1,0:T(8,128)}, f32[48,768]{1,0:T(8,128)}, f32[96,1536]{1,0:T(8,128)}, f32[192,768]{1,0:T(8,128)}, f32[8,3072]{1,0:T(8,128)}, /*index=5*/bf16[4,832,192]{2,1,0:T(8,128)(2,1)}) custom-call(bf16[832,768]{1,0:T(8,128)(2,1)} %get-tuple-element.44.a0_in, bf16[832,2304]{1,0:T(8,128)(2,1)} %get-tuple-element.58.dqkv_in, ...), custom_call_target="tpu_custom_call" | custom-call | tf_op jit(solution)/shard_map/weight_gradients/pallas_call | solution.py:802
  302.0 0.7 constant_dynamic-slice_fusion.1
  302.7 0.6 fusion.7
  303.3 1.5 slice_bitcast_fusion.1
  304.8 0.1 fusion.3
  305.0 1.5 copy.32
  306.5 0.1 pad_maximum_fusion.1
  306.7 1.1 copy.31
  307.8 1.5 constant_dynamic-slice_fusion.2
  309.3 1.3 constant_dynamic-slice_fusion.5
  310.7 0.8 copy.37
  311.4 0.7 copy.38
  312.1 0.8 copy.39
  312.9 0.8 copy.40
  (39 shorter events, 0.3 us)
Async XLA Ops:
  0.6 2.9 copy-start
  3.8 1.6 copy-start.6
  3.8 1.6 copy-start.7
  3.8 1.6 copy-start.8
  3.8 1.7 copy-start.9
  3.9 1.7 copy-start.10
  3.9 1.8 copy-start.11
  3.9 1.8 copy-start.12
  3.9 1.9 copy-start.5
  306.5 4.2 %copy-start.3 = (f32[96,1152]{1,0:T(8,128)S(1)}, f32[96,1152]{1,0:T(8,128)}, u32[]{:S(2)}) copy-start(f32[96,1152]{1,0:T(8,128)} %get-tuple-element.69) | copy-start | bytes 1327108
  306.5 4.9 %copy-start.4 = (f32[48,768]{1,0:T(8,128)S(1)}, f32[48,768]{1,0:T(8,128)}, u32[]{:S(2)}) copy-start(f32[48,768]{1,0:T(8,128)} %get-tuple-element.71) | copy-start | bytes 442372
  306.6 5.4 %copy-start.2 = (f32[96,1536]{1,0:T(8,128)S(1)}, f32[96,1536]{1,0:T(8,128)}, u32[]{:S(2)}) copy-start(f32[96,1536]{1,0:T(8,128)} %get-tuple-element.72) | copy-start | bytes 1769476
  306.7 6.2 %copy-start.1 = (f32[192,768]{1,0:T(8,128)S(1)}, f32[192,768]{1,0:T(8,128)}, u32[]{:S(2)}) copy-start(f32[192,768]{1,0:T(8,128)} %get-tuple-element.73) | copy-start | bytes 1769476

commit v3 on v2

v3 whole, which is shorter than its diff:
```python
import functools

import jax
import jax.numpy as jnp
from jax import lax
from jax.experimental import pallas as pl
from jax.experimental.pallas import tpu as pltpu
from jax.sharding import PartitionSpec as P

D = 768
HEADS = 12
HEAD_DIM = 64
FF = 3072
WORDS = 64
PAIR_ROWS = 104
HALF = D // 2
HIDDEN_HALF = FF // 2
QUARTER = D // 4
PIPE = 4
GROUP_WIDTH = 2 * HEAD_DIM
GROUPS = HEADS // 2
STACKED = 2 * PAIR_ROWS

EPSILON = 1e-05
NEGATIVE = -1e30
SCALE = HEAD_DIM ** (-0.5)

MESH = pl.DeviceIdType.MESH
BF = jnp.bfloat16
F32 = jnp.float32
VMEM_LIMIT = 60 << 20


def dot_nn(left, right):
    return lax.dot_general(left, right, (((1,), (0,)), ((), ())), preferred_element_type=F32)


def dot_nt(left, right):
    return lax.dot_general(left, right, (((1,), (1,)), ((), ())), preferred_element_type=F32)


def dot_tn(left, right):
    return lax.dot_general(left, right, (((0,), (0,)), ((), ())), preferred_element_type=F32)


def place():
    pipe = lax.axis_index("pipe")
    dp = lax.axis_index("dp")
    layer = pipe // 2
    half = pipe % 2
    across_x = pipe + 1 - 2 * half
    across_y = (pipe + 2) % 4
    core = dp % 2
    other_core = dp + 1 - 2 * core
    return pipe, dp, layer, half, across_x, across_y, core, other_core


def greet(devices):
    barrier = pltpu.get_barrier_semaphore()
    for device in devices:
        pl.semaphore_signal(barrier, inc=1, device_id=device, device_id_type=MESH)
    pl.semaphore_wait(barrier, len(devices))


def remote(source, target, send, recv, device):
    return pltpu.make_async_remote_copy(
        src_ref=source,
        dst_ref=target,
        send_sem=send,
        recv_sem=recv,
        device_id=device,
        device_id_type=MESH,
    )


WEIGHT_SHAPES = [(D, 3 * HALF), (HALF, D), (D, HIDDEN_HALF), (HIDDEN_HALF, D)]
CHUNKS = [(0, 0, 96), (0, 96, 96), (1, 0, 96), (2, 0, 96), (2, 96, 96), (3, 0, 192), (3, 192, 192)]
ATTENTION_CHUNKS = 3
DEPTH = 3


def left_lanes():
    return lax.broadcasted_iota(jnp.int32, (PAIR_ROWS, GROUP_WIDTH), 1) < HEAD_DIM


def stacked(values, scale=None):
    if scale is not None:
        values = values * scale
    left = left_lanes()
    return jnp.concatenate([jnp.where(left, values, 0.0), jnp.where(left, 0.0, values)], 0).astype(BF)


def own_lanes(values):
    return jnp.where(left_lanes(), values[:PAIR_ROWS], values[PAIR_ROWS:])


def normalized(residual):
    average = jnp.mean(residual, axis=-1, keepdims=True)
    centred = residual - average
    variance = jnp.mean(centred * centred, axis=-1, keepdims=True)
    inverse = lax.rsqrt(variance + EPSILON)
    return centred * inverse, inverse


def norm_backward(gradient, norm, inverse, gain):
    scaled = gradient * gain
    first = jnp.mean(scaled, axis=-1, keepdims=True)
    second = jnp.mean(scaled * norm, axis=-1, keepdims=True)
    return (scaled - first - norm * second) * inverse


def column_sums(value):
    return jnp.sum(value, axis=0, keepdims=True)


def layer_kernel(
    micros, block, local_pairs,
    captions, tokens, cotangent, biases, offsets, scaling, centring, lifting, settling, stretch, translate,
    own_proj, own_comb, own_exp, own_red,
    a0_out, context_out, a1_out, hidden_out, dr2_out, du_out, dr1_out, dqkv_out, sums_out, results_out,
    both, own_vectors, joint, mixing, expand, reduce, pieces, other_vectors, vectors, results,
    slots, outgoing, qkv_keep, prob_keep, n1_keep, r1_keep, n2_keep, r2_keep, slope_keep,
    a_s, qkv_s, context_s, dqkv_s,
    send, recv, x_send, x_recv, z_send, z_recv, near_send, near_recv, far_send, far_recv,
    own_sem, piece_send, piece_recv, vec_sem, result_send, result_recv, result_sem,
):
    pipe, dp, layer, half, across_x, across_y, core, other_core = place()
    step = pl.program_id(0)
    pairs = block // PAIR_ROWS
    rows = micros * block
    diagonal = (across_x + 2) % 4
    parity = (dp // 2) % 2
    across_z = dp + 2 - 4 * parity
    mine = 2 * parity + core
    paired = 2 * (1 - parity) + core
    relatives = (across_x, across_y, diagonal)
    owned = [own_proj, own_comb, own_exp, own_red]
    held = [joint, mixing, expand, reduce]
    n = len(CHUNKS)

    def span(chunk, quarter):
        which, start, count = chunk
        return pl.ds(quarter * (WEIGHT_SHAPES[which][0] // 4) + start, count)

    def x_copy(k):
        at = span(CHUNKS[k], mine)
        which = CHUNKS[k][0]
        return remote(owned[which].at[at], held[which].at[half, at], x_send.at[k], x_recv.at[k], (across_x, dp))

    def z_copy(k):
        region = held[CHUNKS[k][0]].at[1 - half, span(CHUNKS[k], mine)]
        return remote(region, region, z_send.at[k], z_recv.at[k], (pipe, across_z))

    def near_copy(k):
        region = held[CHUNKS[k][0]].at[1 - half, span(CHUNKS[k], mine)]
        return remote(region, region, near_send.at[k], near_recv.at[k], (pipe, other_core))

    def far_copy(k):
        region = held[CHUNKS[k][0]].at[1 - half, span(CHUNKS[k], paired)]
        return remote(region, region, far_send.at[k], far_recv.at[k], (pipe, other_core))

    own_copies = [pltpu.make_async_copy(owned[i], held[i].at[half], own_sem.at[i]) for i in range(4)]
    own_piece = pltpu.make_async_copy(both.at[layer, half], pieces.at[pipe], own_sem.at[4])
    vec_copy = remote(own_vectors, other_vectors, vec_sem.at[0], vec_sem.at[1], (across_x, dp))
    piece_copies = [
        remote(
            both.at[target // 2, target % 2], pieces.at[pipe], piece_send.at[j], piece_recv.at[j], (target, dp)
        )
        for j, target in enumerate(relatives)
    ]

    def send_pieces(to_layer):
        for j, target in enumerate(relatives):
            @pl.when(target // 2 == to_layer)
            def _():
                piece_copies[j].start()

    def gathered(first, last):
        for k in range(first, last):
            x_copy(k).wait_recv()
            z_copy(k).start()
            near_copy(k).start()
            if k + DEPTH < n:
                x_copy(k).wait_send()
                x_copy(k + DEPTH).start()
            if k + DEPTH == n - 1:
                send_pieces(1)
        for k in range(first, last):
            z_copy(k).wait_recv()
            far_copy(k).start()
        for k in range(first, last):
            near_copy(k).wait_recv()
            far_copy(k).wait_recv()

    def rest_gathered():
        gathered(ATTENTION_CHUNKS, n)
        own_copies[2].wait()
        own_copies[3].wait()

    def y_copy(index):
        return remote(outgoing.at[index], slots.at[index], send.at[index], recv.at[index], (across_y, dp))

    def rows_of(index):
        return pl.ds(pl.multiple_of(index * block, 16), block)

    def result_copies(index):
        return [
            remote(
                results.at[target, rows_of(index)], results_out.at[pipe, rows_of(index)],
                result_send.at[j, index], result_recv.at[j, index], (target, dp),
            )
            for j, target in enumerate(relatives)
        ]

    def own_result(index):
        return pltpu.make_async_copy(
            results.at[pipe, rows_of(index)], results_out.at[pipe, rows_of(index)], result_sem.at[index]
        )

    def share_result(index, value):
        for i in range(PIPE):
            results[i, rows_of(index), :] = value[:, i * QUARTER : (i + 1) * QUARTER]
        for copy in result_copies(index):
            copy.start()
        own_result(index).start()

    def from_pieces(index):
        folded = micros // 2
        for k in range(2):
            @pl.when(index // folded == k)
            def _():
                at = pl.ds(pl.multiple_of((index - k * folded) * block, 16), block)
                lanes = slice(k * QUARTER, (k + 1) * QUARTER)
                a_s[...] = jnp.concatenate([pieces[i, at, lanes] for i in range(PIPE)], 1)

    @pl.when(step == 0)
    def _():
        for copy in own_copies:
            copy.start()
        fold = rows // 2
        for t, source in enumerate((tokens, cotangent)):
            for h in range(2):
                blocks = []
                for k in range(2):
                    first = h * rows + k * fold
                    value = source[first : min(first + fold, source.shape[0]), :].astype(F32)
                    if value.shape[0] < fold:
                        value = jnp.concatenate([value, jnp.zeros((fold - value.shape[0], QUARTER), F32)], 0)
                    blocks.append(value)
                both[t, h] = jnp.concatenate(blocks, 1).astype(BF)
        for i, source in enumerate((biases, offsets, scaling, centring, lifting, settling, stretch, translate)):
            own_vectors[i : i + 1, : source.shape[1]] = source[...].astype(F32)
        own_piece.start()
        sums_out[...] = jnp.zeros_like(sums_out)
        greet([(across_x, dp), (across_y, dp), (diagonal, dp), (pipe, across_z), (pipe, other_core)])
        vec_copy.start()
        send_pieces(0)
        for k in range(DEPTH):
            x_copy(k).start()
        vec_copy.wait_recv()
        for which in range(2):
            value = jnp.where(half == which, own_vectors[...], other_vectors[...])
            vectors[0:1, which * 3 * HALF : which * 3 * HALF + HALF] = value[0:1, :HALF]
            vectors[0:1, which * 3 * HALF + HALF : which * 3 * HALF + D] = jnp.zeros((1, HALF), F32)
            vectors[0:1, which * 3 * HALF + D : (which + 1) * 3 * HALF] = value[0:1, HALF:D]
            for i in (1, 2, 3, 5, 6, 7):
                vectors[i : i + 1, which * HALF : (which + 1) * HALF] = value[i : i + 1, :HALF]
            vectors[4:5, which * HIDDEN_HALF : (which + 1) * HIDDEN_HALF] = value[4:5, :]
        own_piece.wait()

        @pl.when(layer == 0)
        def _():
            for copy in piece_copies:
                copy.wait_recv()

        gathered(0, ATTENTION_CHUNKS)
        own_copies[0].wait()
        own_copies[1].wait()

        @pl.when(layer == 1)
        def _():
            rest_gathered()

    @pl.when(step < micros)
    def _():
        micro = step

        @pl.when(layer == 0)
        def _():
            from_pieces(micro)

        @pl.when(layer == 1)
        def _():
            y_copy(micro).wait_recv()
            a_s[...] = slots[micro]

        inputs = a_s[...]
        a0_out[...] = inputs
        for which in range(2):
            value = dot_nn(inputs, joint[which]) + vectors[0:1, which * 3 * HALF : (which + 1) * 3 * HALF]
            for part in range(3):
                cols = slice(part * D + which * HALF, part * D + (which + 1) * HALF)
                found = value[:, part * HALF : (part + 1) * HALF]
                qkv_s[:, cols] = found
                qkv_keep[micro, :, cols] = found.astype(BF)
        over = [(pair, group) for pair in range(pairs) for group in range(GROUPS)]
        spans = [
            (
                slice(pair * PAIR_ROWS, (pair + 1) * PAIR_ROWS),
                [slice(part * D + group * GROUP_WIDTH, part * D + (group + 1) * GROUP_WIDTH) for part in range(3)],
            )
            for pair, group in over
        ]
        key = lax.broadcasted_iota(jnp.int32, (PAIR_ROWS, PAIR_ROWS), 0)
        masks = []
        for pair in range(pairs):
            length = captions[jnp.minimum((half * micros + micro) * pairs + pair, local_pairs - 1)]
            masks.append(jnp.where((key >= WORDS) | (key < length), 0.0, NEGATIVE))
        scores = [
            dot_nt(stacked(qkv_s[at, lanes[1]], SCALE), qkv_s[at, lanes[0]].astype(BF)) for at, lanes in spans
        ]
        values = [stacked(qkv_s[at, lanes[2]]) for at, lanes in spans]
        probs = []
        for k, (pair, group) in enumerate(over):
            found = []
            for i in range(2):
                score = scores[k][i * PAIR_ROWS : (i + 1) * PAIR_ROWS] + masks[pair]
                exponent = jnp.exp(score - jnp.max(score, axis=0, keepdims=True))
                found.append(exponent * (1.0 / jnp.sum(exponent, axis=0, keepdims=True)))
            probs.append(jnp.concatenate(found, 0).astype(BF))
        contexts = [dot_tn(probs[k], values[k]) for k in range(len(over))]
        for k, (at, lanes) in enumerate(spans):
            prob_keep[micro, k] = probs[k]
            context_s[at, lanes[0]] = contexts[k]
        context = context_s[...].astype(BF)
        context_out[...] = context
        residual = inputs.astype(F32) + dot_nn(context, mixing[...].reshape(D, D)) + vectors[1:2, :D]
        norm, inverse = normalized(residual)
        n1_keep[micro] = norm.astype(BF)
        r1_keep[micro] = inverse
        attended = (norm * vectors[2:3, :D] + vectors[3:4, :D]).astype(BF)
        a1_out[...] = attended

        @pl.when((micro == 0) & (layer == 0))
        def _():
            rest_gathered()

        residual = attended.astype(F32) + vectors[5:6, :D]
        for which in range(2):
            cols = slice(which * HIDDEN_HALF, (which + 1) * HIDDEN_HALF)
            raised = dot_nn(attended, expand[which]) + vectors[4:5, cols]
            below = 0.5 * (1.0 + lax.erf(raised * (0.5**0.5)))
            hidden = (raised * below).astype(BF)
            hidden_out[:, cols] = hidden
            density = jnp.exp(raised * raised * (-0.5)) * 0.3989422804014327
            slope_keep[micro, :, cols] = (below + raised * density).astype(BF)
            residual = residual + dot_nn(hidden, reduce[which])
        norm, inverse = normalized(residual)
        n2_keep[micro] = norm.astype(BF)
        r2_keep[micro] = inverse
        result = (norm * vectors[6:7, :D] + vectors[7:8, :D]).astype(BF)

        @pl.when(layer == 0)
        def _():
            outgoing[micro] = result
            y_copy(micro).start()

        @pl.when(layer == 1)
        def _():
            share_result(micro, result)

    def add_sum(row, value):
        width = value.shape[1]
        sums_out[row : row + 1, :width] += column_sums(value)

    @pl.when(step >= micros)
    def _():
        micro = step - micros

        @pl.when((layer == 1) & (micro == 0))
        def _():
            for copy in piece_copies:
                copy.wait_recv()

        @pl.when(layer == 1)
        def _():
            from_pieces(micro)

        @pl.when(layer == 0)
        def _():
            y_copy(micro).wait_recv()
            a_s[...] = slots[micro]

        gradient = a_s[...].astype(F32)
        norm = n2_keep[micro].astype(F32)
        add_sum(6, gradient * norm)
        add_sum(7, gradient)
        grad_residual = norm_backward(gradient, norm, r2_keep[micro], vectors[6:7, :D])
        add_sum(5, grad_residual)
        branch = grad_residual.astype(BF)
        dr2_out[...] = branch
        total = grad_residual
        for which in range(2):
            cols = slice(which * HIDDEN_HALF, (which + 1) * HIDDEN_HALF)
            raised = dot_nt(branch, reduce[which]) * slope_keep[micro, :, cols].astype(F32)
            sums_out[4:5, cols] += column_sums(raised)
            raised = raised.astype(BF)
            du_out[:, cols] = raised
            total = total + dot_nt(raised, expand[which])

        gradient = total.astype(BF).astype(F32)
        norm = n1_keep[micro].astype(F32)
        add_sum(2, gradient * norm)
        add_sum(3, gradient)
        grad_residual = norm_backward(gradient, norm, r1_keep[micro], vectors[2:3, :D])
        add_sum(1, grad_residual)
        branch = grad_residual.astype(BF)
        dr1_out[...] = branch
        context_s[...] = dot_nt(branch, mixing[...].reshape(D, D))
        qkv_s[...] = qkv_keep[micro].astype(F32)
        spans = [
            (
                slice(pair * PAIR_ROWS, (pair + 1) * PAIR_ROWS),
                [slice(part * D + group * GROUP_WIDTH, part * D + (group + 1) * GROUP_WIDTH) for part in range(3)],
            )
            for pair in range(pairs)
            for group in range(GROUPS)
        ]
        over = range(len(spans))
        queries = [qkv_s[at, lanes[0]].astype(BF) for at, lanes in spans]
        keys = [stacked(qkv_s[at, lanes[1]], SCALE) for at, lanes in spans]
        values = [stacked(qkv_s[at, lanes[2]]) for at, lanes in spans]
        grads = [context_s[at, lanes[0]].astype(BF) for at, lanes in spans]
        rounded = [prob_keep[micro, g] for g in over]
        grad_probs = [dot_nt(values[g], grads[g]) for g in over]
        grad_values = [dot_nn(rounded[g], grads[g]) for g in over]
        grad_scores = []
        for g in over:
            probs = rounded[g].astype(F32)
            weighted = probs * grad_probs[g]
            found = []
            for i in range(2):
                at = slice(i * PAIR_ROWS, (i + 1) * PAIR_ROWS)
                found.append(weighted[at] - probs[at] * column_sums(weighted[at]))
            grad_scores.append(jnp.concatenate(found, 0).astype(BF))
        grad_keys = [dot_nn(grad_scores[g], queries[g]) for g in over]
        grad_queries = [dot_tn(grad_scores[g], keys[g]) for g in over]
        for g, (at, lanes) in enumerate(spans):
            dqkv_s[at, lanes[0]] = grad_queries[g]
            dqkv_s[at, lanes[1]] = own_lanes(grad_keys[g]) * SCALE
            dqkv_s[at, lanes[2]] = own_lanes(grad_values[g])
        total = grad_residual
        for which in range(2):
            value = jnp.concatenate(
                [dqkv_s[:, part * D + which * HALF : part * D + (which + 1) * HALF] for part in range(3)], 1
            ).astype(BF)
            cols = slice(which * 3 * HALF, (which + 1) * 3 * HALF)
            dqkv_out[:, cols] = value
            sums_out[0:1, cols] += column_sums(value.astype(F32))
            total = total + dot_nt(value, joint[which])
        result = total.astype(BF)

        @pl.when(layer == 1)
        def _():
            outgoing[micro] = result
            y_copy(micro).start()

        @pl.when(layer == 0)
        def _():
            share_result(micro, result)

    @pl.when(step == 2 * micros - 1)
    def _():
        for index in range(micros):
            y_copy(index).wait_send()
            own_result(index).wait()
            for copy in result_copies(index):
                copy.wait()
        for k in range(n):
            if k + DEPTH >= n:
                x_copy(k).wait_send()
            z_copy(k).wait_send()
            near_copy(k).wait_send()
            far_copy(k).wait_send()
        for copy in piece_copies + [vec_copy]:
            copy.wait_send()


def layer_passes(micros, block, captions, small, tokens, cotangent, owned):
    rows = micros * block
    n = len(CHUNKS)
    vmem = pl.BlockSpec(memory_space=pltpu.VMEM)
    hbm = pl.BlockSpec(memory_space=pl.ANY)

    def forward_rows(width):
        return pl.BlockSpec((block, width), lambda s: (jnp.minimum(s, micros - 1), 0))

    def backward_rows(width):
        return pl.BlockSpec((block, width), lambda s: (jnp.maximum(s - micros, 0), 0))

    forward_widths = [D, D, D, FF]
    backward_widths = [D, FF, D, 3 * D]
    pairs = block // PAIR_ROWS
    return pl.pallas_call(
        functools.partial(layer_kernel, micros, block, captions.shape[0]),
        grid=(2 * micros,),
        out_shape=[jax.ShapeDtypeStruct((rows, w), BF) for w in forward_widths + backward_widths]
        + [jax.ShapeDtypeStruct((8, FF), F32), jax.ShapeDtypeStruct((PIPE, rows, QUARTER), BF)],
        in_specs=[pl.BlockSpec(memory_space=pltpu.SMEM)] + [vmem] * 10 + [hbm] * 4,
        out_specs=[forward_rows(w) for w in forward_widths]
        + [backward_rows(w) for w in backward_widths]
        + [vmem, hbm],
        scratch_shapes=[
            pltpu.VMEM((2, 2, rows // 2, 2 * QUARTER), BF),
            pltpu.VMEM((8, HIDDEN_HALF), F32),
        ]
        + [pltpu.VMEM((2,) + shape, BF) for shape in WEIGHT_SHAPES]
        + [
            pltpu.VMEM((PIPE, rows // 2, 2 * QUARTER), BF),
            pltpu.VMEM((8, HIDDEN_HALF), F32),
            pltpu.VMEM((8, FF), F32),
            pltpu.VMEM((PIPE, rows, QUARTER), BF),
            pltpu.VMEM((micros, block, D), BF),
            pltpu.VMEM((micros, block, D), BF),
            pltpu.VMEM((micros, block, 3 * D), BF),
            pltpu.VMEM((micros, pairs * GROUPS, STACKED, PAIR_ROWS), BF),
            pltpu.VMEM((micros, block, D), BF),
            pltpu.VMEM((micros, block, 1), F32),
            pltpu.VMEM((micros, block, D), BF),
            pltpu.VMEM((micros, block, 1), F32),
            pltpu.VMEM((micros, block, FF), BF),
            pltpu.VMEM((block, D), BF),
            pltpu.VMEM((block, 3 * D), F32),
            pltpu.VMEM((block, D), F32),
            pltpu.VMEM((block, 3 * D), F32),
            pltpu.SemaphoreType.DMA((micros,)),
            pltpu.SemaphoreType.DMA((micros,)),
        ]
        + [pltpu.SemaphoreType.DMA((n,))] * 8
        + [
            pltpu.SemaphoreType.DMA((5,)),
            pltpu.SemaphoreType.DMA((3,)),
            pltpu.SemaphoreType.DMA((3,)),
            pltpu.SemaphoreType.DMA((2,)),
            pltpu.SemaphoreType.DMA((3, micros)),
            pltpu.SemaphoreType.DMA((3, micros)),
            pltpu.SemaphoreType.DMA((micros,)),
        ],
        compiler_params=pltpu.CompilerParams(collective_id=1, has_side_effects=True, vmem_limit_bytes=VMEM_LIMIT),
        name="layer_passes",
    )(captions, tokens, cotangent, *small, *owned)


TILE = 384


def weights_kernel(
    n_dp,
    a0_in, dqkv_in, context_in, dr1_in, a1_in, du_in, hidden_in, dr2_in, sums,
    g_proj, g_comb, g_exp, g_red, sums_out,
    b_proj, b_comb, b_exp, b_red,
    c_proj, c_comb, c_exp, c_red,
    x_proj, x_comb, x_exp, x_red,
    z_proj, z_comb, z_exp, z_red,
    sums_core, sums_x, sums_z, sums_a, sums_b,
    a0, dqkv, context, dr1, a1, du, hidden, dr2,
    core_send, core_recv, x_send, x_recv, z_send, z_recv,
    small_send, small_recv, load_sem,
):
    pipe, dp, layer, half, across_x, across_y, core, other_core = place()
    n_z = n_dp // 2
    z = dp // 2
    offsets = sorted(range(1, n_z), key=lambda off: -min(off, n_z - off)) + [0]
    z_order = [(z + off) % n_z for off in offsets]
    z_others = z_order[:-1]
    loads = [
        pltpu.make_async_copy(source, target, load_sem.at[i])
        for i, (source, target) in enumerate((
            (hidden_in, hidden), (dr2_in, dr2), (a1_in, a1), (du_in, du),
            (a0_in, a0), (dqkv_in, dqkv), (context_in, context), (dr1_in, dr1),
        ))
    ]
    for copy in loads:
        copy.start()
    greet(
        [(across_x, dp), (pipe, other_core)]
        + [(pipe, 2 * other + core) for other in z_others]
    )

    mine = [b_red, b_exp, b_proj, b_comb]
    from_core = [c_red, c_exp, c_proj, c_comb]
    from_x = [x_red, x_exp, x_proj, x_comb]
    from_z = [z_red, z_exp, z_proj, z_comb]
    outs = [g_red, g_exp, g_proj, g_comb]

    def spread(target, tile, cast=BF):
        r = target.shape[-2]
        for k in range(tile.shape[0] // (2 * r)):
            for c in range(2):
                yield c, k, tile[(2 * k + c) * r : (2 * k + c + 1) * r].astype(cast)

    def fill_red(h):
        for part in range(HIDDEN_HALF // D):
            lanes = pl.ds(pl.multiple_of(h * HIDDEN_HALF + part * D, 128), D)
            shards_here = D // (2 * b_red.shape[3])
            for c, k, rows in spread(b_red, dot_tn(hidden[:, lanes], dr2[...])):
                b_red[c, h, part * shards_here + k] = rows

    def fill_exp(step, carry):
        i, h = step // 2, step % 2
        tile = dot_tn(
            a1[:, pl.ds(pl.multiple_of(i * TILE, 128), TILE)],
            du[:, pl.ds(pl.multiple_of(h * HIDDEN_HALF, 128), HIDDEN_HALF)],
        )
        for c, k, rows in spread(b_exp, tile):
            b_exp[c, h, i * (TILE // (2 * b_exp.shape[3])) + k] = rows
        return carry

    def fill_proj(h, carry):
        tile = dot_tn(a0[...], dqkv[:, pl.ds(pl.multiple_of(h * 3 * HALF, 128), 3 * HALF)])
        for c, k, rows in spread(b_proj, tile):
            b_proj[c, h, k] = rows
        return carry

    def fill_comb():
        tile = dot_tn(context[...], dr1[...])
        for h in range(2):
            for c, k, rows in spread(b_comb, tile[h * HALF : (h + 1) * HALF]):
                b_comb[c, h, k] = rows

    def core_copy(a, which):
        at = 1 - half if which == 0 else half
        return remote(
            mine[a].at[1 - core, at], from_core[a].at[at], core_send.at[a, which], core_recv.at[a, which],
            (pipe, other_core),
        )

    def x_copy(k):
        a, i = chunks[k]
        return remote(
            mine[a].at[core, 1 - half, z_order[i]], from_x[a].at[z_order[i]], x_send.at[a, i], x_recv.at[a, i],
            (across_x, dp),
        )

    def z_copy(a, i):
        other = z_order[i]
        return remote(
            mine[a].at[core, half, other], from_z[a].at[i], z_send.at[a, i], z_recv.at[a, i],
            (pipe, 2 * other + core),
        )

    chunks = [(a, i) for a in range(4) for i in range(n_z)]

    def start_x(k):
        if k >= len(chunks):
            return
        a, i = chunks[k]
        at = z_order[i]
        total = mine[a][core, 1 - half, at].astype(F32) + from_core[a][1 - half, at].astype(F32)
        mine[a][core, 1 - half, at] = total.astype(BF)
        x_copy(k).start()

    def after_x(k):
        a, i = chunks[k]
        at = z_order[i]
        x_copy(k).wait()
        start_x(k + DEPTH)
        if i == 0:
            core_copy(a, 1).wait_recv()
        total = mine[a][core, half, at].astype(F32) + from_core[a][half, at].astype(F32) + from_x[a][at].astype(F32)
        if i < n_z - 1:
            mine[a][core, half, at] = total.astype(BF)
            z_copy(a, i).start()
        else:
            outs[a][...] = total

    def after_z(a):
        total = outs[a][...]
        for i in range(n_z - 1):
            z_copy(a, i).wait()
            total = total + from_z[a][i].astype(F32)
        outs[a][...] = total

    sums_copy_core = remote(sums, sums_core, small_send.at[0], small_recv.at[0], (pipe, other_core))
    sums_copy_x = remote(sums_a, sums_x, small_send.at[1], small_recv.at[1], (across_x, dp))
    sums_copies_z = [
        remote(sums_b, sums_z.at[i], small_send.at[2 + i], small_recv.at[2 + i], (pipe, 2 * other + core))
        for i, other in enumerate(z_others)
    ]

    sums_copy_core.start()
    loads[0].wait()
    loads[1].wait()
    fill_red(1 - half)
    core_copy(0, 0).start()
    fill_red(half)
    core_copy(0, 1).start()
    core_copy(0, 0).wait_recv()
    for k in range(DEPTH):
        start_x(k)
    loads[2].wait()
    loads[3].wait()
    lax.fori_loop(0, 2 * D // TILE, fill_exp, 0)
    core_copy(1, 0).start()
    core_copy(1, 1).start()
    sums_copy_core.wait()
    sums_a[...] = sums[...] + sums_core[...]
    sums_copy_x.start()
    core_copy(1, 0).wait_recv()
    after_x(0)
    loads[4].wait()
    loads[5].wait()
    lax.fori_loop(0, 2, fill_proj, 0)
    core_copy(2, 0).start()
    core_copy(2, 1).start()
    after_x(1)
    loads[6].wait()
    loads[7].wait()
    fill_comb()
    core_copy(3, 0).start()
    core_copy(3, 1).start()
    sums_copy_x.wait()
    sums_b[...] = sums_a[...] + sums_x[...]
    for copy in sums_copies_z:
        copy.start()
    core_copy(2, 0).wait_recv()
    core_copy(3, 0).wait_recv()
    for k in range(2, len(chunks)):
        after_x(k)
        if k % n_z == n_z - 2 and k >= n_z:
            after_z(k // n_z - 1)
    after_z(3)
    for a in range(4):
        for which in range(2):
            core_copy(a, which).wait_send()
    total = sums_b[...]
    for i in range(n_z - 1):
        sums_copies_z[i].wait()
        total = total + sums_z[i]
    sums_out[...] = total


def weight_gradients(n_dp, a0, dqkv, context, dr1, a1, du, hidden, dr2, sums):
    vmem = pl.BlockSpec(memory_space=pltpu.VMEM)
    hbm = pl.BlockSpec(memory_space=pl.ANY)
    n_z = n_dp // 2
    shapes = [(D // n_dp, 3 * HALF), (HALF // n_dp, D), (D // n_dp, HIDDEN_HALF), (HIDDEN_HALF // n_dp, D)]
    return pl.pallas_call(
        functools.partial(weights_kernel, n_dp),
        out_shape=[jax.ShapeDtypeStruct(s, F32) for s in shapes]
        + [jax.ShapeDtypeStruct(sums.shape, F32)],
        in_specs=[hbm] * 8 + [vmem],
        out_specs=[vmem] * 5,
        scratch_shapes=[pltpu.VMEM((2, 2, n_z) + s, BF) for s in shapes]
        + [pltpu.VMEM((2, n_z) + s, BF) for s in shapes]
        + [pltpu.VMEM((n_z,) + s, BF) for s in shapes]
        + [pltpu.VMEM((n_z - 1,) + s, BF) for s in shapes]
        + [
            pltpu.VMEM(sums.shape, F32),
            pltpu.VMEM(sums.shape, F32),
            pltpu.VMEM((n_z - 1,) + sums.shape, F32),
            pltpu.VMEM(sums.shape, F32),
            pltpu.VMEM(sums.shape, F32),
        ]
        + [pltpu.VMEM(v.shape, BF) for v in (a0, dqkv, context, dr1, a1, du, hidden, dr2)]
        + [
            pltpu.SemaphoreType.DMA((4, 2)),
            pltpu.SemaphoreType.DMA((4, 2)),
            pltpu.SemaphoreType.DMA((4, n_z)),
            pltpu.SemaphoreType.DMA((4, n_z)),
            pltpu.SemaphoreType.DMA((4, n_z - 1)),
            pltpu.SemaphoreType.DMA((4, n_z - 1)),
            pltpu.SemaphoreType.DMA((n_z + 1,)),
            pltpu.SemaphoreType.DMA((n_z + 1,)),
            pltpu.SemaphoreType.DMA((8,)),
        ],
        compiler_params=pltpu.CompilerParams(collective_id=3, has_side_effects=True, vmem_limit_bytes=VMEM_LIMIT),
        name="weight_gradients",
    )(a0, dqkv, context, dr1, a1, du, hidden, dr2, sums)


def finish_kernel(n_dp, small, results, *refs):
    pipe, dp, layer, half, across_x, across_y, core, other_core = place()
    sources, encoded, tokens_grad, outs, parts = refs[:4], refs[4], refs[5], refs[6:10], refs[10:]
    for source, out in zip(sources, outs):
        out[0] = source[...]
    rows = results.shape[1]
    spare = encoded.shape[0] - rows
    tokens_grad[:rows] = results[0].astype(F32)
    tokens_grad[rows:] = results[1, :spare].astype(F32)
    encoded[:rows] = results[2]
    encoded[rows:] = results[3, :spare]
    for row, out in enumerate(parts):
        count = out.shape[1]
        width = n_dp * count
        found = jnp.zeros(out.shape, F32)
        for h in range(2):
            for d in range(n_dp):
                at = d * count
                if row == 0:
                    at = h * 3 * HALF + at + (HALF if at >= HALF else 0)
                else:
                    at = h * width + at
                found = jnp.where((half == h) & (dp == d), small[row : row + 1, at : at + count], found)
        out[...] = found


def finish(n_dp, local_rows, small, results, grads):
    vmem = pl.BlockSpec(memory_space=pltpu.VMEM)
    widths = [D, HALF, HALF, HALF, HIDDEN_HALF, HALF, HALF, HALF]
    return pl.pallas_call(
        functools.partial(finish_kernel, n_dp),
        out_shape=[
            jax.ShapeDtypeStruct((local_rows, QUARTER), BF),
            jax.ShapeDtypeStruct((local_rows, QUARTER), F32),
        ]
        + [jax.ShapeDtypeStruct((1,) + g.shape, F32) for g in grads]
        + [jax.ShapeDtypeStruct((1, w // n_dp), F32) for w in widths],
        in_specs=[vmem] * 6,
        out_specs=[vmem] * 14,
        compiler_params=pltpu.CompilerParams(vmem_limit_bytes=VMEM_LIMIT),
        name="finish",
    )(small, results, *grads)


def weight_gradients_by_scatter(n_dp, a0, dqkv, context, dr1, a1, du, hidden, dr2, sums):
    half = lax.axis_index("pipe") % 2
    halves = (
        dot_tn(a0, dqkv).reshape(D, 2, 3 * HALF).transpose(1, 0, 2),
        dot_tn(context, dr1).reshape(2, HALF, D),
        dot_tn(a1, du).reshape(D, 2, HIDDEN_HALF).transpose(1, 0, 2),
        dot_tn(hidden, dr2).reshape(2, HIDDEN_HALF, D),
    )
    swap = [(i, i ^ 1) for i in range(PIPE)]
    found = []
    for member in halves:
        part = lax.psum_scatter(member, "dp", scatter_dimension=1, tiled=True)
        keep = lax.dynamic_index_in_dim(part, half, 0, keepdims=False)
        send = lax.dynamic_index_in_dim(part, 1 - half, 0, keepdims=False)
        found.append(keep + lax.ppermute(send.astype(BF), "pipe", swap).astype(F32))
    small = lax.psum(sums, "dp")
    return found + [small + lax.ppermute(small, "pipe", swap)]


def shards(
    n_dp,
    tokens, cotangent, captions, projection, biases, combiner, offsets, scaling, centring,
    expansion, lifting, reduction, settling, stretch, translate,
):
    local_rows = tokens.shape[0]
    local_pairs = local_rows // PAIR_ROWS
    pairs = 2 * ((local_pairs + 3) // 4)
    block = 2 * PAIR_ROWS
    micros = pairs // 2
    owned = (projection[0], combiner[0], expansion[0], reduction[0])
    small = (biases, offsets, scaling, centring, lifting, settling, stretch, translate)
    *kept, results = layer_passes(micros, block, captions, small, tokens, cotangent, owned)
    a0, context, a1, hidden, dr2, du, dr1, dqkv, sums = kept
    whole_tiles = HALF % (16 * n_dp) == 0
    collect = weight_gradients if whole_tiles else weight_gradients_by_scatter
    *grads, sums = collect(n_dp, a0, dqkv, context, dr1, a1, du, hidden, dr2, sums)
    encoded, tokens_grad, g_proj, g_comb, g_exp, g_red, *parts = finish(n_dp, local_rows, sums, results, grads)
    return (
        encoded, tokens_grad, g_proj, parts[0], g_comb, parts[1], parts[2], parts[3],
        g_exp, parts[4], g_red, parts[5], parts[6], parts[7],
    )


def solution(mesh):
    rows = P("dp", "pipe")
    matrix = P("pipe", None, None)
    vector = P("pipe", None)
    matrix_out = P("pipe", "dp", None)
    vector_out = P("pipe", "dp")
    in_specs = (
        rows, rows, P("dp"), matrix, vector, matrix, vector, vector, vector,
        matrix, vector, matrix, vector, vector, vector,
    )
    out_specs = (
        rows, rows, matrix_out, vector_out, matrix_out, vector_out, vector_out, vector_out,
        matrix_out, vector_out, matrix_out, vector_out, vector_out, vector_out,
    )
    return jax.shard_map(
        functools.partial(shards, mesh.shape["dp"]),
        mesh=mesh, in_specs=in_specs, out_specs=out_specs, check_vma=False,
    )
```

time: 314 us -> 275 us (0.88)
  Pallas kernels: 295 us -> 266 us
  local copies, waits for them, and re-layouts: 14.1 us -> 8.74 us
    pallas_call x2, Pallas kernels: 179 us -> 159 us  [the longest x1 154 us: layer_passes(): pl.pallas_call(functools.partial(layer_kernel, micros, block, captions.sh...]
    pallas_call x1, Pallas kernels: 117 us -> 107 us  [weight_gradients(): pl.pallas_call(functools.partial(weights_kernel, n_dp), out_shape=[jax.Sh...]
    dynamic_slice x3 -> x0, local copies, waits for them, and re-layouts: 3.65 us -> none  [the longest x2 2.86 us: own(): lax.dynamic_slice(small, (row, start + half * width + dp * count), (1, co...]
    unnamed x34 -> x6, local copies, waits for them, and re-layouts: 7.43 us -> 8.74 us
where the time goes in v3:
time: 275 us
  Pallas kernels  266 us (97%)
  local copies, waits for them, and re-layouts  8.74 us (3%)
    pallas_call x1, Pallas kernels, layer_passes(): pl.pallas_call(functools.partial(layer_kernel, micros, block, captions.sh...  154 us
    pallas_call x1, Pallas kernels, weight_gradients(): pl.pallas_call(functools.partial(weights_kernel, n_dp), out_shape=[jax.Sh...  107 us
    unnamed x6, local copies, waits for them, and re-layouts  8.74 us

profile of v3, /device:TPU:0, one launch (start us, length us, event | category | flops | bytes accessed | tf_op | source)
XLA Modules:
  0.0 275.1 jit_solution(14125505627981296441)
XLA Ops:
  0.6 0.0 copy-start
  0.7 2.3 copy.29.tokens
  3.0 0.0 copy-done
  3.0 1.2 copy.30.cotangent
  4.2 153.8 %layer_passes.1 = (bf16[832,768]{1,0:T(8,128)(2,1)}, bf16[832,768]{1,0:T(8,128)(2,1)}, bf16[832,768]{1,0:T(8,128)(2,1)}, bf16[832,3072]{1,0:T(8,128)(2,1)}, bf16...) custom-call(s32[15]{0:T(128)} %captions.1, ...), custom_call_target="tpu_custom_call" | custom-call | tf_op jit(solution)/shard_map/layer_passes/pallas_call | solution.py:504
  158.0 106.7 %weight_gradients.1 = (f32[96,1152]{1,0:T(8,128)}, f32[48,768]{1,0:T(8,128)}, f32[96,1536]{1,0:T(8,128)}, f32[192,768]{1,0:T(8,128)}, f32[8,3072]{1,0:T(8,128)}) custom-call(bf16[832,768]{1,0:T(8,128)(2,1)} %get-tuple-element.43.a0_in, bf16[832,2304]{1,0:T(8,128)(2,1)} %get-tuple-element.44.dqkv_in, bf16[832,768]{1,0:T(8,128)(2,1)} %get-tuple-element.45.context_in, ...), custom_call_target="tpu_custom_call" | custom-call | tf_op jit(solution)/shard_map/weight_gradients/pallas_call | solution.py:748
  264.8 5.1 %finish.1 = (bf16[1560,192]{1,0:T(8,128)(2,1)}, f32[1560,192]{1,0:T(8,128)}, f32[1,96,1152]{2,1,0:T(8,128)}, f32[1,48,768]{2,1,0:T(8,128)}, f32[1,96,1536]{2,1,0...) custom-call(f32[8,3072]{1,0:T(8,128)} %get-tuple-element.52.small, ...), custom_call_target="tpu_custom_call" | custom-call | tf_op jit(solution)/shard_map/finish/pallas_call | solution.py:811
  269.9 2.3 copy.31
  272.2 2.9 %copy.32 = f32[1560,192]{0,1:T(8,128)} copy(f32[1560,192]{1,0:T(8,128)} %get-tuple-element.73) | data formatting | bytes 2396160
Async XLA Ops:
  0.6 2.3 copy-start

commit v4 on v3

--- a/solution.py
+++ b/solution.py
@@ -74,9 +74,11 @@
 
 
 WEIGHT_SHAPES = [(D, 3 * HALF), (HALF, D), (D, HIDDEN_HALF), (HIDDEN_HALF, D)]
-CHUNKS = [(0, 0, 96), (0, 96, 96), (1, 0, 96), (2, 0, 96), (2, 96, 96), (3, 0, 192), (3, 192, 192)]
+CHUNKS = [(0, 0, 96), (0, 96, 96), (1, 0, 96)] + [(2, i*48, 48) for i in range(4)] + [(3, i*96, 96) for i in range(4)]
 ATTENTION_CHUNKS = 3
 DEPTH = 3
+LAG = 2
+REDUCE_DEPTH = 3
 
 
 def left_lanes():
@@ -117,12 +119,13 @@
     micros, block, local_pairs,
     captions, tokens, cotangent, biases, offsets, scaling, centring, lifting, settling, stretch, translate,
     own_proj, own_comb, own_exp, own_red,
-    a0_out, context_out, a1_out, hidden_out, dr2_out, du_out, dr1_out, dqkv_out, sums_out, results_out,
-    both, own_vectors, joint, mixing, expand, reduce, pieces, other_vectors, vectors, results,
+    a0_hbm, context_hbm, a1_hbm, hidden_hbm, dr2_hbm, du_hbm, dr1_hbm, dqkv_hbm, sums_out, results_out, last_out,
+    both, own_vectors, joint, mixing, expand, reduce, pieces, unpacked, other_vectors, vectors, results,
     slots, outgoing, qkv_keep, prob_keep, n1_keep, r1_keep, n2_keep, r2_keep, slope_keep,
     a_s, qkv_s, context_s, dqkv_s,
+    a0_ring, context_ring, a1_ring, hidden_ring, dr2_ring, du_ring, dr1_ring, dqkv_ring,
     send, recv, x_send, x_recv, z_send, z_recv, near_send, near_recv, far_send, far_recv,
-    own_sem, piece_send, piece_recv, vec_sem, result_send, result_recv, result_sem,
+    own_sem, piece_send, piece_recv, vec_sem, result_send, result_recv, result_sem, ring_sem,
 ):
     pipe, dp, layer, half, across_x, across_y, core, other_core = place()
     step = pl.program_id(0)
@@ -175,8 +178,17 @@
             def _():
                 piece_copies[j].start()
 
-    def gathered(first, last):
+    def hand_on(k):
+        z_copy(k).wait_recv()
+        far_copy(k).start()
+
+    def arrived(first, last):
         for k in range(first, last):
+            near_copy(k).wait_recv()
+            far_copy(k).wait_recv()
+
+    def gather_most():
+        for k in range(n):
             x_copy(k).wait_recv()
             z_copy(k).start()
             near_copy(k).start()
@@ -185,15 +197,16 @@
                 x_copy(k + DEPTH).start()
             if k + DEPTH == n - 1:
                 send_pieces(1)
-        for k in range(first, last):
-            z_copy(k).wait_recv()
-            far_copy(k).start()
-        for k in range(first, last):
-            near_copy(k).wait_recv()
-            far_copy(k).wait_recv()
-
-    def rest_gathered():
-        gathered(ATTENTION_CHUNKS, n)
+            if k >= LAG:
+                hand_on(k - LAG)
+        arrived(0, ATTENTION_CHUNKS)
+        own_copies[0].wait()
+        own_copies[1].wait()
+
+    def gather_rest():
+        for k in range(n - LAG, n):
+            hand_on(k)
+        arrived(ATTENTION_CHUNKS, n)
         own_copies[2].wait()
         own_copies[3].wait()
 
@@ -224,36 +237,67 @@
             copy.start()
         own_result(index).start()
 
-    def from_pieces(index):
-        folded = micros // 2
-        for k in range(2):
-            @pl.when(index // folded == k)
+    def wait_results(index):
+        final = index == micros - 1
+        for j, copy in enumerate(result_copies(index)):
+            if not final:
+                copy.wait()
+                continue
+
+            @pl.when(layer == 1)
             def _():
-                at = pl.ds(pl.multiple_of((index - k * folded) * block, 16), block)
-                lanes = slice(k * QUARTER, (k + 1) * QUARTER)
-                a_s[...] = jnp.concatenate([pieces[i, at, lanes] for i in range(PIPE)], 1)
+                copy.wait_send()
+
+            @pl.when(relatives[j] // 2 == 1)
+            def _():
+                copy.wait_recv()
+
+        @pl.when((layer == 1) | (not final))
+        def _():
+            own_result(index).wait()
+
+    rings = [
+        (a0_ring, a0_hbm), (context_ring, context_hbm), (a1_ring, a1_hbm), (hidden_ring, hidden_hbm),
+        (dr2_ring, dr2_hbm), (du_ring, du_hbm), (dr1_ring, dr1_hbm), (dqkv_ring, dqkv_hbm),
+    ]
+
+    def ring_copy(which, index):
+        ring, target = rings[which]
+        return pltpu.make_async_copy(ring.at[index % 2], target.at[rows_of(index)], ring_sem.at[which, index])
+
+    def ring_slots(first, last, index):
+        @pl.when(index >= 2)
+        def _():
+            for which in range(first, last):
+                ring_copy(which, index - 2).wait()
+
+        return [rings[which][0].at[index % 2] for which in range(first, last)]
+
+    def ring_start(first, last, index):
+        for which in range(first, last):
+            ring_copy(which, index).start()
+
+    def unpack_pieces():
+        for copy in piece_copies:
+            copy.wait_recv()
+        unpacked[...] = pieces[...].reshape(D, rows).astype(F32).T.astype(BF)
 
     @pl.when(step == 0)
     def _():
         for copy in own_copies:
             copy.start()
-        fold = rows // 2
         for t, source in enumerate((tokens, cotangent)):
-            for h in range(2):
-                blocks = []
-                for k in range(2):
-                    first = h * rows + k * fold
-                    value = source[first : min(first + fold, source.shape[0]), :].astype(F32)
-                    if value.shape[0] < fold:
-                        value = jnp.concatenate([value, jnp.zeros((fold - value.shape[0], QUARTER), F32)], 0)
-                    blocks.append(value)
-                both[t, h] = jnp.concatenate(blocks, 1).astype(BF)
+            whole = source[...].astype(F32)
+            spare = jnp.zeros((QUARTER, 2 * rows - whole.shape[1]), F32)
+            both[t, 0] = whole[:, :rows].astype(BF)
+            both[t, 1] = jnp.concatenate([whole[:, rows:], spare], 1).astype(BF)
         for i, source in enumerate((biases, offsets, scaling, centring, lifting, settling, stretch, translate)):
             own_vectors[i : i + 1, : source.shape[1]] = source[...].astype(F32)
         own_piece.start()
         sums_out[...] = jnp.zeros_like(sums_out)
         greet([(across_x, dp), (across_y, dp), (diagonal, dp), (pipe, across_z), (pipe, other_core)])
         vec_copy.start()
+
         send_pieces(0)
         for k in range(DEPTH):
             x_copy(k).start()
@@ -267,27 +311,24 @@
                 vectors[i : i + 1, which * HALF : (which + 1) * HALF] = value[i : i + 1, :HALF]
             vectors[4:5, which * HIDDEN_HALF : (which + 1) * HIDDEN_HALF] = value[4:5, :]
         own_piece.wait()
+        gather_most()
+
+        @pl.when(layer == 1)
+        def _():
+            gather_rest()
+
+    @pl.when(((layer == 0) & (step < micros)) | ((layer == 1) & (step % 2 == 0)))
+    def _():
+        micro = (1 - layer) * step + layer * (step // 2)
+        a0_out, context_out, a1_out, hidden_out = ring_slots(0, 4, micro)
+
+        @pl.when((layer == 0) & (micro == 0))
+        def _():
+            unpack_pieces()
 
         @pl.when(layer == 0)
         def _():
-            for copy in piece_copies:
-                copy.wait_recv()
-
-        gathered(0, ATTENTION_CHUNKS)
-        own_copies[0].wait()
-        own_copies[1].wait()
-
-        @pl.when(layer == 1)
-        def _():
-            rest_gathered()
-
-    @pl.when(step < micros)
-    def _():
-        micro = step
-
-        @pl.when(layer == 0)
-        def _():
-            from_pieces(micro)
+            a_s[...] = unpacked[rows_of(micro), :]
 
         @pl.when(layer == 1)
         def _():
@@ -343,7 +384,7 @@
 
         @pl.when((micro == 0) & (layer == 0))
         def _():
-            rest_gathered()
+            gather_rest()
 
         residual = attended.astype(F32) + vectors[5:6, :D]
         for which in range(2):
@@ -369,22 +410,24 @@
         def _():
             share_result(micro, result)
 
+        ring_start(0, 4, micro)
+
     def add_sum(row, value):
         width = value.shape[1]
         sums_out[row : row + 1, :width] += column_sums(value)
 
-    @pl.when(step >= micros)
+    @pl.when(((layer == 0) & (step >= micros)) | ((layer == 1) & (step % 2 == 1)))
     def _():
-        micro = step - micros
+        micro = (1 - layer) * (step - micros) + layer * (step // 2)
+        dr2_out, du_out, dr1_out, dqkv_out = ring_slots(4, 8, micro)
 
         @pl.when((layer == 1) & (micro == 0))
         def _():
-            for copy in piece_copies:
-                copy.wait_recv()
+            unpack_pieces()
 
         @pl.when(layer == 1)
         def _():
-            from_pieces(micro)
+            a_s[...] = unpacked[rows_of(micro), :]
 
         @pl.when(layer == 0)
         def _():
@@ -465,17 +508,25 @@
             outgoing[micro] = result
             y_copy(micro).start()
 
-        @pl.when(layer == 0)
+        ring_start(4, 8, micro)
+
+        @pl.when((layer == 0) & (micro < micros - 1))
         def _():
             share_result(micro, result)
+
+        @pl.when((layer == 0) & (micro == micros - 1))
+        def _():
+            for i in range(PIPE):
+                last_out[i] = result[:, i * QUARTER : (i + 1) * QUARTER]
 
     @pl.when(step == 2 * micros - 1)
     def _():
         for index in range(micros):
             y_copy(index).wait_send()
-            own_result(index).wait()
-            for copy in result_copies(index):
-                copy.wait()
+            wait_results(index)
+        for index in range(max(micros - 2, 0), micros):
+            for which in range(8):
+                ring_copy(which, index).wait()
         for k in range(n):
             if k + DEPTH >= n:
                 x_copy(k).wait_send()
@@ -492,12 +543,6 @@
     vmem = pl.BlockSpec(memory_space=pltpu.VMEM)
     hbm = pl.BlockSpec(memory_space=pl.ANY)
 
-    def forward_rows(width):
-        return pl.BlockSpec((block, width), lambda s: (jnp.minimum(s, micros - 1), 0))
-
-    def backward_rows(width):
-        return pl.BlockSpec((block, width), lambda s: (jnp.maximum(s - micros, 0), 0))
-
     forward_widths = [D, D, D, FF]
     backward_widths = [D, FF, D, 3 * D]
     pairs = block // PAIR_ROWS
@@ -505,18 +550,21 @@
         functools.partial(layer_kernel, micros, block, captions.shape[0]),
         grid=(2 * micros,),
         out_shape=[jax.ShapeDtypeStruct((rows, w), BF) for w in forward_widths + backward_widths]
-        + [jax.ShapeDtypeStruct((8, FF), F32), jax.ShapeDtypeStruct((PIPE, rows, QUARTER), BF)],
+        + [
+            jax.ShapeDtypeStruct((8, FF), F32),
+            jax.ShapeDtypeStruct((PIPE, rows, QUARTER), BF),
+            jax.ShapeDtypeStruct((PIPE, block, QUARTER), BF),
+        ],
         in_specs=[pl.BlockSpec(memory_space=pltpu.SMEM)] + [vmem] * 10 + [hbm] * 4,
-        out_specs=[forward_rows(w) for w in forward_widths]
-        + [backward_rows(w) for w in backward_widths]
-        + [vmem, hbm],
+        out_specs=[hbm] * 8 + [vmem, hbm, vmem],
         scratch_shapes=[
-            pltpu.VMEM((2, 2, rows // 2, 2 * QUARTER), BF),
+            pltpu.VMEM((2, 2, QUARTER, rows), BF),
             pltpu.VMEM((8, HIDDEN_HALF), F32),
         ]
         + [pltpu.VMEM((2,) + shape, BF) for shape in WEIGHT_SHAPES]
         + [
-            pltpu.VMEM((PIPE, rows // 2, 2 * QUARTER), BF),
+            pltpu.VMEM((PIPE, QUARTER, rows), BF),
+            pltpu.VMEM((rows, D), BF),
             pltpu.VMEM((8, HIDDEN_HALF), F32),
             pltpu.VMEM((8, FF), F32),
             pltpu.VMEM((PIPE, rows, QUARTER), BF),
@@ -533,9 +581,9 @@
             pltpu.VMEM((block, 3 * D), F32),
             pltpu.VMEM((block, D), F32),
             pltpu.VMEM((block, 3 * D), F32),
-            pltpu.SemaphoreType.DMA((micros,)),
-            pltpu.SemaphoreType.DMA((micros,)),
         ]
+        + [pltpu.VMEM((2, block, w), BF) for w in forward_widths + backward_widths]
+        + [pltpu.SemaphoreType.DMA((micros,))] * 2
         + [pltpu.SemaphoreType.DMA((n,))] * 8
         + [
             pltpu.SemaphoreType.DMA((5,)),
@@ -545,6 +593,7 @@
             pltpu.SemaphoreType.DMA((3, micros)),
             pltpu.SemaphoreType.DMA((3, micros)),
             pltpu.SemaphoreType.DMA((micros,)),
+            pltpu.SemaphoreType.DMA((8, micros)),
         ],
         compiler_params=pltpu.CompilerParams(collective_id=1, has_side_effects=True, vmem_limit_bytes=VMEM_LIMIT),
         name="layer_passes",
@@ -556,41 +605,63 @@
 
 def weights_kernel(
     n_dp,
-    a0_in, dqkv_in, context_in, dr1_in, a1_in, du_in, hidden_in, dr2_in, sums,
-    g_proj, g_comb, g_exp, g_red, sums_out,
+    a0_in, dqkv_in, context_in, dr1_in, a1_in, du_in, hidden_in, dr2_in, sums, last,
+    g_proj, g_comb, g_exp, g_red, sums_out, last_out,
     b_proj, b_comb, b_exp, b_red,
     c_proj, c_comb, c_exp, c_red,
     x_proj, x_comb, x_exp, x_red,
+    p_proj, p_comb, p_exp, p_red,
     z_proj, z_comb, z_exp, z_red,
-    sums_core, sums_x, sums_z, sums_a, sums_b,
+    sums_core, sums_x, sums_z, sums_a, sums_b, sums_c,
     a0, dqkv, context, dr1, a1, du, hidden, dr2,
     core_send, core_recv, x_send, x_recv, z_send, z_recv,
-    small_send, small_recv, load_sem,
+    small_send, small_recv, load_sem, last_send, last_recv,
 ):
     pipe, dp, layer, half, across_x, across_y, core, other_core = place()
     n_z = n_dp // 2
     z = dp // 2
-    offsets = sorted(range(1, n_z), key=lambda off: -min(off, n_z - off)) + [0]
-    z_order = [(z + off) % n_z for off in offsets]
-    z_others = z_order[:-1]
+    near_z = z + 1 - 2 * (z % 2)
+    steps = n_z // 2
+    z_order = [(near_z + 2 * (step + 1)) % n_z for step in range(steps - 1)] + [near_z]
+    z_order += [(z + 2 * (step + 1)) % n_z for step in range(steps - 1)] + [z]
+    same_parity = z_order[steps:-1]
+    def hidden_lanes(h):
+        return pl.ds(pl.multiple_of(h * HIDDEN_HALF, 128), HIDDEN_HALF)
+
     loads = [
         pltpu.make_async_copy(source, target, load_sem.at[i])
         for i, (source, target) in enumerate((
-            (hidden_in, hidden), (dr2_in, dr2), (a1_in, a1), (du_in, du),
-            (a0_in, a0), (dqkv_in, dqkv), (context_in, context), (dr1_in, dr1),
+            (dr2_in, dr2),
+            (hidden_in.at[:, hidden_lanes(1 - half)], hidden.at[:, hidden_lanes(1 - half)]),
+            (hidden_in.at[:, hidden_lanes(half)], hidden.at[:, hidden_lanes(half)]),
+            (a1_in, a1), (du_in, du), (a0_in, a0), (dqkv_in, dqkv), (context_in, context), (dr1_in, dr1),
         ))
     ]
     for copy in loads:
         copy.start()
+    relatives = (across_x, across_y, (across_x + 2) % 4)
     greet(
-        [(across_x, dp), (pipe, other_core)]
-        + [(pipe, 2 * other + core) for other in z_others]
+        [(target, dp) for target in relatives] + [(pipe, other_core)]
+        + [(pipe, 2 * other + core) for other in [near_z] + same_parity]
     )
+
+    last_copies = [
+        remote(last.at[target], last_out.at[half], last_send.at[j], last_recv.at[j], (target, dp))
+        for j, target in enumerate(relatives)
+    ]
+    last_own = pltpu.make_async_copy(last.at[pipe], last_out.at[half], load_sem.at[9])
+
+    @pl.when(layer == 0)
+    def _():
+        for copy in last_copies:
+            copy.start()
+        last_own.start()
 
     mine = [b_red, b_exp, b_proj, b_comb]
     from_core = [c_red, c_exp, c_proj, c_comb]
     from_x = [x_red, x_exp, x_proj, x_comb]
-    from_z = [z_red, z_exp, z_proj, z_comb]
+    from_pair = [p_red, p_exp, p_proj, p_comb]
+    from_far = [z_red, z_exp, z_proj, z_comb]
     outs = [g_red, g_exp, g_proj, g_comb]
 
     def spread(target, tile, cast=BF):
@@ -599,12 +670,11 @@
             for c in range(2):
                 yield c, k, tile[(2 * k + c) * r : (2 * k + c + 1) * r].astype(cast)
 
-    def fill_red(h):
-        for part in range(HIDDEN_HALF // D):
-            lanes = pl.ds(pl.multiple_of(h * HIDDEN_HALF + part * D, 128), D)
-            shards_here = D // (2 * b_red.shape[3])
-            for c, k, rows in spread(b_red, dot_tn(hidden[:, lanes], dr2[...])):
-                b_red[c, h, part * shards_here + k] = rows
+    def fill_red(h, at):
+        width = 2 * b_red.shape[3]
+        lanes = pl.ds(pl.multiple_of(h * HIDDEN_HALF + at * width, 128), width)
+        for c, k, rows in spread(b_red, dot_tn(hidden[:, lanes], dr2[...])):
+            b_red[c, h, at] = rows
 
     def fill_exp(step, carry):
         i, h = step // 2, step % 2
@@ -628,12 +698,17 @@
             for c, k, rows in spread(b_comb, tile[h * HALF : (h + 1) * HALF]):
                 b_comb[c, h, k] = rows
 
-    def core_copy(a, which):
-        at = 1 - half if which == 0 else half
+    def core_copy(a, which, i):
+        h = 1 - half if which == 0 else half
+        at = z_order[i]
         return remote(
-            mine[a].at[1 - core, at], from_core[a].at[at], core_send.at[a, which], core_recv.at[a, which],
+            mine[a].at[1 - core, h, at], from_core[a].at[h, at], core_send.at[a, which, i], core_recv.at[a, which, i],
             (pipe, other_core),
         )
+
+    def send_core(a, which):
+        for i in range(n_z):
+            core_copy(a, which, i).start()
 
     def x_copy(k):
         a, i = chunks[k]
@@ -642,10 +717,16 @@
             (across_x, dp),
         )
 
-    def z_copy(a, i):
-        other = z_order[i]
+    def pair_copy(a, i):
         return remote(
-            mine[a].at[core, half, other], from_z[a].at[i], z_send.at[a, i], z_recv.at[a, i],
+            mine[a].at[core, half, z_order[i]], from_pair[a].at[i], z_send.at[a, i], z_recv.at[a, i],
+            (pipe, 2 * near_z + core),
+        )
+
+    def far_copy(a, i):
+        other = same_parity[i]
+        return remote(
+            mine[a].at[core, half, other], from_far[a].at[i], z_send.at[a, steps + i], z_recv.at[a, steps + i],
             (pipe, 2 * other + core),
         )
 
@@ -656,6 +737,7 @@
             return
         a, i = chunks[k]
         at = z_order[i]
+        core_copy(a, 0, i).wait_recv()
         total = mine[a][core, 1 - half, at].astype(F32) + from_core[a][1 - half, at].astype(F32)
         mine[a][core, 1 - half, at] = total.astype(BF)
         x_copy(k).start()
@@ -664,83 +746,108 @@
         a, i = chunks[k]
         at = z_order[i]
         x_copy(k).wait()
-        start_x(k + DEPTH)
-        if i == 0:
-            core_copy(a, 1).wait_recv()
+        start_x(k + REDUCE_DEPTH)
+        core_copy(a, 1, i).wait_recv()
         total = mine[a][core, half, at].astype(F32) + from_core[a][half, at].astype(F32) + from_x[a][at].astype(F32)
+        if i < steps:
+            mine[a][core, half, at] = total.astype(BF)
+            pair_copy(a, i).start()
+            return
+        pair_copy(a, i - steps).wait_recv()
+        total = total + from_pair[a][i - steps].astype(F32)
         if i < n_z - 1:
             mine[a][core, half, at] = total.astype(BF)
-            z_copy(a, i).start()
+            far_copy(a, i - steps).start()
         else:
             outs[a][...] = total
 
     def after_z(a):
         total = outs[a][...]
-        for i in range(n_z - 1):
-            z_copy(a, i).wait()
-            total = total + from_z[a][i].astype(F32)
+        for i in range(steps - 1):
+            far_copy(a, i).wait()
+            total = total + from_far[a][i].astype(F32)
         outs[a][...] = total
+        for i in range(steps):
+            pair_copy(a, i).wait_send()
 
     sums_copy_core = remote(sums, sums_core, small_send.at[0], small_recv.at[0], (pipe, other_core))
     sums_copy_x = remote(sums_a, sums_x, small_send.at[1], small_recv.at[1], (across_x, dp))
-    sums_copies_z = [
-        remote(sums_b, sums_z.at[i], small_send.at[2 + i], small_recv.at[2 + i], (pipe, 2 * other + core))
-        for i, other in enumerate(z_others)
+    sums_copy_pair = remote(
+        sums_b, sums_z.at[steps - 1], small_send.at[2], small_recv.at[2], (pipe, 2 * near_z + core)
+    )
+    sums_copies_far = [
+        remote(sums_c, sums_z.at[i], small_send.at[3 + i], small_recv.at[3 + i], (pipe, 2 * other + core))
+        for i, other in enumerate(same_parity)
     ]
 
     sums_copy_core.start()
     loads[0].wait()
     loads[1].wait()
-    fill_red(1 - half)
-    core_copy(0, 0).start()
-    fill_red(half)
-    core_copy(0, 1).start()
-    core_copy(0, 0).wait_recv()
-    for k in range(DEPTH):
-        start_x(k)
+    for i in range(n_z):
+        fill_red(1 - half, z_order[i])
+        core_copy(0, 0, i).start()
+        if 1 <= i <= REDUCE_DEPTH:
+            start_x(i - 1)
     loads[2].wait()
+    for i in range(n_z):
+        fill_red(half, z_order[i])
+        core_copy(0, 1, i).start()
     loads[3].wait()
+    loads[4].wait()
     lax.fori_loop(0, 2 * D // TILE, fill_exp, 0)
-    core_copy(1, 0).start()
-    core_copy(1, 1).start()
+    send_core(1, 0)
+    send_core(1, 1)
     sums_copy_core.wait()
     sums_a[...] = sums[...] + sums_core[...]
     sums_copy_x.start()
-    core_copy(1, 0).wait_recv()
     after_x(0)
-    loads[4].wait()
     loads[5].wait()
+    loads[6].wait()
     lax.fori_loop(0, 2, fill_proj, 0)
-    core_copy(2, 0).start()
-    core_copy(2, 1).start()
+    send_core(2, 0)
+    send_core(2, 1)
     after_x(1)
-    loads[6].wait()
     loads[7].wait()
+    loads[8].wait()
     fill_comb()
-    core_copy(3, 0).start()
-    core_copy(3, 1).start()
+    send_core(3, 0)
+    send_core(3, 1)
     sums_copy_x.wait()
     sums_b[...] = sums_a[...] + sums_x[...]
-    for copy in sums_copies_z:
-        copy.start()
-    core_copy(2, 0).wait_recv()
-    core_copy(3, 0).wait_recv()
+    sums_copy_pair.start()
     for k in range(2, len(chunks)):
         after_x(k)
+        if k == n_z:
+            sums_copy_pair.wait()
+            sums_c[...] = sums_b[...] + sums_z[steps - 1]
+            for copy in sums_copies_far:
+                copy.start()
         if k % n_z == n_z - 2 and k >= n_z:
             after_z(k // n_z - 1)
     after_z(3)
     for a in range(4):
         for which in range(2):
-            core_copy(a, which).wait_send()
-    total = sums_b[...]
-    for i in range(n_z - 1):
-        sums_copies_z[i].wait()
+            for i in range(n_z):
+                core_copy(a, which, i).wait_send()
+    total = sums_c[...]
+    for i in range(steps - 1):
+        sums_copies_far[i].wait()
         total = total + sums_z[i]
     sums_out[...] = total
 
-
-def weight_gradients(n_dp, a0, dqkv, context, dr1, a1, du, hidden, dr2, sums):
+    @pl.when(layer == 0)
+    def _():
+        for copy in last_copies:
+            copy.wait_send()
+        last_own.wait()
+
+    for j, source in enumerate(relatives):
+        @pl.when(source // 2 == 0)
+        def _():
+            last_copies[j].wait_recv()
+
+
+def weight_gradients(n_dp, a0, dqkv, context, dr1, a1, du, hidden, dr2, sums, last):
     vmem = pl.BlockSpec(memory_space=pltpu.VMEM)
     hbm = pl.BlockSpec(memory_space=pl.ANY)
     n_z = n_dp // 2
@@ -748,48 +855,55 @@
     return pl.pallas_call(
         functools.partial(weights_kernel, n_dp),
         out_shape=[jax.ShapeDtypeStruct(s, F32) for s in shapes]
-        + [jax.ShapeDtypeStruct(sums.shape, F32)],
-        in_specs=[hbm] * 8 + [vmem],
-        out_specs=[vmem] * 5,
+        + [jax.ShapeDtypeStruct(sums.shape, F32), jax.ShapeDtypeStruct((2,) + last.shape[1:], BF)],
+        in_specs=[hbm] * 8 + [vmem, hbm],
+        out_specs=[vmem] * 5 + [hbm],
         scratch_shapes=[pltpu.VMEM((2, 2, n_z) + s, BF) for s in shapes]
         + [pltpu.VMEM((2, n_z) + s, BF) for s in shapes]
         + [pltpu.VMEM((n_z,) + s, BF) for s in shapes]
-        + [pltpu.VMEM((n_z - 1,) + s, BF) for s in shapes]
+        + [pltpu.VMEM((n_z // 2,) + s, BF) for s in shapes]
+        + [pltpu.VMEM((max(n_z // 2 - 1, 1),) + s, BF) for s in shapes]
         + [
             pltpu.VMEM(sums.shape, F32),
             pltpu.VMEM(sums.shape, F32),
-            pltpu.VMEM((n_z - 1,) + sums.shape, F32),
+            pltpu.VMEM((n_z // 2,) + sums.shape, F32),
+            pltpu.VMEM(sums.shape, F32),
             pltpu.VMEM(sums.shape, F32),
             pltpu.VMEM(sums.shape, F32),
         ]
         + [pltpu.VMEM(v.shape, BF) for v in (a0, dqkv, context, dr1, a1, du, hidden, dr2)]
         + [
-            pltpu.SemaphoreType.DMA((4, 2)),
-            pltpu.SemaphoreType.DMA((4, 2)),
+            pltpu.SemaphoreType.DMA((4, 2, n_z)),
+            pltpu.SemaphoreType.DMA((4, 2, n_z)),
             pltpu.SemaphoreType.DMA((4, n_z)),
             pltpu.SemaphoreType.DMA((4, n_z)),
             pltpu.SemaphoreType.DMA((4, n_z - 1)),
             pltpu.SemaphoreType.DMA((4, n_z - 1)),
             pltpu.SemaphoreType.DMA((n_z + 1,)),
             pltpu.SemaphoreType.DMA((n_z + 1,)),
-            pltpu.SemaphoreType.DMA((8,)),
+            pltpu.SemaphoreType.DMA((10,)),
+            pltpu.SemaphoreType.DMA((3,)),
+            pltpu.SemaphoreType.DMA((3,)),
         ],
         compiler_params=pltpu.CompilerParams(collective_id=3, has_side_effects=True, vmem_limit_bytes=VMEM_LIMIT),
         name="weight_gradients",
-    )(a0, dqkv, context, dr1, a1, du, hidden, dr2, sums)
-
-
-def finish_kernel(n_dp, small, results, *refs):
+    )(a0, dqkv, context, dr1, a1, du, hidden, dr2, sums, last)
+
+
+def finish_kernel(n_dp, small, results, last, *refs):
     pipe, dp, layer, half, across_x, across_y, core, other_core = place()
     sources, encoded, tokens_grad, outs, parts = refs[:4], refs[4], refs[5], refs[6:10], refs[10:]
     for source, out in zip(sources, outs):
         out[0] = source[...]
-    rows = results.shape[1]
-    spare = encoded.shape[0] - rows
-    tokens_grad[:rows] = results[0].astype(F32)
-    tokens_grad[rows:] = results[1, :spare].astype(F32)
-    encoded[:rows] = results[2]
-    encoded[rows:] = results[3, :spare]
+    for first, out in ((0, tokens_grad), (2, encoded)):
+        parts_of = []
+        for i in (first, first + 1):
+            if first == 0:
+                parts_of += [results[i, : results.shape[1] - last.shape[1], :], last[i]]
+            else:
+                parts_of.append(results[i])
+        value = jnp.concatenate(parts_of, 0).astype(F32).T
+        out[...] = value[:, : out.shape[1]].astype(out.dtype)
     for row, out in enumerate(parts):
         count = out.shape[1]
         width = n_dp * count
@@ -805,25 +919,25 @@
         out[...] = found
 
 
-def finish(n_dp, local_rows, small, results, grads):
+def finish(n_dp, local_rows, small, results, last, grads):
     vmem = pl.BlockSpec(memory_space=pltpu.VMEM)
     widths = [D, HALF, HALF, HALF, HIDDEN_HALF, HALF, HALF, HALF]
     return pl.pallas_call(
         functools.partial(finish_kernel, n_dp),
         out_shape=[
-            jax.ShapeDtypeStruct((local_rows, QUARTER), BF),
-            jax.ShapeDtypeStruct((local_rows, QUARTER), F32),
+            jax.ShapeDtypeStruct((QUARTER, local_rows), BF),
+            jax.ShapeDtypeStruct((QUARTER, local_rows), F32),
         ]
         + [jax.ShapeDtypeStruct((1,) + g.shape, F32) for g in grads]
         + [jax.ShapeDtypeStruct((1, w // n_dp), F32) for w in widths],
-        in_specs=[vmem] * 6,
+        in_specs=[vmem] * 7,
         out_specs=[vmem] * 14,
         compiler_params=pltpu.CompilerParams(vmem_limit_bytes=VMEM_LIMIT),
         name="finish",
-    )(small, results, *grads)
-
-
-def weight_gradients_by_scatter(n_dp, a0, dqkv, context, dr1, a1, du, hidden, dr2, sums):
+    )(small, results, last, *grads)
+
+
+def weight_gradients_by_scatter(n_dp, a0, dqkv, context, dr1, a1, du, hidden, dr2, sums, last):
     half = lax.axis_index("pipe") % 2
     halves = (
         dot_tn(a0, dqkv).reshape(D, 2, 3 * HALF).transpose(1, 0, 2),
@@ -839,7 +953,8 @@
         send = lax.dynamic_index_in_dim(part, 1 - half, 0, keepdims=False)
         found.append(keep + lax.ppermute(send.astype(BF), "pipe", swap).astype(F32))
     small = lax.psum(sums, "dp")
-    return found + [small + lax.ppermute(small, "pipe", swap)]
+    received = lax.all_to_all(last, "pipe", 0, 0, tiled=False)
+    return found + [small + lax.ppermute(small, "pipe", swap), received[:2]]
 
 
 def shards(
@@ -854,14 +969,14 @@
     micros = pairs // 2
     owned = (projection[0], combiner[0], expansion[0], reduction[0])
     small = (biases, offsets, scaling, centring, lifting, settling, stretch, translate)
-    *kept, results = layer_passes(micros, block, captions, small, tokens, cotangent, owned)
+    *kept, results, last = layer_passes(micros, block, captions, small, tokens.T, cotangent.T, owned)
     a0, context, a1, hidden, dr2, du, dr1, dqkv, sums = kept
     whole_tiles = HALF % (16 * n_dp) == 0
     collect = weight_gradients if whole_tiles else weight_gradients_by_scatter
-    *grads, sums = collect(n_dp, a0, dqkv, context, dr1, a1, du, hidden, dr2, sums)
-    encoded, tokens_grad, g_proj, g_comb, g_exp, g_red, *parts = finish(n_dp, local_rows, sums, results, grads)
+    *grads, sums, last = collect(n_dp, a0, dqkv, context, dr1, a1, du, hidden, dr2, sums, last)
+    encoded, tokens_grad, g_proj, g_comb, g_exp, g_red, *parts = finish(n_dp, local_rows, sums, results, last, grads)
     return (
-        encoded, tokens_grad, g_proj, parts[0], g_comb, parts[1], parts[2], parts[3],
+        encoded.T, tokens_grad.T, g_proj, parts[0], g_comb, parts[1], parts[2], parts[3],
         g_exp, parts[4], g_red, parts[5], parts[6], parts[7],
     )
 

time: 275 us -> 243 us (0.88)
  Pallas kernels: 266 us -> 242 us
  local copies, waits for them, and re-layouts: 8.74 us -> 0 us
    pallas_call x1, Pallas kernels: 154 us -> 140 us  [layer_passes(): pl.pallas_call(functools.partial(layer_kernel, micros, block, captions.sh...]
    pallas_call x1, Pallas kernels: 107 us -> 95.7 us  [weight_gradients(): pl.pallas_call(functools.partial(weights_kernel, n_dp), out_shape=[jax.Sh...]
    unnamed x6 -> x0, local copies, waits for them, and re-layouts: 8.74 us -> none
where the time goes in v4:
time: 243 us; the launch traced here: 242 us
  Pallas kernels  242 us (100%)
    pallas_call x1, Pallas kernels, layer_passes(): pl.pallas_call(functools.partial(layer_kernel, micros, block, captions.sh...  140 us
    pallas_call x1, Pallas kernels, weight_gradients(): pl.pallas_call(functools.partial(weights_kernel, n_dp), out_shape=[jax.Sh...  95.7 us
    pallas_call x1, Pallas kernels, finish(): pl.pallas_call(functools.partial(finish_kernel, n_dp), out_shape=[jax.Sha...  5.59 us

profile of v4, /device:TPU:0, one launch (start us, length us, event | category | flops | bytes accessed | tf_op | source)
XLA Modules:
  0.0 242.3 jit_solution(9702950937974158842)
XLA Ops:
  0.7 140.2 %layer_passes.1 = (bf16[832,768]{1,0:T(8,128)(2,1)}, bf16[832,768]{1,0:T(8,128)(2,1)}, bf16[832,768]{1,0:T(8,128)(2,1)}, bf16[832,3072]{1,0:T(8,128)(2,1)}, bf16...) custom-call(s32[15]{0:T(128)} %captions.1, ...), custom_call_target="tpu_custom_call" | custom-call | tf_op jit(solution)/shard_map/layer_passes/pallas_call | solution.py:549
  140.8 95.7 %weight_gradients.1 = (f32[96,1152]{1,0:T(8,128)}, f32[48,768]{1,0:T(8,128)}, f32[96,1536]{1,0:T(8,128)}, f32[192,768]{1,0:T(8,128)}, f32[8,3072]{1,0:T(8,128)}, /*index=5*/bf16[2,208,192]{2,1,0:T(8,128)(2,1)}) custom-call(bf16[832,768]{1,0:T(8,128)(2,1)} %get-tuple-element.45.a0_in, bf16[832,2304]{1,0:T(8,128)(2,1)} %get-tuple-element.46.dqkv_in, ...), custom_call_target="tpu_custom_call" | custom-call | tf_op jit(solution)/shard_map/weight_gradients/pallas_call | solution.py:855
  236.6 5.6 %finish.1 = (bf16[192,1560]{1,0:T(8,128)(2,1)}, f32[192,1560]{1,0:T(8,128)}, f32[1,96,1152]{2,1,0:T(8,128)}, f32[1,48,768]{2,1,0:T(8,128)}, f32[1,96,1536]{2,1,0...) custom-call(f32[8,3072]{1,0:T(8,128)} %get-tuple-element.55.small, ...), custom_call_target="tpu_custom_call" | custom-call | tf_op jit(solution)/shard_map/finish/pallas_call | solution.py:925

commit v5 on v4

--- a/solution.py
+++ b/solution.py
@@ -76,9 +76,11 @@
 WEIGHT_SHAPES = [(D, 3 * HALF), (HALF, D), (D, HIDDEN_HALF), (HIDDEN_HALF, D)]
 CHUNKS = [(0, 0, 96), (0, 96, 96), (1, 0, 96)] + [(2, i*48, 48) for i in range(4)] + [(3, i*96, 96) for i in range(4)]
 ATTENTION_CHUNKS = 3
+FIRST_LANES = 256
 DEPTH = 3
 LAG = 2
 REDUCE_DEPTH = 3
+LOW_AT = (4, 7)
 
 
 def left_lanes():
@@ -164,19 +166,25 @@
 
     own_copies = [pltpu.make_async_copy(owned[i], held[i].at[half], own_sem.at[i]) for i in range(4)]
     own_piece = pltpu.make_async_copy(both.at[layer, half], pieces.at[pipe], own_sem.at[4])
+    lanes_held = both.shape[3]
+    lanes_of = (pl.ds(0, FIRST_LANES), pl.ds(FIRST_LANES, lanes_held - FIRST_LANES))
     vec_copy = remote(own_vectors, other_vectors, vec_sem.at[0], vec_sem.at[1], (across_x, dp))
     piece_copies = [
-        remote(
-            both.at[target // 2, target % 2], pieces.at[pipe], piece_send.at[j], piece_recv.at[j], (target, dp)
-        )
-        for j, target in enumerate(relatives)
+        [
+            remote(
+                both.at[target // 2, target % 2, :, lanes], pieces.at[pipe, :, lanes],
+                piece_send.at[part, j], piece_recv.at[part, j], (target, dp),
+            )
+            for j, target in enumerate(relatives)
+        ]
+        for part, lanes in enumerate(lanes_of)
     ]
 
-    def send_pieces(to_layer):
+    def send_pieces(to_layer, part):
         for j, target in enumerate(relatives):
             @pl.when(target // 2 == to_layer)
             def _():
-                piece_copies[j].start()
+                piece_copies[part][j].start()
 
     def hand_on(k):
         z_copy(k).wait_recv()
@@ -196,7 +204,9 @@
                 x_copy(k).wait_send()
                 x_copy(k + DEPTH).start()
             if k + DEPTH == n - 1:
-                send_pieces(1)
+                send_pieces(0, 1)
+                send_pieces(1, 0)
+                send_pieces(1, 1)
             if k >= LAG:
                 hand_on(k - LAG)
         arrived(0, ATTENTION_CHUNKS)
@@ -277,10 +287,12 @@
         for which in range(first, last):
             ring_copy(which, index).start()
 
-    def unpack_pieces():
-        for copy in piece_copies:
+    def unpack_pieces(part):
+        for copy in piece_copies[part]:
             copy.wait_recv()
-        unpacked[...] = pieces[...].reshape(D, rows).astype(F32).T.astype(BF)
+        at = lanes_of[part]
+        value = pieces[:, :, at.start : at.start + at.size].reshape(D, at.size)
+        unpacked[at.start : at.start + at.size, :] = value.astype(F32).T.astype(BF)
 
     @pl.when(step == 0)
     def _():
@@ -288,9 +300,10 @@
             copy.start()
         for t, source in enumerate((tokens, cotangent)):
             whole = source[...].astype(F32)
-            spare = jnp.zeros((QUARTER, 2 * rows - whole.shape[1]), F32)
-            both[t, 0] = whole[:, :rows].astype(BF)
-            both[t, 1] = jnp.concatenate([whole[:, rows:], spare], 1).astype(BF)
+            for h in range(2):
+                value = whole[:, h * rows : (h + 1) * rows]
+                spare = jnp.zeros((QUARTER, lanes_held - value.shape[1]), F32)
+                both[t, h] = jnp.concatenate([value, spare], 1).astype(BF)
         for i, source in enumerate((biases, offsets, scaling, centring, lifting, settling, stretch, translate)):
             own_vectors[i : i + 1, : source.shape[1]] = source[...].astype(F32)
         own_piece.start()
@@ -298,7 +311,7 @@
         greet([(across_x, dp), (across_y, dp), (diagonal, dp), (pipe, across_z), (pipe, other_core)])
         vec_copy.start()
 
-        send_pieces(0)
+        send_pieces(0, 0)
         for k in range(DEPTH):
             x_copy(k).start()
         vec_copy.wait_recv()
@@ -322,9 +335,10 @@
         micro = (1 - layer) * step + layer * (step // 2)
         a0_out, context_out, a1_out, hidden_out = ring_slots(0, 4, micro)
 
-        @pl.when((layer == 0) & (micro == 0))
-        def _():
-            unpack_pieces()
+        for part in range(2):
+            @pl.when((layer == 0) & (micro == part))
+            def _():
+                unpack_pieces(part)
 
         @pl.when(layer == 0)
         def _():
@@ -423,7 +437,8 @@
 
         @pl.when((layer == 1) & (micro == 0))
         def _():
-            unpack_pieces()
+            unpack_pieces(0)
+            unpack_pieces(1)
 
         @pl.when(layer == 1)
         def _():
@@ -533,13 +548,14 @@
             z_copy(k).wait_send()
             near_copy(k).wait_send()
             far_copy(k).wait_send()
-        for copy in piece_copies + [vec_copy]:
+        for copy in piece_copies[0] + piece_copies[1] + [vec_copy]:
             copy.wait_send()
 
 
 def layer_passes(micros, block, captions, small, tokens, cotangent, owned):
     rows = micros * block
     n = len(CHUNKS)
+    lanes_held = (rows + 127) // 128 * 128
     vmem = pl.BlockSpec(memory_space=pltpu.VMEM)
     hbm = pl.BlockSpec(memory_space=pl.ANY)
 
@@ -558,13 +574,13 @@
         in_specs=[pl.BlockSpec(memory_space=pltpu.SMEM)] + [vmem] * 10 + [hbm] * 4,
         out_specs=[hbm] * 8 + [vmem, hbm, vmem],
         scratch_shapes=[
-            pltpu.VMEM((2, 2, QUARTER, rows), BF),
+            pltpu.VMEM((2, 2, QUARTER, lanes_held), BF),
             pltpu.VMEM((8, HIDDEN_HALF), F32),
         ]
         + [pltpu.VMEM((2,) + shape, BF) for shape in WEIGHT_SHAPES]
         + [
-            pltpu.VMEM((PIPE, QUARTER, rows), BF),
-            pltpu.VMEM((rows, D), BF),
+            pltpu.VMEM((PIPE, QUARTER, lanes_held), BF),
+            pltpu.VMEM((lanes_held, D), BF),
             pltpu.VMEM((8, HIDDEN_HALF), F32),
             pltpu.VMEM((8, FF), F32),
             pltpu.VMEM((PIPE, rows, QUARTER), BF),
@@ -587,8 +603,8 @@
         + [pltpu.SemaphoreType.DMA((n,))] * 8
         + [
             pltpu.SemaphoreType.DMA((5,)),
-            pltpu.SemaphoreType.DMA((3,)),
-            pltpu.SemaphoreType.DMA((3,)),
+            pltpu.SemaphoreType.DMA((2, 3)),
+            pltpu.SemaphoreType.DMA((2, 3)),
             pltpu.SemaphoreType.DMA((2,)),
             pltpu.SemaphoreType.DMA((3, micros)),
             pltpu.SemaphoreType.DMA((3, micros)),
@@ -613,9 +629,10 @@
     p_proj, p_comb, p_exp, p_red,
     z_proj, z_comb, z_exp, z_red,
     sums_core, sums_x, sums_z, sums_a, sums_b, sums_c,
+    low_from_pair, low_from_far, low_from_x, low_own,
     a0, dqkv, context, dr1, a1, du, hidden, dr2,
     core_send, core_recv, x_send, x_recv, z_send, z_recv,
-    small_send, small_recv, load_sem, last_send, last_recv,
+    small_send, small_recv, load_sem, last_send, last_recv, low_send, low_recv,
 ):
     pipe, dp, layer, half, across_x, across_y, core, other_core = place()
     n_z = n_dp // 2
@@ -698,12 +715,18 @@
             for c, k, rows in spread(b_comb, tile[h * HALF : (h + 1) * HALF]):
                 b_comb[c, h, k] = rows
 
+    low = b_red.shape[3] // 32 * 16
+    low_rows = pl.ds(0, low)
+    rows_of = [pl.ds(low, b_red.shape[3] - low)] + [pl.ds(0, b.shape[3]) for b in mine[1:]]
+
+    def half_of(which):
+        return 1 - half if which == 0 else half
+
     def core_copy(a, which, i):
-        h = 1 - half if which == 0 else half
-        at = z_order[i]
+        h, at = half_of(which), z_order[i]
         return remote(
-            mine[a].at[1 - core, h, at], from_core[a].at[h, at], core_send.at[a, which, i], core_recv.at[a, which, i],
-            (pipe, other_core),
+            mine[a].at[1 - core, h, at, rows_of[a]], from_core[a].at[h, at, rows_of[a]],
+            core_send.at[a, which, i], core_recv.at[a, which, i], (pipe, other_core),
         )
 
     def send_core(a, which):
@@ -712,22 +735,23 @@
 
     def x_copy(k):
         a, i = chunks[k]
+        at = z_order[i]
         return remote(
-            mine[a].at[core, 1 - half, z_order[i]], from_x[a].at[z_order[i]], x_send.at[a, i], x_recv.at[a, i],
-            (across_x, dp),
+            mine[a].at[core, 1 - half, at, rows_of[a]], from_x[a].at[at, rows_of[a]],
+            x_send.at[a, i], x_recv.at[a, i], (across_x, dp),
         )
 
     def pair_copy(a, i):
         return remote(
-            mine[a].at[core, half, z_order[i]], from_pair[a].at[i], z_send.at[a, i], z_recv.at[a, i],
-            (pipe, 2 * near_z + core),
+            mine[a].at[core, half, z_order[i], rows_of[a]], from_pair[a].at[i, rows_of[a]],
+            z_send.at[a, i], z_recv.at[a, i], (pipe, 2 * near_z + core),
         )
 
     def far_copy(a, i):
         other = same_parity[i]
         return remote(
-            mine[a].at[core, half, other], from_far[a].at[i], z_send.at[a, steps + i], z_recv.at[a, steps + i],
-            (pipe, 2 * other + core),
+            mine[a].at[core, half, other, rows_of[a]], from_far[a].at[i, rows_of[a]],
+            z_send.at[a, steps + i], z_recv.at[a, steps + i], (pipe, 2 * other + core),
         )
 
     chunks = [(a, i) for a in range(4) for i in range(n_z)]
@@ -736,39 +760,112 @@
         if k >= len(chunks):
             return
         a, i = chunks[k]
-        at = z_order[i]
+        at, rows = z_order[i], rows_of[a]
         core_copy(a, 0, i).wait_recv()
-        total = mine[a][core, 1 - half, at].astype(F32) + from_core[a][1 - half, at].astype(F32)
-        mine[a][core, 1 - half, at] = total.astype(BF)
+        total = mine[a][core, 1 - half, at, rows, :].astype(F32) + from_core[a][1 - half, at, rows, :].astype(F32)
+        mine[a][core, 1 - half, at, rows, :] = total.astype(BF)
         x_copy(k).start()
 
     def after_x(k):
         a, i = chunks[k]
-        at = z_order[i]
+        at, rows = z_order[i], rows_of[a]
         x_copy(k).wait()
         start_x(k + REDUCE_DEPTH)
         core_copy(a, 1, i).wait_recv()
-        total = mine[a][core, half, at].astype(F32) + from_core[a][half, at].astype(F32) + from_x[a][at].astype(F32)
+        total = mine[a][core, half, at, rows, :].astype(F32) + from_core[a][half, at, rows, :].astype(F32)
+        total = total + from_x[a][at, rows, :].astype(F32)
         if i < steps:
-            mine[a][core, half, at] = total.astype(BF)
+            mine[a][core, half, at, rows, :] = total.astype(BF)
             pair_copy(a, i).start()
             return
         pair_copy(a, i - steps).wait_recv()
-        total = total + from_pair[a][i - steps].astype(F32)
+        total = total + from_pair[a][i - steps, rows, :].astype(F32)
         if i < n_z - 1:
-            mine[a][core, half, at] = total.astype(BF)
+            mine[a][core, half, at, rows, :] = total.astype(BF)
             far_copy(a, i - steps).start()
         else:
-            outs[a][...] = total
+            outs[a][rows, :] = total
 
     def after_z(a):
-        total = outs[a][...]
+        rows = rows_of[a]
+        total = outs[a][rows, :]
         for i in range(steps - 1):
             far_copy(a, i).wait()
-            total = total + from_far[a][i].astype(F32)
-        outs[a][...] = total
+            total = total + from_far[a][i, rows, :].astype(F32)
+        outs[a][rows, :] = total
         for i in range(steps):
             pair_copy(a, i).wait_send()
+
+    def low_core(which, i):
+        h, at = half_of(which), z_order[i]
+        return remote(
+            b_red.at[1 - core, h, at, low_rows], c_red.at[h, at, low_rows],
+            low_send.at[which, i], low_recv.at[which, i], (pipe, other_core),
+        )
+
+    def low_pair(which, i):
+        return remote(
+            b_red.at[core, half_of(which), z_order[i], low_rows], low_from_pair.at[which, i],
+            low_send.at[2 + which, i], low_recv.at[2 + which, i], (pipe, 2 * near_z + core),
+        )
+
+    def low_far(which, i):
+        other = same_parity[i]
+        return remote(
+            b_red.at[core, half_of(which), other, low_rows], low_from_far.at[which, i],
+            low_send.at[2 + which, steps + i], low_recv.at[2 + which, steps + i], (pipe, 2 * other + core),
+        )
+
+    low_x = remote(
+        b_red.at[core, 1 - half, z, low_rows], low_from_x,
+        low_send.at[2, n_z - 1], low_recv.at[2, n_z - 1], (across_x, dp),
+    )
+
+    def low_sum(which, i):
+        h, at = half_of(which), z_order[i]
+        low_core(which, i).wait_recv()
+        return b_red[core, h, at, low_rows, :].astype(F32) + c_red[h, at, low_rows, :].astype(F32)
+
+    def low_to_pair():
+        for which in range(2):
+            for i in range(steps):
+                b_red[core, half_of(which), z_order[i], low_rows, :] = low_sum(which, i).astype(BF)
+                low_pair(which, i).start()
+
+    def low_to_far():
+        for which in range(2):
+            for i in range(steps, n_z):
+                total = low_sum(which, i)
+                low_pair(which, i - steps).wait_recv()
+                total = total + low_from_pair[which, i - steps].astype(F32)
+                if i < n_z - 1:
+                    b_red[core, half_of(which), z_order[i], low_rows, :] = total.astype(BF)
+                    low_far(which, i - steps).start()
+                else:
+                    low_own[which] = total
+
+    def low_to_x():
+        for which in range(2):
+            total = low_own[which]
+            for i in range(steps - 1):
+                low_far(which, i).wait_recv()
+                total = total + low_from_far[which, i].astype(F32)
+            if which == 0:
+                b_red[core, 1 - half, z, low_rows, :] = total.astype(BF)
+                low_x.start()
+            else:
+                g_red[low_rows, :] = total
+
+    def low_done():
+        low_x.wait()
+        g_red[low_rows, :] = g_red[low_rows, :] + low_from_x[...].astype(F32)
+        for which in range(2):
+            for i in range(n_z):
+                low_core(which, i).wait_send()
+            for i in range(steps):
+                low_pair(which, i).wait_send()
+            for i in range(steps - 1):
+                low_far(which, i).wait_send()
 
     sums_copy_core = remote(sums, sums_core, small_send.at[0], small_recv.at[0], (pipe, other_core))
     sums_copy_x = remote(sums_a, sums_x, small_send.at[1], small_recv.at[1], (across_x, dp))
@@ -786,12 +883,15 @@
     for i in range(n_z):
         fill_red(1 - half, z_order[i])
         core_copy(0, 0, i).start()
+        low_core(0, i).start()
         if 1 <= i <= REDUCE_DEPTH:
             start_x(i - 1)
     loads[2].wait()
     for i in range(n_z):
         fill_red(half, z_order[i])
+        low_core(1, i).start()
         core_copy(0, 1, i).start()
+    low_to_pair()
     loads[3].wait()
     loads[4].wait()
     lax.fori_loop(0, 2 * D // TILE, fill_exp, 0)
@@ -801,12 +901,13 @@
     sums_a[...] = sums[...] + sums_core[...]
     sums_copy_x.start()
     after_x(0)
+    after_x(1)
     loads[5].wait()
     loads[6].wait()
     lax.fori_loop(0, 2, fill_proj, 0)
     send_core(2, 0)
     send_core(2, 1)
-    after_x(1)
+    after_x(2)
     loads[7].wait()
     loads[8].wait()
     fill_comb()
@@ -815,8 +916,12 @@
     sums_copy_x.wait()
     sums_b[...] = sums_a[...] + sums_x[...]
     sums_copy_pair.start()
-    for k in range(2, len(chunks)):
+    for k in range(3, len(chunks)):
         after_x(k)
+        if k == LOW_AT[0]:
+            low_to_far()
+        if k == LOW_AT[1]:
+            low_to_x()
         if k == n_z:
             sums_copy_pair.wait()
             sums_c[...] = sums_b[...] + sums_z[steps - 1]
@@ -824,6 +929,7 @@
                 copy.start()
         if k % n_z == n_z - 2 and k >= n_z:
             after_z(k // n_z - 1)
+    low_done()
     after_z(3)
     for a in range(4):
         for which in range(2):
@@ -851,6 +957,7 @@
     vmem = pl.BlockSpec(memory_space=pltpu.VMEM)
     hbm = pl.BlockSpec(memory_space=pl.ANY)
     n_z = n_dp // 2
+    low = HIDDEN_HALF // n_dp // 32 * 16
     shapes = [(D // n_dp, 3 * HALF), (HALF // n_dp, D), (D // n_dp, HIDDEN_HALF), (HIDDEN_HALF // n_dp, D)]
     return pl.pallas_call(
         functools.partial(weights_kernel, n_dp),
@@ -870,6 +977,10 @@
             pltpu.VMEM(sums.shape, F32),
             pltpu.VMEM(sums.shape, F32),
             pltpu.VMEM(sums.shape, F32),
+            pltpu.VMEM((2, n_z // 2, low, D), BF),
+            pltpu.VMEM((2, max(n_z // 2 - 1, 1), low, D), BF),
+            pltpu.VMEM((low, D), BF),
+            pltpu.VMEM((2, low, D), F32),
         ]
         + [pltpu.VMEM(v.shape, BF) for v in (a0, dqkv, context, dr1, a1, du, hidden, dr2)]
         + [
@@ -884,6 +995,8 @@
             pltpu.SemaphoreType.DMA((10,)),
             pltpu.SemaphoreType.DMA((3,)),
             pltpu.SemaphoreType.DMA((3,)),
+            pltpu.SemaphoreType.DMA((4, n_z)),
+            pltpu.SemaphoreType.DMA((4, n_z)),
         ],
         compiler_params=pltpu.CompilerParams(collective_id=3, has_side_effects=True, vmem_limit_bytes=VMEM_LIMIT),
         name="weight_gradients",

time: 243 us -> 235 us (0.967)
  Pallas kernels: 242 us -> 234 us
    pallas_call x1, Pallas kernels: 95.7 us -> 91.1 us  [weight_gradients(): pl.pallas_call(functools.partial(weights_kernel, n_dp), out_shape=[jax.Sh...]
    pallas_call x1, Pallas kernels: 140 us -> 137 us  [layer_passes(): pl.pallas_call(functools.partial(layer_kernel, micros, block, captions.sh...]
where the time goes in v5:
time: 235 us; the launch traced here: 234 us
  Pallas kernels  234 us (100%)
    pallas_call x1, Pallas kernels, layer_passes(): pl.pallas_call(functools.partial(layer_kernel, micros, block, captions.sh...  137 us
    pallas_call x1, Pallas kernels, weight_gradients(): pl.pallas_call(functools.partial(weights_kernel, n_dp), out_shape=[jax.Sh...  91.1 us
    pallas_call x1, Pallas kernels, finish(): pl.pallas_call(functools.partial(finish_kernel, n_dp), out_shape=[jax.Sha...  5.59 us

profile of v5, /device:TPU:0, one launch (start us, length us, event | category | flops | bytes accessed | tf_op | source)
XLA Modules:
  0.0 234.4 jit_solution(3043861272399012804)
XLA Ops:
  0.7 136.9 %layer_passes.1 = (bf16[832,768]{1,0:T(8,128)(2,1)}, bf16[832,768]{1,0:T(8,128)(2,1)}, bf16[832,768]{1,0:T(8,128)(2,1)}, bf16[832,3072]{1,0:T(8,128)(2,1)}, bf16...) custom-call(s32[15]{0:T(128)} %captions.1, ...), custom_call_target="tpu_custom_call" | custom-call | tf_op jit(solution)/shard_map/layer_passes/pallas_call | solution.py:565
  137.5 91.1 %weight_gradients.1 = (f32[96,1152]{1,0:T(8,128)}, f32[48,768]{1,0:T(8,128)}, f32[96,1536]{1,0:T(8,128)}, f32[192,768]{1,0:T(8,128)}, f32[8,3072]{1,0:T(8,128)}, /*index=5*/bf16[2,208,192]{2,1,0:T(8,128)(2,1)}) custom-call(bf16[832,768]{1,0:T(8,128)(2,1)} %get-tuple-element.45.a0_in, bf16[832,2304]{1,0:T(8,128)(2,1)} %get-tuple-element.46.dqkv_in, ...), custom_call_target="tpu_custom_call" | custom-call | tf_op jit(solution)/shard_map/weight_gradients/pallas_call | solution.py:962
  228.6 5.6 %finish.1 = (bf16[192,1560]{1,0:T(8,128)(2,1)}, f32[192,1560]{1,0:T(8,128)}, f32[1,96,1152]{2,1,0:T(8,128)}, f32[1,48,768]{2,1,0:T(8,128)}, f32[1,96,1536]{2,1,0...) custom-call(f32[8,3072]{1,0:T(8,128)} %get-tuple-element.55.small, ...), custom_call_target="tpu_custom_call" | custom-call | tf_op jit(solution)/shard_map/finish/pallas_call | solution.py:1038

commit v6 on v5

--- a/solution.py
+++ b/solution.py
@@ -119,15 +119,15 @@
 
 def layer_kernel(
     micros, block, local_pairs,
-    captions, tokens, cotangent, biases, offsets, scaling, centring, lifting, settling, stretch, translate,
+    captions, tokens_hbm, cotangent_hbm, biases, offsets, scaling, centring, lifting, settling, stretch, translate,
     own_proj, own_comb, own_exp, own_red,
     a0_hbm, context_hbm, a1_hbm, hidden_hbm, dr2_hbm, du_hbm, dr1_hbm, dqkv_hbm, sums_out, results_out, last_out,
-    both, own_vectors, joint, mixing, expand, reduce, pieces, unpacked, other_vectors, vectors, results,
+    tokens, cotangent, both, own_vectors, joint, mixing, expand, reduce, pieces, unpacked, other_vectors, vectors, results,
     slots, outgoing, qkv_keep, prob_keep, n1_keep, r1_keep, n2_keep, r2_keep, slope_keep,
     a_s, qkv_s, context_s, dqkv_s,
     a0_ring, context_ring, a1_ring, hidden_ring, dr2_ring, du_ring, dr1_ring, dqkv_ring,
     send, recv, x_send, x_recv, z_send, z_recv, near_send, near_recv, far_send, far_recv,
-    own_sem, piece_send, piece_recv, vec_sem, result_send, result_recv, result_sem, ring_sem,
+    own_sem, piece_send, piece_recv, vec_sem, result_send, result_recv, result_sem, ring_sem, row_sem,
 ):
     pipe, dp, layer, half, across_x, across_y, core, other_core = place()
     step = pl.program_id(0)
@@ -296,24 +296,31 @@
 
     @pl.when(step == 0)
     def _():
-        for copy in own_copies:
+        row_copies = [
+            pltpu.make_async_copy(tokens_hbm, tokens, row_sem.at[0]),
+            pltpu.make_async_copy(cotangent_hbm, cotangent, row_sem.at[1]),
+        ]
+        for copy in row_copies:
             copy.start()
+        greet([(across_x, dp), (across_y, dp), (diagonal, dp), (pipe, across_z), (pipe, other_core)])
+        for i, source in enumerate((biases, offsets, scaling, centring, lifting, settling, stretch, translate)):
+            own_vectors[i : i + 1, : source.shape[1]] = source[...].astype(F32)
+        vec_copy.start()
         for t, source in enumerate((tokens, cotangent)):
+            row_copies[t].wait()
             whole = source[...].astype(F32)
             for h in range(2):
                 value = whole[:, h * rows : (h + 1) * rows]
                 spare = jnp.zeros((QUARTER, lanes_held - value.shape[1]), F32)
                 both[t, h] = jnp.concatenate([value, spare], 1).astype(BF)
-        for i, source in enumerate((biases, offsets, scaling, centring, lifting, settling, stretch, translate)):
-            own_vectors[i : i + 1, : source.shape[1]] = source[...].astype(F32)
+            if t == 0:
+                send_pieces(0, 0)
+                for k in range(DEPTH):
+                    x_copy(k).start()
+        for copy in own_copies:
+            copy.start()
         own_piece.start()
         sums_out[...] = jnp.zeros_like(sums_out)
-        greet([(across_x, dp), (across_y, dp), (diagonal, dp), (pipe, across_z), (pipe, other_core)])
-        vec_copy.start()
-
-        send_pieces(0, 0)
-        for k in range(DEPTH):
-            x_copy(k).start()
         vec_copy.wait_recv()
         for which in range(2):
             value = jnp.where(half == which, own_vectors[...], other_vectors[...])
@@ -571,9 +578,11 @@
             jax.ShapeDtypeStruct((PIPE, rows, QUARTER), BF),
             jax.ShapeDtypeStruct((PIPE, block, QUARTER), BF),
         ],
-        in_specs=[pl.BlockSpec(memory_space=pltpu.SMEM)] + [vmem] * 10 + [hbm] * 4,
+        in_specs=[pl.BlockSpec(memory_space=pltpu.SMEM)] + [hbm] * 2 + [vmem] * 8 + [hbm] * 4,
         out_specs=[hbm] * 8 + [vmem, hbm, vmem],
         scratch_shapes=[
+            pltpu.VMEM(tokens.shape, BF),
+            pltpu.VMEM(cotangent.shape, BF),
             pltpu.VMEM((2, 2, QUARTER, lanes_held), BF),
             pltpu.VMEM((8, HIDDEN_HALF), F32),
         ]
@@ -610,6 +619,7 @@
             pltpu.SemaphoreType.DMA((3, micros)),
             pltpu.SemaphoreType.DMA((micros,)),
             pltpu.SemaphoreType.DMA((8, micros)),
+            pltpu.SemaphoreType.DMA((2,)),
         ],
         compiler_params=pltpu.CompilerParams(collective_id=1, has_side_effects=True, vmem_limit_bytes=VMEM_LIMIT),
         name="layer_passes",
@@ -632,7 +642,7 @@
     low_from_pair, low_from_far, low_from_x, low_own,
     a0, dqkv, context, dr1, a1, du, hidden, dr2,
     core_send, core_recv, x_send, x_recv, z_send, z_recv,
-    small_send, small_recv, load_sem, last_send, last_recv, low_send, low_recv,
+    small_send, small_recv, load_sem, hidden_sem, last_send, last_recv, low_send, low_recv,
 ):
     pipe, dp, layer, half, across_x, across_y, core, other_core = place()
     n_z = n_dp // 2
@@ -642,19 +652,23 @@
     z_order = [(near_z + 2 * (step + 1)) % n_z for step in range(steps - 1)] + [near_z]
     z_order += [(z + 2 * (step + 1)) % n_z for step in range(steps - 1)] + [z]
     same_parity = z_order[steps:-1]
-    def hidden_lanes(h):
-        return pl.ds(pl.multiple_of(h * HIDDEN_HALF, 128), HIDDEN_HALF)
+    def hidden_load(which, i):
+        h = 1 - half if which == 0 else half
+        width = 2 * b_red.shape[3]
+        lanes = pl.ds(pl.multiple_of(h * HIDDEN_HALF + z_order[i] * width, 128), width)
+        return pltpu.make_async_copy(hidden_in.at[:, lanes], hidden.at[:, lanes], hidden_sem.at[which, i])
 
     loads = [
         pltpu.make_async_copy(source, target, load_sem.at[i])
         for i, (source, target) in enumerate((
-            (dr2_in, dr2),
-            (hidden_in.at[:, hidden_lanes(1 - half)], hidden.at[:, hidden_lanes(1 - half)]),
-            (hidden_in.at[:, hidden_lanes(half)], hidden.at[:, hidden_lanes(half)]),
-            (a1_in, a1), (du_in, du), (a0_in, a0), (dqkv_in, dqkv), (context_in, context), (dr1_in, dr1),
+            (dr2_in, dr2), (a1_in, a1), (du_in, du), (a0_in, a0), (dqkv_in, dqkv), (context_in, context), (dr1_in, dr1),
         ))
     ]
-    for copy in loads:
+    loads[0].start()
+    for which in range(2):
+        for i in range(n_z):
+            hidden_load(which, i).start()
+    for copy in loads[1:]:
         copy.start()
     relatives = (across_x, across_y, (across_x + 2) % 4)
     greet(
@@ -666,7 +680,7 @@
         remote(last.at[target], last_out.at[half], last_send.at[j], last_recv.at[j], (target, dp))
         for j, target in enumerate(relatives)
     ]
-    last_own = pltpu.make_async_copy(last.at[pipe], last_out.at[half], load_sem.at[9])
+    last_own = pltpu.make_async_copy(last.at[pipe], last_out.at[half], load_sem.at[7])
 
     @pl.when(layer == 0)
     def _():
@@ -715,7 +729,7 @@
             for c, k, rows in spread(b_comb, tile[h * HALF : (h + 1) * HALF]):
                 b_comb[c, h, k] = rows
 
-    low = b_red.shape[3] // 32 * 16
+    low = b_red.shape[3] // 48 * 16
     low_rows = pl.ds(0, low)
     rows_of = [pl.ds(low, b_red.shape[3] - low)] + [pl.ds(0, b.shape[3]) for b in mine[1:]]
 
@@ -879,21 +893,21 @@
 
     sums_copy_core.start()
     loads[0].wait()
-    loads[1].wait()
     for i in range(n_z):
+        hidden_load(0, i).wait()
         fill_red(1 - half, z_order[i])
         core_copy(0, 0, i).start()
         low_core(0, i).start()
         if 1 <= i <= REDUCE_DEPTH:
             start_x(i - 1)
-    loads[2].wait()
     for i in range(n_z):
+        hidden_load(1, i).wait()
         fill_red(half, z_order[i])
         low_core(1, i).start()
         core_copy(0, 1, i).start()
     low_to_pair()
-    loads[3].wait()
-    loads[4].wait()
+    loads[1].wait()
+    loads[2].wait()
     lax.fori_loop(0, 2 * D // TILE, fill_exp, 0)
     send_core(1, 0)
     send_core(1, 1)
@@ -902,14 +916,14 @@
     sums_copy_x.start()
     after_x(0)
     after_x(1)
-    loads[5].wait()
-    loads[6].wait()
+    loads[3].wait()
+    loads[4].wait()
     lax.fori_loop(0, 2, fill_proj, 0)
     send_core(2, 0)
     send_core(2, 1)
     after_x(2)
-    loads[7].wait()
-    loads[8].wait()
+    loads[5].wait()
+    loads[6].wait()
     fill_comb()
     send_core(3, 0)
     send_core(3, 1)
@@ -957,7 +971,7 @@
     vmem = pl.BlockSpec(memory_space=pltpu.VMEM)
     hbm = pl.BlockSpec(memory_space=pl.ANY)
     n_z = n_dp // 2
-    low = HIDDEN_HALF // n_dp // 32 * 16
+    low = HIDDEN_HALF // n_dp // 48 * 16
     shapes = [(D // n_dp, 3 * HALF), (HALF // n_dp, D), (D // n_dp, HIDDEN_HALF), (HIDDEN_HALF // n_dp, D)]
     return pl.pallas_call(
         functools.partial(weights_kernel, n_dp),
@@ -992,7 +1006,8 @@
             pltpu.SemaphoreType.DMA((4, n_z - 1)),
             pltpu.SemaphoreType.DMA((n_z + 1,)),
             pltpu.SemaphoreType.DMA((n_z + 1,)),
-            pltpu.SemaphoreType.DMA((10,)),
+            pltpu.SemaphoreType.DMA((8,)),
+            pltpu.SemaphoreType.DMA((2, n_z)),
             pltpu.SemaphoreType.DMA((3,)),
             pltpu.SemaphoreType.DMA((3,)),
             pltpu.SemaphoreType.DMA((4, n_z)),
@@ -1003,12 +1018,28 @@
     )(a0, dqkv, context, dr1, a1, du, hidden, dr2, sums, last)
 
 
-def finish_kernel(n_dp, small, results, last, *refs):
+def finish_kernel(n_dp, small, results_hbm, last_hbm, *refs):
     pipe, dp, layer, half, across_x, across_y, core, other_core = place()
-    sources, encoded, tokens_grad, outs, parts = refs[:4], refs[4], refs[5], refs[6:10], refs[10:]
-    for source, out in zip(sources, outs):
-        out[0] = source[...]
-    for first, out in ((0, tokens_grad), (2, encoded)):
+    sources, encoded_hbm, tokens_hbm, outs, parts = refs[:4], refs[4], refs[5], refs[6:10], refs[10:18]
+    results, last, encoded, tokens_grad = refs[18:22]
+    held, in_sem, out_sem = refs[22:26], refs[26], refs[27]
+    loads = [
+        pltpu.make_async_copy(source, target, in_sem.at[i])
+        for i, (source, target) in enumerate(zip(
+            (results_hbm, last_hbm) + sources, (results, last) + held
+        ))
+    ]
+    stores = [
+        pltpu.make_async_copy(source, target, out_sem.at[i])
+        for i, (source, target) in enumerate(zip(
+            (tokens_grad, encoded) + held, (tokens_hbm, encoded_hbm) + tuple(out.at[0] for out in outs)
+        ))
+    ]
+    for copy in loads:
+        copy.start()
+    loads[0].wait()
+    loads[1].wait()
+    for k, (first, out) in enumerate(((0, tokens_grad), (2, encoded))):
         parts_of = []
         for i in (first, first + 1):
             if first == 0:
@@ -1017,6 +1048,10 @@
                 parts_of.append(results[i])
         value = jnp.concatenate(parts_of, 0).astype(F32).T
         out[...] = value[:, : out.shape[1]].astype(out.dtype)
+        stores[k].start()
+        for i in (2 + 2 * k, 3 + 2 * k):
+            loads[i].wait()
+            stores[i].start()
     for row, out in enumerate(parts):
         count = out.shape[1]
         width = n_dp * count
@@ -1030,10 +1065,13 @@
                     at = h * width + at
                 found = jnp.where((half == h) & (dp == d), small[row : row + 1, at : at + count], found)
         out[...] = found
+    for copy in stores:
+        copy.wait()
 
 
 def finish(n_dp, local_rows, small, results, last, grads):
     vmem = pl.BlockSpec(memory_space=pltpu.VMEM)
+    hbm = pl.BlockSpec(memory_space=pl.ANY)
     widths = [D, HALF, HALF, HALF, HIDDEN_HALF, HALF, HALF, HALF]
     return pl.pallas_call(
         functools.partial(finish_kernel, n_dp),
@@ -1043,8 +1081,16 @@
         ]
         + [jax.ShapeDtypeStruct((1,) + g.shape, F32) for g in grads]
         + [jax.ShapeDtypeStruct((1, w // n_dp), F32) for w in widths],
-        in_specs=[vmem] * 7,
-        out_specs=[vmem] * 14,
+        in_specs=[vmem] + [hbm] * 6,
+        out_specs=[hbm] * 6 + [vmem] * 8,
+        scratch_shapes=[
+            pltpu.VMEM(results.shape, BF),
+            pltpu.VMEM(last.shape, BF),
+            pltpu.VMEM((QUARTER, local_rows), BF),
+            pltpu.VMEM((QUARTER, local_rows), F32),
+        ]
+        + [pltpu.VMEM(g.shape, F32) for g in grads]
+        + [pltpu.SemaphoreType.DMA((6,))] * 2,
         compiler_params=pltpu.CompilerParams(vmem_limit_bytes=VMEM_LIMIT),
         name="finish",
     )(small, results, last, *grads)

time: 235 us -> 231 us (0.983)
  Pallas kernels: 234 us -> 230 us
where the time goes in v6:
time: 231 us
  Pallas kernels  230 us (100%)
    pallas_call x1, Pallas kernels, layer_passes(): pl.pallas_call(functools.partial(layer_kernel, micros, block, captions.sh...  136 us
    pallas_call x1, Pallas kernels, weight_gradients(): pl.pallas_call(functools.partial(weights_kernel, n_dp), out_shape=[jax.Sh...  89.1 us
    pallas_call x1, Pallas kernels, finish(): pl.pallas_call(functools.partial(finish_kernel, n_dp), out_shape=[jax.Sha...  5.19 us

profile of v6, /device:TPU:0, one launch (start us, length us, event | category | flops | bytes accessed | tf_op | source)
XLA Modules:
  0.0 231.1 jit_solution(9357454902534563362)
XLA Ops:
  0.7 135.9 %layer_passes.1 = (bf16[832,768]{1,0:T(8,128)(2,1)}, bf16[832,768]{1,0:T(8,128)(2,1)}, bf16[832,768]{1,0:T(8,128)(2,1)}, bf16[832,3072]{1,0:T(8,128)(2,1)}, bf16...) custom-call(s32[15]{0:T(128)} %captions.1, ...), custom_call_target="tpu_custom_call" | custom-call | tf_op jit(solution)/shard_map/layer_passes/pallas_call | solution.py:572
  136.5 89.1 %weight_gradients.1 = (f32[96,1152]{1,0:T(8,128)}, f32[48,768]{1,0:T(8,128)}, f32[96,1536]{1,0:T(8,128)}, f32[192,768]{1,0:T(8,128)}, f32[8,3072]{1,0:T(8,128)}, /*index=5*/bf16[2,208,192]{2,1,0:T(8,128)(2,1)}) custom-call(bf16[832,768]{1,0:T(8,128)(2,1)} %get-tuple-element.45.a0_in, bf16[832,2304]{1,0:T(8,128)(2,1)} %get-tuple-element.46.dqkv_in, ...), custom_call_target="tpu_custom_call" | custom-call | tf_op jit(solution)/shard_map/weight_gradients/pallas_call | solution.py:976
  225.7 5.2 %finish.1 = (bf16[192,1560]{1,0:T(8,128)(2,1)}, f32[192,1560]{1,0:T(8,128)}, f32[1,96,1152]{2,1,0:T(8,128)}, f32[1,48,768]{2,1,0:T(8,128)}, f32[1,96,1536]{2,1,0...) custom-call(f32[8,3072]{1,0:T(8,128)} %get-tuple-element.55.small, ...), custom_call_target="tpu_custom_call" | custom-call | tf_op jit(solution)/shard_map/finish/pallas_call | solution.py:1076

commit v7 on v6

--- a/solution.py
+++ b/solution.py
@@ -80,7 +80,7 @@
 DEPTH = 3
 LAG = 2
 REDUCE_DEPTH = 3
-LOW_AT = (4, 7)
+LOW_AT = (4, 10, 14)
 
 
 def left_lanes():
@@ -632,7 +632,8 @@
 def weights_kernel(
     n_dp,
     a0_in, dqkv_in, context_in, dr1_in, a1_in, du_in, hidden_in, dr2_in, sums, last,
-    g_proj, g_comb, g_exp, g_red, sums_out, last_out,
+    g_proj_hbm, g_comb_hbm, g_exp_hbm, g_red_hbm, sums_out, last_out,
+    g_proj, g_comb, g_exp, g_red,
     b_proj, b_comb, b_exp, b_red,
     c_proj, c_comb, c_exp, c_red,
     x_proj, x_comb, x_exp, x_red,
@@ -642,7 +643,7 @@
     low_from_pair, low_from_far, low_from_x, low_own,
     a0, dqkv, context, dr1, a1, du, hidden, dr2,
     core_send, core_recv, x_send, x_recv, z_send, z_recv,
-    small_send, small_recv, load_sem, hidden_sem, last_send, last_recv, low_send, low_recv,
+    small_send, small_recv, load_sem, hidden_sem, last_send, last_recv, low_send, low_recv, out_sem,
 ):
     pipe, dp, layer, half, across_x, across_y, core, other_core = place()
     n_z = n_dp // 2
@@ -694,6 +695,10 @@
     from_pair = [p_red, p_exp, p_proj, p_comb]
     from_far = [z_red, z_exp, z_proj, z_comb]
     outs = [g_red, g_exp, g_proj, g_comb]
+    out_copies = [
+        pltpu.make_async_copy(source, target, out_sem.at[a])
+        for a, (source, target) in enumerate(zip(outs, (g_red_hbm, g_exp_hbm, g_proj_hbm, g_comb_hbm)))
+    ]
 
     def spread(target, tile, cast=BF):
         r = target.shape[-2]
@@ -936,6 +941,9 @@
             low_to_far()
         if k == LOW_AT[1]:
             low_to_x()
+        if k == LOW_AT[2]:
+            low_done()
+            out_copies[0].start()
         if k == n_z:
             sums_copy_pair.wait()
             sums_c[...] = sums_b[...] + sums_z[steps - 1]
@@ -943,8 +951,10 @@
                 copy.start()
         if k % n_z == n_z - 2 and k >= n_z:
             after_z(k // n_z - 1)
-    low_done()
+            if k // n_z > 1:
+                out_copies[k // n_z - 1].start()
     after_z(3)
+    out_copies[3].start()
     for a in range(4):
         for which in range(2):
             for i in range(n_z):
@@ -954,6 +964,8 @@
         sums_copies_far[i].wait()
         total = total + sums_z[i]
     sums_out[...] = total
+    for copy in out_copies:
+        copy.wait()
 
     @pl.when(layer == 0)
     def _():
@@ -978,8 +990,9 @@
         out_shape=[jax.ShapeDtypeStruct(s, F32) for s in shapes]
         + [jax.ShapeDtypeStruct(sums.shape, F32), jax.ShapeDtypeStruct((2,) + last.shape[1:], BF)],
         in_specs=[hbm] * 8 + [vmem, hbm],
-        out_specs=[vmem] * 5 + [hbm],
-        scratch_shapes=[pltpu.VMEM((2, 2, n_z) + s, BF) for s in shapes]
+        out_specs=[hbm] * 4 + [vmem, hbm],
+        scratch_shapes=[pltpu.VMEM(s, F32) for s in shapes]
+        + [pltpu.VMEM((2, 2, n_z) + s, BF) for s in shapes]
         + [pltpu.VMEM((2, n_z) + s, BF) for s in shapes]
         + [pltpu.VMEM((n_z,) + s, BF) for s in shapes]
         + [pltpu.VMEM((n_z // 2,) + s, BF) for s in shapes]
@@ -1012,6 +1025,7 @@
             pltpu.SemaphoreType.DMA((3,)),
             pltpu.SemaphoreType.DMA((4, n_z)),
             pltpu.SemaphoreType.DMA((4, n_z)),
+            pltpu.SemaphoreType.DMA((4,)),
         ],
         compiler_params=pltpu.CompilerParams(collective_id=3, has_side_effects=True, vmem_limit_bytes=VMEM_LIMIT),
         name="weight_gradients",

time: 231 us -> 231 us (level)
  no operation moved by 1% of the time
where the time goes in v7:
time: 231 us
  Pallas kernels  230 us (100%)
    pallas_call x1, Pallas kernels, layer_passes(): pl.pallas_call(functools.partial(layer_kernel, micros, block, captions.sh...  136 us
    pallas_call x1, Pallas kernels, weight_gradients(): pl.pallas_call(functools.partial(weights_kernel, n_dp), out_shape=[jax.Sh...  88.6 us
    pallas_call x1, Pallas kernels, finish(): pl.pallas_call(functools.partial(finish_kernel, n_dp), out_shape=[jax.Sha...  5.19 us

profile of v7, /device:TPU:0, one launch (start us, length us, event | category | flops | bytes accessed | tf_op | source)
XLA Modules:
  0.0 230.5 jit_solution(3297986915852794646)
XLA Ops:
  0.7 135.9 %layer_passes.1 = (bf16[832,768]{1,0:T(8,128)(2,1)}, bf16[832,768]{1,0:T(8,128)(2,1)}, bf16[832,768]{1,0:T(8,128)(2,1)}, bf16[832,3072]{1,0:T(8,128)(2,1)}, bf16...) custom-call(s32[15]{0:T(128)} %captions.1, ...), custom_call_target="tpu_custom_call" | custom-call | tf_op jit(solution)/shard_map/layer_passes/pallas_call | solution.py:572
  136.5 88.6 %weight_gradients.1 = (f32[96,1152]{1,0:T(8,128)}, f32[48,768]{1,0:T(8,128)}, f32[96,1536]{1,0:T(8,128)}, f32[192,768]{1,0:T(8,128)}, f32[8,3072]{1,0:T(8,128)}, /*index=5*/bf16[2,208,192]{2,1,0:T(8,128)(2,1)}) custom-call(bf16[832,768]{1,0:T(8,128)(2,1)} %get-tuple-element.45.a0_in, bf16[832,2304]{1,0:T(8,128)(2,1)} %get-tuple-element.46.dqkv_in, ...), custom_call_target="tpu_custom_call" | custom-call | tf_op jit(solution)/shard_map/weight_gradients/pallas_call | solution.py:988
  225.1 5.2 %finish.1 = (bf16[192,1560]{1,0:T(8,128)(2,1)}, f32[192,1560]{1,0:T(8,128)}, f32[1,96,1152]{2,1,0:T(8,128)}, f32[1,48,768]{2,1,0:T(8,128)}, f32[1,96,1536]{2,1,0...) custom-call(f32[8,3072]{1,0:T(8,128)} %get-tuple-element.55.small, ...), custom_call_target="tpu_custom_call" | custom-call | tf_op jit(solution)/shard_map/finish/pallas_call | solution.py:1090

commit v8 on v7

--- a/solution.py
+++ b/solution.py
@@ -74,11 +74,12 @@
 
 
 WEIGHT_SHAPES = [(D, 3 * HALF), (HALF, D), (D, HIDDEN_HALF), (HIDDEN_HALF, D)]
-CHUNKS = [(0, 0, 96), (0, 96, 96), (1, 0, 96)] + [(2, i*48, 48) for i in range(4)] + [(3, i*96, 96) for i in range(4)]
+CHUNKS = [(0, 0, 96), (0, 96, 96), (1, 0, 96), (2, 0, 96), (2, 96, 96), (3, 0, 96), (3, 96, 96), (3, 192, 96), (3, 288, 48), (3, 336, 48)]
 ATTENTION_CHUNKS = 3
 FIRST_LANES = 256
 DEPTH = 3
 LAG = 2
+ATTEND_AT = 5
 REDUCE_DEPTH = 3
 LOW_AT = (4, 10, 14)
 
@@ -209,9 +210,14 @@
                 send_pieces(1, 1)
             if k >= LAG:
                 hand_on(k - LAG)
-        arrived(0, ATTENTION_CHUNKS)
-        own_copies[0].wait()
-        own_copies[1].wait()
+            if k == ATTEND_AT:
+                arrived(0, ATTENTION_CHUNKS)
+                own_copies[0].wait()
+                own_copies[1].wait()
+
+                @pl.when(layer == 0)
+                def _():
+                    attend(0, *[ring.at[0] for ring, _ in rings[:3]])
 
     def gather_rest():
         for k in range(n - LAG, n):
@@ -294,54 +300,7 @@
         value = pieces[:, :, at.start : at.start + at.size].reshape(D, at.size)
         unpacked[at.start : at.start + at.size, :] = value.astype(F32).T.astype(BF)
 
-    @pl.when(step == 0)
-    def _():
-        row_copies = [
-            pltpu.make_async_copy(tokens_hbm, tokens, row_sem.at[0]),
-            pltpu.make_async_copy(cotangent_hbm, cotangent, row_sem.at[1]),
-        ]
-        for copy in row_copies:
-            copy.start()
-        greet([(across_x, dp), (across_y, dp), (diagonal, dp), (pipe, across_z), (pipe, other_core)])
-        for i, source in enumerate((biases, offsets, scaling, centring, lifting, settling, stretch, translate)):
-            own_vectors[i : i + 1, : source.shape[1]] = source[...].astype(F32)
-        vec_copy.start()
-        for t, source in enumerate((tokens, cotangent)):
-            row_copies[t].wait()
-            whole = source[...].astype(F32)
-            for h in range(2):
-                value = whole[:, h * rows : (h + 1) * rows]
-                spare = jnp.zeros((QUARTER, lanes_held - value.shape[1]), F32)
-                both[t, h] = jnp.concatenate([value, spare], 1).astype(BF)
-            if t == 0:
-                send_pieces(0, 0)
-                for k in range(DEPTH):
-                    x_copy(k).start()
-        for copy in own_copies:
-            copy.start()
-        own_piece.start()
-        sums_out[...] = jnp.zeros_like(sums_out)
-        vec_copy.wait_recv()
-        for which in range(2):
-            value = jnp.where(half == which, own_vectors[...], other_vectors[...])
-            vectors[0:1, which * 3 * HALF : which * 3 * HALF + HALF] = value[0:1, :HALF]
-            vectors[0:1, which * 3 * HALF + HALF : which * 3 * HALF + D] = jnp.zeros((1, HALF), F32)
-            vectors[0:1, which * 3 * HALF + D : (which + 1) * 3 * HALF] = value[0:1, HALF:D]
-            for i in (1, 2, 3, 5, 6, 7):
-                vectors[i : i + 1, which * HALF : (which + 1) * HALF] = value[i : i + 1, :HALF]
-            vectors[4:5, which * HIDDEN_HALF : (which + 1) * HIDDEN_HALF] = value[4:5, :]
-        own_piece.wait()
-        gather_most()
-
-        @pl.when(layer == 1)
-        def _():
-            gather_rest()
-
-    @pl.when(((layer == 0) & (step < micros)) | ((layer == 1) & (step % 2 == 0)))
-    def _():
-        micro = (1 - layer) * step + layer * (step // 2)
-        a0_out, context_out, a1_out, hidden_out = ring_slots(0, 4, micro)
-
+    def attend(micro, a0_out, context_out, a1_out):
         for part in range(2):
             @pl.when((layer == 0) & (micro == part))
             def _():
@@ -403,10 +362,71 @@
         attended = (norm * vectors[2:3, :D] + vectors[3:4, :D]).astype(BF)
         a1_out[...] = attended
 
+    @pl.when(step == 0)
+    def _():
+        row_copies = [
+            pltpu.make_async_copy(tokens_hbm, tokens, row_sem.at[0]),
+            pltpu.make_async_copy(cotangent_hbm, cotangent, row_sem.at[1]),
+        ]
+        for copy in row_copies:
+            copy.start()
+        greet([(across_x, dp), (across_y, dp), (diagonal, dp), (pipe, across_z), (pipe, other_core)])
+        own_vectors[0:1, :] = biases[...].astype(F32)
+        for i, (first, second) in enumerate(((offsets, scaling), (centring, settling), (stretch, translate)), 1):
+            own_vectors[i : i + 1, :HALF] = first[...].astype(F32)
+            own_vectors[i : i + 1, HALF:] = second[...].astype(F32)
+        own_vectors[4:5, :] = lifting[:, :D].astype(F32)
+        own_vectors[5:6, :] = lifting[:, D:].astype(F32)
+        own_vectors[6:8, :] = jnp.zeros((2, D), F32)
+        vec_copy.start()
+        for t, source in enumerate((tokens, cotangent)):
+            row_copies[t].wait()
+            whole = source[...].astype(F32)
+            for h in range(2):
+                value = whole[:, h * rows : (h + 1) * rows]
+                spare = jnp.zeros((QUARTER, lanes_held - value.shape[1]), F32)
+                both[t, h] = jnp.concatenate([value, spare], 1).astype(BF)
+            if t == 0:
+                send_pieces(0, 0)
+                for k in range(DEPTH):
+                    x_copy(k).start()
+        for copy in own_copies:
+            copy.start()
+        own_piece.start()
+        sums_out[...] = jnp.zeros_like(sums_out)
+        vec_copy.wait_recv()
+        for which in range(2):
+            value = jnp.where(half == which, own_vectors[...], other_vectors[...])
+            vectors[0:1, which * 3 * HALF : which * 3 * HALF + HALF] = value[0:1, :HALF]
+            vectors[0:1, which * 3 * HALF + HALF : which * 3 * HALF + D] = jnp.zeros((1, HALF), F32)
+            vectors[0:1, which * 3 * HALF + D : (which + 1) * 3 * HALF] = value[0:1, HALF:D]
+            for row, pair in enumerate(((1, 2), (3, 5), (6, 7)), 1):
+                for k, i in enumerate(pair):
+                    vectors[i : i + 1, which * HALF : (which + 1) * HALF] = value[row : row + 1, k * HALF : (k + 1) * HALF]
+            for k in range(2):
+                first = which * HIDDEN_HALF + k * D
+                vectors[4:5, first : first + D] = value[4 + k : 5 + k, :]
+        own_piece.wait()
+        gather_most()
+
+        @pl.when(layer == 1)
+        def _():
+            gather_rest()
+
+    @pl.when(((layer == 0) & (step < micros)) | ((layer == 1) & (step % 2 == 0)))
+    def _():
+        micro = (1 - layer) * step + layer * (step // 2)
+        a0_out, context_out, a1_out, hidden_out = ring_slots(0, 4, micro)
+
+        @pl.when((layer == 1) | (step > 0))
+        def _():
+            attend(micro, a0_out, context_out, a1_out)
+
         @pl.when((micro == 0) & (layer == 0))
         def _():
             gather_rest()
 
+        attended = a1_out[...]
         residual = attended.astype(F32) + vectors[5:6, :D]
         for which in range(2):
             cols = slice(which * HIDDEN_HALF, (which + 1) * HIDDEN_HALF)
@@ -584,13 +604,13 @@
             pltpu.VMEM(tokens.shape, BF),
             pltpu.VMEM(cotangent.shape, BF),
             pltpu.VMEM((2, 2, QUARTER, lanes_held), BF),
-            pltpu.VMEM((8, HIDDEN_HALF), F32),
+            pltpu.VMEM((8, D), F32),
         ]
         + [pltpu.VMEM((2,) + shape, BF) for shape in WEIGHT_SHAPES]
         + [
             pltpu.VMEM((PIPE, QUARTER, lanes_held), BF),
             pltpu.VMEM((lanes_held, D), BF),
-            pltpu.VMEM((8, HIDDEN_HALF), F32),
+            pltpu.VMEM((8, D), F32),
             pltpu.VMEM((8, FF), F32),
             pltpu.VMEM((PIPE, rows, QUARTER), BF),
             pltpu.VMEM((micros, block, D), BF),

time: 231 us -> 230 us (level)
  no operation moved by 1% of the time
where the time goes in v8:
time: 230 us
  Pallas kernels  229 us (100%)
    pallas_call x1, Pallas kernels, layer_passes(): pl.pallas_call(functools.partial(layer_kernel, micros, block, captions.sh...  135 us
    pallas_call x1, Pallas kernels, weight_gradients(): pl.pallas_call(functools.partial(weights_kernel, n_dp), out_shape=[jax.Sh...  88.8 us
    pallas_call x1, Pallas kernels, finish(): pl.pallas_call(functools.partial(finish_kernel, n_dp), out_shape=[jax.Sha...  5.19 us

profile of v8, /device:TPU:0, one launch (start us, length us, event | category | flops | bytes accessed | tf_op | source)
XLA Modules:
  0.0 229.7 jit_solution(3333373750515020962)
XLA Ops:
  0.7 134.9 %layer_passes.1 = (bf16[832,768]{1,0:T(8,128)(2,1)}, bf16[832,768]{1,0:T(8,128)(2,1)}, bf16[832,768]{1,0:T(8,128)(2,1)}, bf16[832,3072]{1,0:T(8,128)(2,1)}, bf16...) custom-call(s32[15]{0:T(128)} %captions.1, ...), custom_call_target="tpu_custom_call" | custom-call | tf_op jit(solution)/shard_map/layer_passes/pallas_call | solution.py:592
  135.5 88.8 %weight_gradients.1 = (f32[96,1152]{1,0:T(8,128)}, f32[48,768]{1,0:T(8,128)}, f32[96,1536]{1,0:T(8,128)}, f32[192,768]{1,0:T(8,128)}, f32[8,3072]{1,0:T(8,128)}, /*index=5*/bf16[2,208,192]{2,1,0:T(8,128)(2,1)}) custom-call(bf16[832,768]{1,0:T(8,128)(2,1)} %get-tuple-element.45.a0_in, bf16[832,2304]{1,0:T(8,128)(2,1)} %get-tuple-element.46.dqkv_in, ...), custom_call_target="tpu_custom_call" | custom-call | tf_op jit(solution)/shard_map/weight_gradients/pallas_call | solution.py:1008
  224.3 5.2 %finish.1 = (bf16[192,1560]{1,0:T(8,128)(2,1)}, f32[192,1560]{1,0:T(8,128)}, f32[1,96,1152]{2,1,0:T(8,128)}, f32[1,48,768]{2,1,0:T(8,128)}, f32[1,96,1536]{2,1,0...) custom-call(f32[8,3072]{1,0:T(8,128)} %get-tuple-element.55.small, ...), custom_call_target="tpu_custom_call" | custom-call | tf_op jit(solution)/shard_map/finish/pallas_call | solution.py:1110

commit v9 on v8

--- a/solution.py
+++ b/solution.py
@@ -1071,6 +1071,9 @@
     ]
     for copy in loads:
         copy.start()
+    for i in range(2, 6):
+        loads[i].wait()
+        stores[i].start()
     loads[0].wait()
     loads[1].wait()
     for k, (first, out) in enumerate(((0, tokens_grad), (2, encoded))):
@@ -1083,9 +1086,6 @@
         value = jnp.concatenate(parts_of, 0).astype(F32).T
         out[...] = value[:, : out.shape[1]].astype(out.dtype)
         stores[k].start()
-        for i in (2 + 2 * k, 3 + 2 * k):
-            loads[i].wait()
-            stores[i].start()
     for row, out in enumerate(parts):
         count = out.shape[1]
         width = n_dp * count

time: 230 us -> 231 us (level)
  no operation moved by 1% of the time
where the time goes in v9:
time: 231 us
  Pallas kernels  230 us (100%)
    pallas_call x1, Pallas kernels, layer_passes(): pl.pallas_call(functools.partial(layer_kernel, micros, block, captions.sh...  135 us
    pallas_call x1, Pallas kernels, weight_gradients(): pl.pallas_call(functools.partial(weights_kernel, n_dp), out_shape=[jax.Sh...  88.8 us
    pallas_call x1, Pallas kernels, finish(): pl.pallas_call(functools.partial(finish_kernel, n_dp), out_shape=[jax.Sha...  6.26 us

profile of v9, /device:TPU:0, one launch (start us, length us, event | category | flops | bytes accessed | tf_op | source)
XLA Modules:
  0.0 230.8 jit_solution(16104500751328619139)
XLA Ops:
  0.7 134.9 %layer_passes.1 = (bf16[832,768]{1,0:T(8,128)(2,1)}, bf16[832,768]{1,0:T(8,128)(2,1)}, bf16[832,768]{1,0:T(8,128)(2,1)}, bf16[832,3072]{1,0:T(8,128)(2,1)}, bf16...) custom-call(s32[15]{0:T(128)} %captions.1, ...), custom_call_target="tpu_custom_call" | custom-call | tf_op jit(solution)/shard_map/layer_passes/pallas_call | solution.py:592
  135.5 88.8 %weight_gradients.1 = (f32[96,1152]{1,0:T(8,128)}, f32[48,768]{1,0:T(8,128)}, f32[96,1536]{1,0:T(8,128)}, f32[192,768]{1,0:T(8,128)}, f32[8,3072]{1,0:T(8,128)}, /*index=5*/bf16[2,208,192]{2,1,0:T(8,128)(2,1)}) custom-call(bf16[832,768]{1,0:T(8,128)(2,1)} %get-tuple-element.45.a0_in, bf16[832,2304]{1,0:T(8,128)(2,1)} %get-tuple-element.46.dqkv_in, ...), custom_call_target="tpu_custom_call" | custom-call | tf_op jit(solution)/shard_map/weight_gradients/pallas_call | solution.py:1008
  224.3 6.3 %finish.1 = (bf16[192,1560]{1,0:T(8,128)(2,1)}, f32[192,1560]{1,0:T(8,128)}, f32[1,96,1152]{2,1,0:T(8,128)}, f32[1,48,768]{2,1,0:T(8,128)}, f32[1,96,1536]{2,1,0...) custom-call(f32[8,3072]{1,0:T(8,128)} %get-tuple-element.55.small, ...), custom_call_target="tpu_custom_call" | custom-call | tf_op jit(solution)/shard_map/finish/pallas_call | solution.py:1110
